TPU v7x, 128 devices: a whole 4x4x4 slice. The times are simulated.
128 devices in a mesh: stream: 16 (over x, z), tensor: 8 (over y, core).
Axes of the slice: x: 4, y: 4, z: 4, core: 2. Of those that a mesh axis runs over, the one named last changes fastest.
Arguments:
- hidden: bfloat16 [1024, 8192], P('stream', 'tensor'), may hold values from -600 to 600
- norm_gain: bfloat16 [8192], replicated, may hold values from 0.099609375 to 1.8984375
- head_weight: bfloat16 [8192, 128256], P(None, ('stream', 'tensor')), may hold values from -32 to 32
- floor_counts: int32 [128256], P(('stream', 'tensor')), may hold values from 1 to 7
- totals: int32 [1024], replicated, may hold values from 1048576 to 4194304
- targets: int32 [1024], replicated, may hold values from 0 to 128255
Outputs:
- cumulative: float32 [1024, 128256], P(None, ('stream', 'tensor'))
- code_bits: float32 [1024], replicated
All inputs are finite; a program needn't handle non-finite values.
Results may differ from a plain program's by a relative error of at most 0.0003.
The roundings to bfloat16 on the way count: a program that leaves them out, or rounds other values in their place, can miss the bound.
Values may be sent and summed in bfloat16 or wider, within the bound.
No kernel may reach another device: no remote copies, remote signals or barrier semaphores. Data moves between devices by JAX's collectives and lax.ppermute only.
A program may use at most 128 MiB of HBM per device.

v0:
```python
import jax
import jax.numpy as jnp
from jax import lax
from jax.sharding import PartitionSpec as P

epsilon = 1e-05


def prefix(value, axis, join, neutral):
    count, mine = (lax.axis_size(axis), lax.axis_index(axis))
    pieces = lax.all_gather(value, axis)
    subtotal = jnp.full_like(value, 0) + jnp.asarray(neutral, value.dtype)

    def hop(position, subtotal):
        longer = join(subtotal, pieces[position])
        return jnp.where(position < mine, longer, subtotal)

    return lax.fori_loop(0, count - 1, hop, subtotal)


def normalize(features, norm_gain):
    widened = features.astype(jnp.float32)
    mean_square = jnp.mean(widened * widened, axis=1, keepdims=True)
    return (
        widened * lax.rsqrt(mean_square + epsilon) * norm_gain.astype(jnp.float32)[None, :]
    ).astype(jnp.bfloat16)


def add_terms(earlier, latter):
    return earlier + latter


def local(hidden, norm_gain, head_weight, floor_counts, totals, targets):
    vocab_width = head_weight.shape[1]
    gathered = lax.all_gather(hidden, "tensor", axis=1, tiled=True)
    normed = normalize(gathered, norm_gain)
    logits = jnp.dot(
        lax.all_gather(normed, "stream", axis=0, tiled=True),
        head_weight,
        preferred_element_type=jnp.float32,
    )
    local_peak = jnp.max(logits, axis=1)
    floor_float = floor_counts.astype(jnp.float32)
    floor_local = jnp.sum(floor_float)
    token_total = totals.astype(jnp.float32)
    position = lax.axis_index(("stream", "tensor"))
    column_ids = position * vocab_width + jnp.arange(vocab_width, dtype=jnp.int32)
    target_hit = column_ids[None, :] == targets[:, None]
    row_peak = lax.pmax(local_peak, ("stream", "tensor"))
    exponent = jnp.exp(logits - row_peak[:, None])
    row_mass, floor_sum = lax.psum((jnp.sum(exponent, axis=1), floor_local), ("stream", "tensor"))
    probabilities = exponent / row_mass[:, None]
    quantized = (
        floor_float[None, :] + probabilities * (token_total[:, None] - floor_sum)
    ) / token_total[:, None]
    row_sum = jnp.sum(quantized, axis=1)
    picked_local = jnp.sum(jnp.where(target_hit, quantized, 0.0), axis=1)
    offsets = prefix(row_sum, ("stream", "tensor"), add_terms, jnp.zeros_like(row_sum))
    picked = lax.psum(picked_local, ("stream", "tensor"))
    row_ids = jnp.arange(vocab_width, dtype=jnp.int32)
    upper_mask = (row_ids[:, None] < row_ids[None, :]).astype(jnp.float32)
    within = jnp.dot(quantized, upper_mask, precision=lax.Precision.HIGHEST)
    cumulative = offsets[:, None] + within
    code_bits = -jnp.log2(picked)
    return (cumulative, code_bits)


def solution(mesh):
    in_specs = (
        P("stream", "tensor"),
        P(),
        P(None, ("stream", "tensor")),
        P(("stream", "tensor")),
        P(),
        P(),
    )
    out_specs = (P(None, ("stream", "tensor")), P())
    return jax.shard_map(local, mesh=mesh, in_specs=in_specs, out_specs=out_specs, check_vma=False)
```

profile of v0, /device:TPU:0, one launch (start us, length us, event | category | flops | bytes accessed | tf_op | source)
XLA Modules:
  0.0 432.6 jit_solution(7343238317693981664)
XLA Ops:
  7.2 0.0 copy-start
  7.2 0.0 all-gather.4.cloned.1.call-start
  7.2 0.7 all-gather.4.cloned.1.call-update
  7.9 0.0 all-gather.6.cloned.1.call-start
  8.0 0.7 convert_element_type.18
  8.7 26.9 %all-gather.4.cloned.1.call-done = bf16[64,8192]{1,0:T(8,128)(2,1)} async-done(((bf16[64,1024]{1,0:T(8,128)(2,1)}), bf16[64,8192]{1,0:T(8,128)(2,1)}) %all-gather.4.cloned.1.call-update) | async-done | bytes 1048592 | tf_op jit(solution)/shard_map/all_gather | solution.py:35
  35.6 1.5 fusion.2
  37.1 2.5 fusion.4
  39.6 0.0 all-gather.6.cloned.1.call-update
  39.7 0.0 copy-done.1
  39.7 0.7 convert_reduce_fusion
  40.4 110.7 %all-gather.6.cloned.1.call-done = bf16[1024,8192]{1,0:T(8,128)(2,1)} async-done(((bf16[64,8192]{1,0:T(8,128)(2,1)}), bf16[1024,8192]{1,0:T(8,128)(2,1)}) %all-gather.6.cloned.1.call-update) | async-done | bytes 16777232 | tf_op jit(solution)/shard_map/all_gather | solution.py:38
  151.1 23.7 %fusion.5 = (f32[1024]{0:T(1024)S(1)}, f32[1024,1002]{0,1:T(8,128)}) fusion(bf16[1024,8192]{1,0:T(8,128)(2,1)} %all-gather.6.cloned.1.call-done, bf16[8192,1002]{0,1:T(8,128)(2,1)} %param.10), kind=kOutput, calls=%fused_computation.19 | convolution fusion | flops 16811795456 | bytes 37302272 | tf_op jit(solution)/shard_map/dot_general | solution.py:37
  174.8 64.5 %pmax.7 = f32[1024]{0:T(1024)S(1)} all-reduce(f32[1024]{0:T(1024)S(1)} %get-tuple-element.110), channel_id=1, replica_groups=mesh['stream'=16,'tensor'=8] {'stream','tensor'}, use_global_device_ids=true, to_apply=%region_2.0 | all-reduce | flops 1024 | bytes 8192 | tf_op jit(solution)/shard_map/pmax | solution.py:49
  239.3 2.8 fusion.1
  242.1 64.4 %all-reduce = (f32[]{:T(128)}, f32[1024]{0:T(1024)S(1)}) all-reduce(f32[]{:T(128)} %convert_reduce_fusion, f32[1024]{0:T(1024)S(1)} %fusion.1), channel_id=1, replica_groups=mesh['stream'=16,'tensor'=8] {'stream','tensor'}, use_global_device_ids=true, to_apply=%region_6.0 | all-reduce | flops 1025 | bytes 8200 | tf_op jit(solution)/shard_map/psum | solution.py:51
  306.4 0.7 broadcast_subtract_fusion
  307.2 4.6 %select_reduce_fusion = (f32[1024]{0:T(1024)S(1)}, f32[1024]{0:T(1024)S(1)}, f32[1024,1002]{0,1:T(8,128)}) fusion(s32[1024]{0:T(1024)S(1)} %copy-done.2, s32[1002]{0:T(1024)S(1)} %iota_add_fusion, f32[1024]{0:T(1024)S(1)} %convert_element_type.20, f32[1024]{0:T(1024)S(1)} %broadcast_subtract_fusion, f32[1024]{0:T(1024)S(1)} %get-tuple-element.108, ...), kind=kLoop, calls=%fused_computation.2 | loop fusion | flops 9232384 | bytes 8245072 | tf_op jit(solution)/shard_map/reduce_sum | solution.py:57
  311.8 33.5 %all-gather = f32[131072]{0:T(1024)S(1)} all-gather(f32[1024]{0:T(1024)S(1)} %get-tuple-element.98), channel_id=2, replica_groups=mesh['stream'=16,'tensor'=8] {'stream','tensor'}, dimensions={0}, use_global_device_ids=true | all-gather | bytes 528384 | tf_op jit(solution)/shard_map/all_gather | solution.py:11
  345.3 0.1 reshape.25
  345.4 6.9 %while.14 = (s32[]{:T(128)}, f32[1024]{0:T(1024)S(1)}, s32[]{:T(128)}, f32[128,1024]{1,0:T(8,128)S(1)}, s32[]{:T(128)}, /*index=5*/s32[]{:T(128)}) while((s32[]{:T(128)}, f32[1024]{0:T(1024)S(1)}, s32[]{:T(128)}, f32[128,1024]{1,0:T(8,128)S(1)}, s32[]{:T(128)}, /*index=5*/s32[]{:T(128)}) %tuple.39), condition=%wide.region_9.10_spmd.clone, body=%wide.region_8.9_spmd.clone.sunk | while | flops 3076 | bytes 20573 | solution.py:18
  352.3 63.1 %psum.23 = f32[1024]{0:T(1024)S(1)} all-reduce(f32[1024]{0:T(1024)S(1)} %get-tuple-element.97), channel_id=1, replica_groups=mesh['stream'=16,'tensor'=8] {'stream','tensor'}, use_global_device_ids=true, to_apply=%region_11.12 | all-reduce | flops 1024 | bytes 8192 | tf_op jit(solution)/shard_map/psum | solution.py:59
  415.3 0.6 multiply_negate_fusion
  415.9 9.8 %broadcast_add_fusion = f32[1024,1002]{0,1:T(8,128)} fusion(f32[1024]{0:T(1024)S(1)} %get-tuple-element.81, f32[1024,1002]{0,1:T(8,128)} %get-tuple-element.109), kind=kOutput, calls=%fused_computation.13 | convolution fusion | flops 12339230720 | bytes 8212480 | tf_op jit(solution)/shard_map/dot_general | solution.py:62
  (263 shorter events, 2.3 us)
Async XLA Ops:
  7.2 32.5 %copy-start = (s32[1002]{0:T(1024)S(1)}, s32[1002]{0:T(1024)}, u32[]{:S(2)}) copy-start(s32[1002]{0:T(1024)} %param.11) | copy-start | bytes 12028
  7.2 32.5 %copy-start.1 = (s32[1024]{0:T(1024)S(1)}, s32[1024]{0:T(1024)}, u32[]{:S(2)}) copy-start(s32[1024]{0:T(1024)} %param.12) | copy-start | bytes 12292
  7.2 28.4 %all-gather.4.cloned.1.call-start = ((), (), s32[]{:S(2)}) async-start(), calls=%async_computation | async-start | bytes 1179648 | tf_op jit(solution)/shard_map/all_gather | solution.py:35
  7.9 143.2 %all-gather.6.cloned.1.call-start = ((), (), s32[]{:S(2)}) async-start(), calls=%async_computation.1 | async-start | bytes 17825792 | tf_op jit(solution)/shard_map/all_gather | solution.py:38
  174.8 132.3 %copy-start.2 = (s32[1024]{0:T(1024)S(1)}, s32[1024]{0:T(1024)}, u32[]{:S(2)}) copy-start(s32[1024]{0:T(1024)} %param.13) | copy-start | bytes 12292
Sparse Core Ops, SparseCore 0:
  9.7 25.8 all-gather.3
  39.8 111.3 all-gather.5
where the time goes:
time: 434 us; the launch traced here: 433 us
  blocking collectives  225 us (52%)
  waiting for transfers between devices  138 us (32%)
  matrix products  33.5 us (8%)
  other arithmetic  15 us (3%)
  between operations  14.2 us (3%)
  loops' own time  4.61 us (1%)
    all_gather x1, waiting for transfers between devices, local(): lax.all_gather(normed, 'stream', axis=0, tiled=True)  111 us
    pmax x1, blocking collectives, local(): row_peak = lax.pmax(local_peak, ('stream', 'tensor'))  64.5 us
    psum x1, blocking collectives, local(): lax.psum((jnp.sum(exponent, axis=1), floor_local), ('stream', 'tensor'))  64.4 us
    psum x1, blocking collectives, local(): picked = lax.psum(picked_local, ('stream', 'tensor'))  63.1 us
    all_gather x1, blocking collectives, prefix(): pieces = lax.all_gather(value, axis)  33.5 us
    all_gather x1, waiting for transfers between devices, local(): gathered = lax.all_gather(hidden, 'tensor', axis=1, tiled=True)  26.9 us
    dot_general x1, matrix products, local(): jnp.dot(lax.all_gather(normed, 'stream', axis=0, tiled=True), head_weight...  23.7 us
    dot_general x1, matrix products, local(): within = jnp.dot(quantized, upper_mask, precision=lax.Precision.HIGHEST)  9.82 us
  transfers between devices with their start and end apart: 2, of which 2 were waited for; matrix products, arithmetic and copies ran while one was open for 0% of the time, Pallas kernels for 0%

commit v1 on v0

v1 whole, which is shorter than its diff:
```python
import jax
import jax.numpy as jnp
from jax import lax
from jax.experimental import pallas as pl
from jax.experimental.pallas import tpu as pltpu
from jax.sharding import PartitionSpec as P

epsilon = 1e-05
STREAM, TENSOR = "stream", "tensor"
BOTH = (STREAM, TENSOR)
SIZES = {"x": 4, "z": 4, "y": 4, "c": 2}
STRIDES = {"x": 32, "z": 8, "y": 2, "c": 1}
ROWS = 8
VMEM = pl.BlockSpec(memory_space=pltpu.VMEM)


def coordinate(axis):
    index = lax.axis_index(STREAM) * 8 + lax.axis_index(TENSOR)
    return lax.rem(lax.div(index, STRIDES[axis]), SIZES[axis])


def shift(value, axis, hops):
    size, stride = SIZES[axis], STRIDES[axis]
    pairs = []
    for source in range(128):
        place = source // stride % size
        pairs.append((source, source + ((place + hops) % size - place) * stride))
    return lax.ppermute(value, BOTH, pairs)


def call(body, out_shape, name, inputs, vmem_mib=32, scratch=(), out_specs=VMEM, **rest):
    return pl.pallas_call(
        body,
        out_shape=out_shape,
        in_specs=[VMEM] * len(inputs),
        out_specs=out_specs,
        scratch_shapes=list(scratch),
        compiler_params=pltpu.CompilerParams(vmem_limit_bytes=vmem_mib << 20),
        name=name,
        **rest,
    )(*inputs)


def local_stats(logits, floors, targets, first_column):
    entries = logits.shape[0]

    def body(first_ref, logits_ref, floors_ref, targets_ref, stats_ref):
        floors = floors_ref[...]
        total = jnp.sum(floors, axis=0, keepdims=True)
        rows = lax.broadcasted_iota(jnp.int32, (entries, 128), 0)
        for j in range(ROWS):
            tile = logits_ref[:, j * 128:(j + 1) * 128]
            peak = jnp.max(tile, axis=0, keepdims=True)
            exponent = jnp.exp(tile - peak)
            hit = rows == targets_ref[j:j + 1, :] - first_ref[0]
            stats_ref[j:j + 1, :] = peak
            stats_ref[8 + j:9 + j, :] = jnp.sum(exponent, axis=0, keepdims=True)
            stats_ref[16 + j:17 + j, :] = jnp.sum(jnp.where(hit, exponent, 0.0), axis=0, keepdims=True)
            stats_ref[24 + j:25 + j, :] = jnp.sum(jnp.where(hit, floors, 0.0), axis=0, keepdims=True)
            stats_ref[32 + j:33 + j, :] = total

    return pl.pallas_call(
        body,
        out_shape=jax.ShapeDtypeStruct((40, 128), jnp.float32),
        in_specs=[pl.BlockSpec(memory_space=pltpu.SMEM), VMEM, VMEM, VMEM],
        out_specs=VMEM,
        compiler_params=pltpu.CompilerParams(vmem_limit_bytes=32 << 20),
        name="local_stats",
    )(first_column, logits, floors, targets)


def running_sums(logits, floors, stats):
    entries, tokens = logits.shape
    block = 256
    blocks = -(-entries // block)

    def body(logits_ref, floors_ref, stats_ref, sums_ref, floor_sums_ref, tail, floor_tail):
        below = lax.broadcasted_iota(jnp.int32, (block, block), 1)
        lower = (below < lax.broadcasted_iota(jnp.int32, (block, block), 0)).astype(jnp.bfloat16)
        carry = [jnp.zeros((1, 128), jnp.float32)] * (ROWS + 1)
        for b in range(blocks):
            start, size = b * block, min(block, entries - b * block)
            for j in range(ROWS + 1):
                lanes = slice(j * 128, (j + 1) * 128)
                if j < ROWS:
                    value = jnp.exp(logits_ref[start:start + size, lanes] - stats_ref[j:j + 1, :])
                else:
                    value = floors_ref[start:start + size, :]
                if size < block:
                    tail[...] = jnp.zeros_like(tail)
                    tail[:size, :] = value
                    value = tail[...]
                high = value.astype(jnp.bfloat16)
                low = (value - high.astype(jnp.float32)).astype(jnp.bfloat16)
                partial = (
                    jnp.dot(lower, high, preferred_element_type=jnp.float32)
                    + jnp.dot(lower, low, preferred_element_type=jnp.float32)
                    + carry[j]
                )
                if j < ROWS:
                    sums_ref[start:start + size, lanes] = partial[:size]
                else:
                    floor_sums_ref[start:start + size, :] = partial[:size]
                carry[j] = carry[j] + jnp.sum(value, axis=0, keepdims=True)

    return call(
        body,
        (
            jax.ShapeDtypeStruct((entries, tokens), jnp.float32),
            jax.ShapeDtypeStruct((entries, 128), jnp.float32),
        ),
        "running_sums",
        (logits, floors, stats),
        scratch=[pltpu.VMEM((block, 128), jnp.float32), pltpu.VMEM((block, 128), jnp.float32)],
        out_specs=(VMEM, VMEM),
        cost_estimate=pl.CostEstimate(flops=2 * 2 * 256 * 1024 * 1024, bytes_accessed=8 << 20, transcendentals=1 << 20),
    )


def join(axis, stats, before, last=None):
    size = SIZES[axis]
    pieces = [stats] + [shift(stats, axis, k) for k in range(1, size)]

    def body(*refs):
        piece_refs, before_ref = refs[:size], refs[size]
        rest = refs[size + 1:]
        held = rest[-1]
        mine = coordinate(axis)
        for k in range(size):
            held[lax.rem(mine - k + size, size)] = piece_refs[k][...]
        peak = held[0, 0:8]
        for i in range(1, size):
            peak = jnp.maximum(peak, held[i, 0:8])
        mass = target = floor = total = jnp.zeros((8, 128), jnp.float32)
        mass_before = before_ref[0:8] * jnp.exp(piece_refs[0][0:8] - peak)
        total_before = before_ref[8:16]
        for i in range(size):
            scale = jnp.exp(held[i, 0:8] - peak)
            part = held[i, 8:16] * scale
            mass = mass + part
            target = target + held[i, 16:24] * scale
            floor = floor + held[i, 24:32]
            total = total + held[i, 32:40]
            earlier = i < mine
            mass_before = mass_before + jnp.where(earlier, part, 0.0)
            total_before = total_before + jnp.where(earlier, held[i, 32:40], 0.0)
        if last is None:
            stats_ref, after_ref = rest[0], rest[1]
            stats_ref[0:8] = peak
            stats_ref[8:16] = mass
            stats_ref[16:24] = target
            stats_ref[24:32] = floor
            stats_ref[32:40] = total
            after_ref[0:8] = mass_before
            after_ref[8:16] = total_before
        else:
            own_ref, totals_ref, terms_ref, bits_ref = rest[:4]
            tokens = totals_ref[...].astype(jnp.float32)
            free = (tokens - total) / mass
            terms_ref[0:8] = jnp.exp(own_ref[0:8] - peak) * free / tokens
            terms_ref[8:16] = 1.0 / tokens
            terms_ref[16:24] = (total_before + mass_before * free) / tokens
            bits_ref[...] = -jnp.log2((floor + target * free) / tokens)

    inputs = pieces + [before] + ([] if last is None else list(last))
    first, second = ((40, 128), (16, 128)) if last is None else ((24, 128), (8, 128))
    return call(
        body,
        (jax.ShapeDtypeStruct(first, jnp.float32), jax.ShapeDtypeStruct(second, jnp.float32)),
        "join_" + axis,
        inputs,
        vmem_mib=4,
        scratch=[pltpu.VMEM((size, 40, 128), jnp.float32)],
        out_specs=(VMEM, VMEM),
    )


def finish(sums, floor_sums, terms):
    entries, tokens = sums.shape
    block = 168

    def body(sums_ref, floors_ref, terms_ref, out_ref):
        for j in range(ROWS):
            lanes = slice(j * 128, (j + 1) * 128)
            out_ref[:, lanes] = (
                sums_ref[:, lanes] * terms_ref[j:j + 1, :]
                + floors_ref[...] * terms_ref[8 + j:9 + j, :]
                + terms_ref[16 + j:17 + j, :]
            )

    return pl.pallas_call(
        body,
        grid=(-(-entries // block),),
        out_shape=jax.ShapeDtypeStruct((entries, tokens), jnp.float32),
        in_specs=[
            pl.BlockSpec((block, tokens), lambda i: (i, 0)),
            pl.BlockSpec((block, 128), lambda i: (i, 0)),
            pl.BlockSpec((24, 128), lambda i: (0, 0)),
        ],
        out_specs=pl.BlockSpec((block, tokens), lambda i: (i, 0)),
        compiler_params=pltpu.CompilerParams(vmem_limit_bytes=16 << 20),
        name="finish",
    )(sums, floor_sums, terms)


def outputs(logits, floor_counts, totals, targets):
    entries = logits.shape[0]
    floors = jnp.broadcast_to(floor_counts.astype(jnp.float32)[:, None], (entries, 128))
    first_column = (lax.axis_index(STREAM) * 8 + lax.axis_index(TENSOR)) * entries
    stats = local_stats(logits, floors, targets.reshape(8, 128), first_column.reshape(1))
    group, before = stats, jnp.zeros((16, 128), jnp.float32)
    sums, floor_sums = running_sums(logits, floors, stats)
    for axis in ("c", "y", "z"):
        group, before = join(axis, group, before)
    terms, bits = join("x", group, before, last=(stats, totals.reshape(8, 128)))
    cumulative = finish(sums, floor_sums, terms)
    return cumulative.T, bits.reshape(1024)


def normalize(features, norm_gain):
    widened = features.astype(jnp.float32)
    mean_square = jnp.mean(widened * widened, axis=1, keepdims=True)
    return (
        widened * lax.rsqrt(mean_square + epsilon) * norm_gain.astype(jnp.float32)[None, :]
    ).astype(jnp.bfloat16)


def local(hidden, norm_gain, head_weight, floor_counts, totals, targets):
    gathered = lax.all_gather(hidden, TENSOR, axis=1, tiled=True)
    normed = normalize(gathered, norm_gain)
    everyone = lax.all_gather(normed, STREAM, axis=0, tiled=True)
    logits = lax.dot_general(
        head_weight, everyone, (((0,), (1,)), ((), ())), preferred_element_type=jnp.float32
    )
    return outputs(logits, floor_counts, totals, targets)


def solution(mesh):
    in_specs = (
        P(STREAM, TENSOR),
        P(),
        P(None, BOTH),
        P(BOTH),
        P(),
        P(),
    )
    out_specs = (P(None, BOTH), P())
    return jax.shard_map(local, mesh=mesh, in_specs=in_specs, out_specs=out_specs, check_vma=False)
```

time: 434 us -> 210 us (0.48)
  blocking collectives: 225 us -> 0 us
  starting transfers between devices: 0.08 us -> 15.6 us
  matrix products: 33.5 us -> 21.7 us
  other arithmetic: 15 us -> 4.77 us
  Pallas kernels: 0 us -> 8.67 us
  waiting for transfers between devices: 138 us -> 145 us
  loops' own time: 4.61 us -> 0 us
    psum x2 -> x0, blocking collectives: 127 us -> none  [the longest x1 64.4 us: local(): lax.psum((jnp.sum(exponent, axis=1), floor_local), ('stream', 'tensor'))]
    pmax x1 -> x0, blocking collectives: 64.5 us -> none  [local(): row_peak = lax.pmax(local_peak, ('stream', 'tensor'))]
    all_gather x1 -> x0, blocking collectives: 33.5 us -> none  [prefix(): pieces = lax.all_gather(value, axis)]
    ppermute x0 -> x10, starting transfers between devices: none -> 15.5 us  [shift(): return lax.ppermute(value, BOTH, pairs)]
    dot_general x2 -> x1, matrix products: 33.5 us -> 21.7 us  [local(): lax.dot_general(head_weight, everyone, (((0,), (1,)), ((), ())), preferre...]
    pallas_call x0 -> x7, Pallas kernels: none -> 8.67 us  [the longest x5 3.39 us: call(): pl.pallas_call(body, out_shape=out_shape, in_specs=[VMEM] * len(inputs),...]
    reduce_sum x3 -> x0, other arithmetic: 8.07 us -> none  [the longest x1 4.61 us: local(): picked_local = jnp.sum(jnp.where(target_hit, quantized, 0.0), axis=1)]
    ppermute x0 -> x10, waiting for transfers between devices: none -> 5.95 us  [shift(): return lax.ppermute(value, BOTH, pairs)]
  transfers between devices with their start and end apart: 2 -> 12, of which waited for: 2 -> 7; matrix products, arithmetic and copies ran while one was open for 0% -> 0% of each run, Pallas kernels for 0% -> 1%
where the time goes in v1:
time: 210 us
  waiting for transfers between devices  145 us (69%)
  matrix products  21.7 us (10%)
  starting transfers between devices  15.6 us (7%)
  between operations  14.2 us (7%)
  Pallas kernels  8.67 us (4%)
  other arithmetic  4.77 us (2%)
    all_gather x1, waiting for transfers between devices, local(): everyone = lax.all_gather(normed, STREAM, axis=0, tiled=True)  111 us
    all_gather x1, waiting for transfers between devices, local(): gathered = lax.all_gather(hidden, TENSOR, axis=1, tiled=True)  26.9 us
    dot_general x1, matrix products, local(): lax.dot_general(head_weight, everyone, (((0,), (1,)), ((), ())), preferre...  21.7 us
    ppermute x10, starting transfers between devices, shift(): return lax.ppermute(value, BOTH, pairs)  15.5 us
    ppermute x10, waiting for transfers between devices, shift(): return lax.ppermute(value, BOTH, pairs)  5.95 us
  transfers between devices with their start and end apart: 12, of which 7 were waited for; matrix products, arithmetic and copies ran while one was open for 0% of the time, Pallas kernels for 1%

profile of v1, /device:TPU:0, one launch (start us, length us, event | category | flops | bytes accessed | tf_op | source)
XLA Modules:
  0.0 210.1 jit_solution(4455272321368683250)
XLA Ops:
  7.2 0.7 all-gather.3.cloned.1.call-update
  8.0 0.7 convert_element_type.13
  8.7 26.9 %all-gather.3.cloned.1.call-done = bf16[64,8192]{1,0:T(8,128)(2,1)} async-done(((bf16[64,1024]{1,0:T(8,128)(2,1)}), bf16[64,8192]{1,0:T(8,128)(2,1)}) %all-gather.3.cloned.1.call-update) | async-done | bytes 1048592 | tf_op jit(solution)/shard_map/all_gather | solution.py:229
  35.6 1.5 fusion
  37.1 2.5 %fusion.2 = bf16[64,8192]{1,0:T(8,128)(2,1)} fusion(bf16[64,8192]{1,0:T(8,128)(2,1)} %all-gather.3.cloned.1.call-done, f32[8192]{0:T(1024)S(1)} %convert_element_type.13, f32[64]{0:T(128)S(1)} %add_rsqrt_fusion), kind=kLoop, calls=%fused_computation.5 | loop fusion | flops 2097152 | bytes 2130176 | tf_op jit(solution)/shard_map/convert_element_type | solution.py:225
  39.7 111.4 %all-gather.5.cloned.1.call-done = bf16[1024,8192]{1,0:T(8,128)(2,1)} async-done(((bf16[64,8192]{1,0:T(8,128)(2,1)}), bf16[1024,8192]{1,0:T(8,128)(2,1)}) %all-gather.5.cloned.1.call-update) | async-done | bytes 16777232 | tf_op jit(solution)/shard_map/all_gather | solution.py:231
  151.1 21.7 %convolution_bitcast_fusion.logits_ref = f32[1002,1024]{1,0:T(8,128)S(1)} fusion(bf16[1024,8192]{1,0:T(8,128)(2,1)} %all-gather.5.cloned.1.call-done, bf16[8192,1002]{0,1:T(8,128)(2,1)} %param.8), kind=kOutput, calls=%fused_computation.2 | convolution fusion | flops 16810770432 | bytes 37298176 | tf_op jit(solution)/shard_map/dot_general | solution.py:232
  173.0 2.2 %local_stats.1.stats_ref.refs_0_.refs_5_ = f32[40,128]{1,0:T(8,128)S(1)} custom-call(s32[1]{0:T(128)} %bitcast.1.first_ref, f32[1002,1024]{1,0:T(8,128)S(1)} %convolution_bitcast_fusion.logits_ref, f32[1002,128]{1,0:T(8,128)S(1)} %broadcast_in_dim.4.floors_ref, s32[8,128]{1,0:T(8,128)S(1)} %bitcast.9), custom_call_target="tpu_custom_call" | custom-call | tf_op jit(solution)/shard_map/local_stats/pallas_call | solution.py:62
  175.3 1.2 collective-permute-done.refs_1_
  176.5 1.6 collective-permute-start.1
  178.1 2.7 %collective-permute-start.2 = (f32[40,128]{1,0:T(8,128)S(1)}, f32[40,128]{1,0:T(8,128)S(1)}, u32[]{:S(2)}, u32[]{:S(2)}) collective-permute-start(f32[40,128]{1,0:T(8,128)S(1)} %get-tuple-element.14.refs_0_), channel_id=1, source_target_pairs={{0,4},{1,5},{2,6},{3,7},{4,0},{5,1},{6,2},{7,3},{8,12},{9,13},{10,... | collective-permute-start | bytes 61448 | tf_op jit(solution)/shard_map/ppermute | solution.py:28
  180.8 1.4 collective-permute-start.3
  182.2 1.1 collective-permute-done.2.refs_2_
  183.4 1.2 collective-permute-done.3.refs_3_
  184.6 1.4 collective-permute-start.4
  186.0 2.9 %collective-permute-start.5 = (f32[40,128]{1,0:T(8,128)S(1)}, f32[40,128]{1,0:T(8,128)S(1)}, u32[]{:S(2)}, u32[]{:S(2)}) collective-permute-start(f32[40,128]{1,0:T(8,128)S(1)} %get-tuple-element.16.refs_0_), channel_id=1, source_target_pairs={{0,16},{1,17},{2,18},{3,19},{4,20},{5,21},{6,22},{7,23},{8,24},{9,... | collective-permute-start | bytes 61448 | tf_op jit(solution)/shard_map/ppermute | solution.py:28
  188.8 1.4 collective-permute-start.6
  190.2 1.1 collective-permute-done.5.refs_2_
  191.3 1.3 collective-permute-done.6.refs_3_
  192.9 2.1 collective-permute-start.8
  195.0 1.8 collective-permute-start.9
  196.8 2.6 %running_sums.1 = (f32[1002,1024]{1,0:T(8,128)S(1)}, f32[1002,128]{1,0:T(8,128)S(1)}) custom-call(f32[1002,1024]{1,0:T(8,128)S(1)} %convolution_bitcast_fusion.logits_ref, f32[1002,128]{1,0:T(8,128)S(1)} %broadcast_in_dim.4.floors_ref, f32[40,128]{1,0:T(8,128)S(1)} %local_stats.1.stats_ref.refs_0_.refs_5_), custom_call_target="tpu_custom_call" | custom-call | flops 1073741824 | bytes 8388608 | tf_op jit(solution)/shard_map/running_sums/pallas_call | solution.py:32
  199.5 0.7 join_x.1
  200.2 3.1 %finish.1 = f32[1002,1024]{1,0:T(8,128)} custom-call(f32[1002,1024]{1,0:T(8,128)S(1)} %get-tuple-element.12.sums_ref, f32[1002,128]{1,0:T(8,128)S(1)} %get-tuple-element.13.floors_ref, f32[24,128]{1,0:T(8,128)S(1)} %get-tuple-element.20.terms_ref), custom_call_target="tpu_custom_call" | custom-call | tf_op jit(solution)/shard_map/finish/pallas_call | solution.py:191
  (23 shorter events, 0.8 us)
Async XLA Ops:
  7.2 32.5 %copy-start.2 = (s32[1002]{0:T(1024)S(1)}, s32[1002]{0:T(1024)}, u32[]{:S(2)}) copy-start(s32[1002]{0:T(1024)} %param.9) | copy-start | bytes 12028
  7.2 28.4 %all-gather.3.cloned.1.call-start = ((), (), s32[]{:S(2)}) async-start(), calls=%async_computation | async-start | bytes 1179648 | tf_op jit(solution)/shard_map/all_gather | solution.py:229
  7.9 143.2 %all-gather.5.cloned.1.call-start = ((), (), s32[]{:S(2)}) async-start(), calls=%async_computation.1 | async-start | bytes 17825792 | tf_op jit(solution)/shard_map/all_gather | solution.py:231
  39.7 133.3 %copy-start = (s32[1024]{0:T(1024)S(1)}, s32[1024]{0:T(1024)}, u32[]{:S(2)}) copy-start(s32[1024]{0:T(1024)} %param.11) | copy-start | bytes 12292
  173.0 26.5 %copy-start.1 = (s32[1024]{0:T(1024)S(1)}, s32[1024]{0:T(1024)}, u32[]{:S(2)}) copy-start(s32[1024]{0:T(1024)} %param.10) | copy-start | bytes 12292
  175.2 1.3 collective-permute-start
  176.5 5.7 %collective-permute-start.1 = (f32[40,128]{1,0:T(8,128)S(1)}, f32[40,128]{1,0:T(8,128)S(1)}, u32[]{:S(2)}, u32[]{:S(2)}) collective-permute-start(f32[40,128]{1,0:T(8,128)S(1)} %get-tuple-element.14.refs_0_), channel_id=1, source_target_pairs={{0,2},{1,3},{2,4},{3,5},{4,6},{5,7},{6,0},{7,1},{8,10},{9,11},{10,... | collective-permute-start | bytes 61448 | tf_op jit(solution)/shard_map/ppermute | solution.py:28
  178.1 5.3 %collective-permute-start.2 = (f32[40,128]{1,0:T(8,128)S(1)}, f32[40,128]{1,0:T(8,128)S(1)}, u32[]{:S(2)}, u32[]{:S(2)}) collective-permute-start(f32[40,128]{1,0:T(8,128)S(1)} %get-tuple-element.14.refs_0_), channel_id=1, source_target_pairs={{0,4},{1,5},{2,6},{3,7},{4,0},{5,1},{6,2},{7,3},{8,12},{9,13},{10,... | collective-permute-start | bytes 61448 | tf_op jit(solution)/shard_map/ppermute | solution.py:28
  180.8 3.8 %collective-permute-start.3 = (f32[40,128]{1,0:T(8,128)S(1)}, f32[40,128]{1,0:T(8,128)S(1)}, u32[]{:S(2)}, u32[]{:S(2)}) collective-permute-start(f32[40,128]{1,0:T(8,128)S(1)} %get-tuple-element.14.refs_0_), channel_id=1, source_target_pairs={{0,6},{1,7},{2,0},{3,1},{4,2},{5,3},{6,4},{7,5},{8,14},{9,15},{10,... | collective-permute-start | bytes 61448 | tf_op jit(solution)/shard_map/ppermute | solution.py:28
  184.6 5.6 %collective-permute-start.4 = (f32[40,128]{1,0:T(8,128)S(1)}, f32[40,128]{1,0:T(8,128)S(1)}, u32[]{:S(2)}, u32[]{:S(2)}) collective-permute-start(f32[40,128]{1,0:T(8,128)S(1)} %get-tuple-element.16.refs_0_), channel_id=1, source_target_pairs={{0,8},{1,9},{2,10},{3,11},{4,12},{5,13},{6,14},{7,15},{8,16},{9,17... | collective-permute-start | bytes 61448 | tf_op jit(solution)/shard_map/ppermute | solution.py:28
  186.0 5.3 %collective-permute-start.5 = (f32[40,128]{1,0:T(8,128)S(1)}, f32[40,128]{1,0:T(8,128)S(1)}, u32[]{:S(2)}, u32[]{:S(2)}) collective-permute-start(f32[40,128]{1,0:T(8,128)S(1)} %get-tuple-element.16.refs_0_), channel_id=1, source_target_pairs={{0,16},{1,17},{2,18},{3,19},{4,20},{5,21},{6,22},{7,23},{8,24},{9,... | collective-permute-start | bytes 61448 | tf_op jit(solution)/shard_map/ppermute | solution.py:28
  188.8 3.8 %collective-permute-start.6 = (f32[40,128]{1,0:T(8,128)S(1)}, f32[40,128]{1,0:T(8,128)S(1)}, u32[]{:S(2)}, u32[]{:S(2)}) collective-permute-start(f32[40,128]{1,0:T(8,128)S(1)} %get-tuple-element.16.refs_0_), channel_id=1, source_target_pairs={{0,24},{1,25},{2,26},{3,27},{4,28},{5,29},{6,30},{7,31},{8,0},{9,1... | collective-permute-start | bytes 61448 | tf_op jit(solution)/shard_map/ppermute | solution.py:28
  192.6 6.8 %collective-permute-start.7 = (f32[40,128]{1,0:T(8,128)S(1)}, f32[40,128]{1,0:T(8,128)S(1)}, u32[]{:S(2)}, u32[]{:S(2)}) collective-permute-start(f32[40,128]{1,0:T(8,128)S(1)} %get-tuple-element.18.refs_0_), channel_id=1, source_target_pairs={{0,32},{1,33},{2,34},{3,35},{4,36},{5,37},{6,38},{7,39},{8,40},{9,... | collective-permute-start | bytes 61448 | tf_op jit(solution)/shard_map/ppermute | solution.py:28
  192.9 6.5 %collective-permute-start.8 = (f32[40,128]{1,0:T(8,128)S(1)}, f32[40,128]{1,0:T(8,128)S(1)}, u32[]{:S(2)}, u32[]{:S(2)}) collective-permute-start(f32[40,128]{1,0:T(8,128)S(1)} %get-tuple-element.18.refs_0_), channel_id=1, source_target_pairs={{0,64},{1,65},{2,66},{3,67},{4,68},{5,69},{6,70},{7,71},{8,72},{9,... | collective-permute-start | bytes 61448 | tf_op jit(solution)/shard_map/ppermute | solution.py:28
  195.0 4.4 %collective-permute-start.9 = (f32[40,128]{1,0:T(8,128)S(1)}, f32[40,128]{1,0:T(8,128)S(1)}, u32[]{:S(2)}, u32[]{:S(2)}) collective-permute-start(f32[40,128]{1,0:T(8,128)S(1)} %get-tuple-element.18.refs_0_), channel_id=1, source_target_pairs={{0,96},{1,97},{2,98},{3,99},{4,100},{5,101},{6,102},{7,103},{8,104... | collective-permute-start | bytes 61448 | tf_op jit(solution)/shard_map/ppermute | solution.py:28
Sparse Core Ops, SparseCore 0:
  9.7 25.8 all-gather.2
  39.8 111.3 all-gather.4

commit v2 on v1

v2 whole, which is shorter than its diff:
```python
import jax
import jax.numpy as jnp
from jax import lax
from jax.experimental import pallas as pl
from jax.experimental.pallas import tpu as pltpu
from jax.sharding import PartitionSpec as P

epsilon = 1e-05
STREAM, TENSOR = "stream", "tensor"
BOTH = (STREAM, TENSOR)
SIZES = {"x": 4, "z": 4, "y": 4, "c": 2}
STRIDES = {"x": 32, "z": 8, "y": 2, "c": 1}
ROWS = 8
VMEM = pl.BlockSpec(memory_space=pltpu.VMEM)


def coordinate(axis):
    index = lax.axis_index(STREAM) * 8 + lax.axis_index(TENSOR)
    return lax.rem(lax.div(index, STRIDES[axis]), SIZES[axis])


def shift(value, axis, hops):
    pairs = []
    for source in range(128):
        name = axis[source % len(axis)]
        size, stride = SIZES[name], STRIDES[name]
        place = source // stride % size
        pairs.append((source, source + ((place + hops) % size - place) * stride))
    return lax.ppermute(value, BOTH, pairs)


def call(body, out_shape, name, inputs, vmem_mib=32, scratch=(), out_specs=VMEM, **rest):
    return pl.pallas_call(
        body,
        out_shape=out_shape,
        in_specs=[VMEM] * len(inputs),
        out_specs=out_specs,
        scratch_shapes=list(scratch),
        compiler_params=pltpu.CompilerParams(vmem_limit_bytes=vmem_mib << 20),
        name=name,
        **rest,
    )(*inputs)


def prepare(floor_counts, gain, targets):
    entries = floor_counts.shape[1]

    def body(floors_ref, gain_ref, targets_ref, columns_ref, gain_out_ref, stats_ref, row):
        row[...] = jnp.zeros_like(row)
        row[:, 0:entries] = jnp.broadcast_to(floors_ref[...].astype(jnp.float32), (8, entries))
        total = jnp.zeros((1, 128), jnp.float32)
        picked = [jnp.zeros((1, 128), jnp.float32)] * ROWS
        for b in range(ROWS):
            columns = jnp.transpose(jnp.concatenate([row[:, b * 128:(b + 1) * 128]] * 16, axis=0))
            columns_ref[b * 128:(b + 1) * 128, :] = columns
            total = total + jnp.sum(columns, axis=0, keepdims=True)
            rows = lax.broadcasted_iota(jnp.int32, (128, 128), 0) + (b * 128 + first_entry(entries))
            for j in range(ROWS):
                hit = jnp.where(rows == targets_ref[j:j + 1, :], columns, 0.0)
                picked[j] = picked[j] + jnp.sum(hit, axis=0, keepdims=True)
        stats_ref[0:8] = jnp.concatenate(picked, axis=0)
        stats_ref[8:16] = jnp.broadcast_to(total, (8, 128))
        gain_out_ref[...] = gain_ref[...].astype(jnp.float32).reshape(1, 8192)

    return call(
        body,
        (
            jax.ShapeDtypeStruct((1024, 128), jnp.float32),
            jax.ShapeDtypeStruct((1, 8192), jnp.float32),
            jax.ShapeDtypeStruct((16, 128), jnp.float32),
        ),
        "prepare",
        (floor_counts, gain, targets),
        vmem_mib=4,
        scratch=[pltpu.VMEM((8, 1024), jnp.float32)],
        out_specs=(VMEM, VMEM, VMEM),
    )


def first_entry(entries):
    return (lax.axis_index(STREAM) * 8 + lax.axis_index(TENSOR)) * entries


def join_halves(products, floor_stats, targets):
    entries = products.shape[2]

    def body(products_ref, floors_ref, targets_ref, logits_ref, stats_ref):
        core = lax.rem(lax.axis_index(TENSOR), 2)
        first = first_entry(entries)
        rows = lax.broadcasted_iota(jnp.int32, (entries, 128), 0)
        left = lax.broadcasted_iota(jnp.int32, (entries, 128), 1) < 64
        logits_ref[1000:1024, :] = jnp.full((24, 1024), -jnp.inf, jnp.float32)
        for j in range(ROWS):
            x, z = j // 2, j % 2 * 2
            near = slice(x // 2 * 128, x // 2 * 128 + 128)
            one, two = products_ref[core, z, :, near], products_ref[core, z + 1, :, near]
            if x % 2 == 0:
                two = pltpu.roll(two, 64, 1)
            else:
                one = pltpu.roll(one, 64, 1)
            tile = products_ref[1 - core, x, :, z * 64:z * 64 + 128] + jnp.where(left, one, two)
            logits_ref[0:entries, j * 128:(j + 1) * 128] = tile
            peak = jnp.max(tile, axis=0, keepdims=True)
            exponent = jnp.exp(tile - peak)
            hit = rows == targets_ref[j:j + 1, :] - first
            stats_ref[j:j + 1, :] = peak
            stats_ref[8 + j:9 + j, :] = jnp.sum(exponent, axis=0, keepdims=True)
            stats_ref[16 + j:17 + j, :] = jnp.sum(jnp.where(hit, exponent, 0.0), axis=0, keepdims=True)
        stats_ref[24:40, :] = floors_ref[...]

    return call(
        body,
        (
            jax.ShapeDtypeStruct((1024, 1024), jnp.float32),
            jax.ShapeDtypeStruct((40, 128), jnp.float32),
        ),
        "join_halves",
        (products, floor_stats, targets),
        vmem_mib=6,
        out_specs=(VMEM, VMEM),
    )


def join(axis, stats, before, last=None):
    size = SIZES[axis]
    hops = [0, 1] if size == 2 else [0, 1, 3, 2]
    pieces = [stats] + [shift(stats, axis, k) for k in hops[1:]]

    def body(*refs):
        piece_refs, rest = refs[:size], refs[size:]
        if before is not None:
            before_ref, rest = rest[0], rest[1:]
        held = rest[-1]
        mine = coordinate(axis)
        for piece_ref, k in zip(piece_refs, hops):
            held[lax.rem(mine - k + size, size)] = piece_ref[...]
        peak = held[0, 0:8]
        for i in range(1, size):
            peak = jnp.maximum(peak, held[i, 0:8])
        mass = target = floor = total = jnp.zeros((8, 128), jnp.float32)
        mass_before = total_before = jnp.zeros((8, 128), jnp.float32)
        if before is not None:
            mass_before = before_ref[0:8] * jnp.exp(piece_refs[0][0:8] - peak)
            total_before = before_ref[8:16]
        for i in range(size):
            scale = jnp.exp(held[i, 0:8] - peak)
            part = held[i, 8:16] * scale
            mass = mass + part
            target = target + held[i, 16:24] * scale
            floor = floor + held[i, 24:32]
            total = total + held[i, 32:40]
            earlier = i < mine
            mass_before = mass_before + jnp.where(earlier, part, 0.0)
            total_before = total_before + jnp.where(earlier, held[i, 32:40], 0.0)
        if last is None:
            stats_ref, after_ref = rest[0], rest[1]
            stats_ref[0:8] = peak
            stats_ref[8:16] = mass
            stats_ref[16:24] = target
            stats_ref[24:32] = floor
            stats_ref[32:40] = total
            after_ref[0:8] = mass_before
            after_ref[8:16] = total_before
        else:
            own_ref, totals_ref, terms_ref, bits_ref = rest[:4]
            tokens = totals_ref[...].astype(jnp.float32)
            free = (tokens - total) / mass
            terms_ref[0:8] = jnp.exp(own_ref[0:8] - peak) * free / tokens
            terms_ref[8:16] = 1.0 / tokens
            terms_ref[16:24] = (total_before + mass_before * free) / tokens
            bits_ref[...] = -jnp.log2((floor + target * free) / tokens)

    inputs = pieces + ([] if before is None else [before]) + ([] if last is None else list(last))
    first, second = ((40, 128), (16, 128)) if last is None else ((24, 128), (8, 128))
    return call(
        body,
        (jax.ShapeDtypeStruct(first, jnp.float32), jax.ShapeDtypeStruct(second, jnp.float32)),
        "join_" + axis,
        inputs,
        vmem_mib=2,
        scratch=[pltpu.VMEM((size, 40, 128), jnp.float32)],
        out_specs=(VMEM, VMEM),
    )


def finish(logits, floors, stats, terms, entries):
    block = 256

    def body(logits_ref, floors_ref, stats_ref, terms_ref, out_ref, carry_ref, floor_carry_ref):
        i = pl.program_id(0)

        @pl.when(i == 0)
        def _():
            carry_ref[...] = jnp.zeros_like(carry_ref)
            floor_carry_ref[...] = jnp.zeros_like(floor_carry_ref)

        rows = pl.ds(pl.multiple_of(i * block, block), block)
        below = lax.broadcasted_iota(jnp.int32, (block, block), 1)
        lower = (below < lax.broadcasted_iota(jnp.int32, (block, block), 0)).astype(jnp.bfloat16)
        floors = floors_ref[rows, :]
        floor_sums = floor_carry_ref[0:1, :] + jnp.dot(
            lower, floors.astype(jnp.bfloat16), preferred_element_type=jnp.float32
        )
        floor_carry_ref[0:1, :] += jnp.sum(floors, axis=0, keepdims=True)
        for j in range(0, ROWS, 2):
            lanes = slice(j * 128, (j + 2) * 128)
            peak, scale, inverse, offset = (
                jnp.concatenate([ref[at + j:at + j + 1, :], ref[at + j + 1:at + j + 2, :]], axis=1)
                for ref, at in ((stats_ref, 0), (terms_ref, 0), (terms_ref, 8), (terms_ref, 16))
            )
            value = jnp.exp(logits_ref[rows, lanes] - peak)
            high = value.astype(jnp.bfloat16)
            low = (value - high.astype(jnp.float32)).astype(jnp.bfloat16)
            sums = jnp.dot(lower, high, preferred_element_type=jnp.float32)
            sums = sums + jnp.dot(lower, low, preferred_element_type=jnp.float32)
            sums = sums + carry_ref[0:1, lanes]
            carry_ref[0:1, lanes] += jnp.sum(value, axis=0, keepdims=True)
            wide = jnp.concatenate([floor_sums, floor_sums], axis=1)
            out_ref[:, lanes] = sums * scale + wide * inverse + offset

    return call(
        body,
        jax.ShapeDtypeStruct((entries, 1024), jnp.float32),
        "finish",
        (logits, floors, stats, terms),
        vmem_mib=8,
        grid=(-(-entries // block),),
        scratch=[pltpu.VMEM((8, 1024), jnp.float32), pltpu.VMEM((8, 128), jnp.float32)],
        out_specs=pl.BlockSpec((block, 1024), lambda i: (i, 0)),
    )


def own_coordinate(axes):
    core = lax.rem(lax.axis_index(TENSOR), 2)
    return jnp.where(core == 0, coordinate(axes[0]), coordinate(axes[1]))


def square_sums(pieces):
    def body(*refs):
        mine = coordinate("y")
        total = jnp.zeros((64, 1), jnp.float32)
        for i, k in enumerate((0, 1, 3, 2)):
            piece = refs[i][...]
            place = lax.rem(mine - k + 4, 4)
            refs[4][:, pl.ds(pl.multiple_of(place * 1024, 1024), 1024)] = piece
            widened = piece.astype(jnp.float32)
            total = total + jnp.sum(widened * widened, axis=1, keepdims=True)
        refs[5][...] = jnp.broadcast_to(total, (64, 128))

    return call(
        body,
        (jax.ShapeDtypeStruct((64, 4096), jnp.bfloat16), jax.ShapeDtypeStruct((64, 128), jnp.float32)),
        "square_sums",
        pieces,
        vmem_mib=4,
        out_specs=(VMEM, VMEM),
    )


def normalize(features, own, other, gain):
    def body(features_ref, own_ref, other_ref, gain_ref, upper_ref, lower_ref):
        core = lax.rem(lax.axis_index(TENSOR), 2)
        mean_square = (own_ref[:, 0:1] + other_ref[:, 0:1]) * (1.0 / 8192)
        scale = lax.rsqrt(mean_square + epsilon)
        for y in range(4):
            lanes = slice(y * 1024, (y + 1) * 1024)
            row = gain_ref[:, pl.ds(pl.multiple_of((y * 2 + core) * 1024, 1024), 1024)]
            value = (features_ref[:, lanes].astype(jnp.float32) * scale * row).astype(jnp.bfloat16)
            upper_ref[:, lanes] = value[:32]
            lower_ref[:, lanes] = value[32:]

    shape = jax.ShapeDtypeStruct((32, 4096), jnp.bfloat16)
    return call(
        body,
        (shape, shape),
        "normalize",
        (features, own, other, gain),
        vmem_mib=4,
        out_specs=(VMEM, VMEM),
    )


def stack(pieces, axes):
    rows = 2 * pieces[0][2].shape[0]
    half = rows // 2

    def body(*refs):
        mine = own_coordinate(axes)
        for (side, hops, _), ref in zip(pieces, refs):
            place = lax.rem(mine + (4 - hops), 4)
            for i, out_ref in enumerate(refs[-2:]):

                @pl.when(place // 2 == i)
                def _():
                    at = pl.multiple_of((place - 2 * i) * rows + side * half, half)
                    out_ref[pl.ds(at, half), :] = ref[...]

    shape = jax.ShapeDtypeStruct((2 * rows, 4096), jnp.bfloat16)
    return call(
        body,
        (shape, shape),
        "stack",
        [piece[2] for piece in pieces],
        vmem_mib=4,
        out_specs=(VMEM, VMEM),
    )


def multiply(weight, products, pieces, side, axes):
    entries = weight.shape[0]
    arrays = [pieces[0][0]] if pieces[0][0] is pieces[1][0] else [piece[0] for piece in pieces]
    inputs = [weight] + ([] if products is None else [products]) + arrays

    def body(*refs):
        weight_ref, out_ref = refs[0], refs[-1]
        token_refs = refs[len(inputs) - len(arrays):len(inputs)]
        core = lax.rem(lax.axis_index(TENSOR), 2)
        features = core if side == 0 else 1 - core
        mine = coordinate_of(features, axes)
        total = None
        for y in range(4):
            far = pl.ds(pl.multiple_of((y * 2 + features) * 1024, 1024), 1024)
            value = [ref[:, y * 1024:(y + 1) * 1024] for ref in token_refs]
            value = value[0] if len(value) == 1 else jnp.concatenate(value, axis=0)
            product = lax.dot_general(
                weight_ref[:, far], value, (((1,), (1,)), ((), ())), preferred_element_type=jnp.float32
            )
            total = product if total is None else total + product
        for i, (_, hops, half) in enumerate(pieces):
            place = lax.rem(mine + (4 - hops), 4)
            out_ref[side, place, :, half * 128:half * 128 + 128] = total[:, i * 128:i * 128 + 128]

    return call(
        body,
        jax.ShapeDtypeStruct((2, 4, entries, 256), jnp.float32),
        "multiply",
        inputs,
        vmem_mib=6,
        input_output_aliases={} if products is None else {1: 0},
        cost_estimate=pl.CostEstimate(flops=2 * entries * 4096 * 256, bytes_accessed=4 << 20, transcendentals=0),
    )


def coordinate_of(core, axes):
    return jnp.where(core == 0, coordinate(axes[0]), coordinate(axes[1]))


def local(hidden, norm_gain, head_weight, floor_counts, totals, targets):
    weight = head_weight.T
    entries = weight.shape[0]
    targets = targets.reshape(8, 128)

    beside = [shift(hidden, "y", k) for k in (1, 3, 2)]
    floors, gain, floor_stats = prepare(floor_counts.reshape(1, entries), norm_gain, targets)
    raw, own = square_sums([hidden] + beside)
    upper, lower = normalize(raw, own, shift(own, "c", 1), gain)
    axes = "xz"
    upper_1, lower_3 = shift(upper, axes, 1), shift(lower, axes, 3)
    upper_3, lower_1 = shift(upper, axes, 3), shift(lower, axes, 1)
    upper_2, lower_2 = shift(upper_1, axes, 1), shift(lower_3, axes, 3)
    pieces = [(0, 0, upper), (1, 0, lower), (0, 1, upper_1), (1, 3, lower_3)]
    pieces += [(0, 3, upper_3), (1, 1, lower_1), (0, 2, upper_2), (1, 2, lower_2)]
    block = stack(pieces, axes)

    axes = "zx"
    swap = lambda value: shift(value, "c", 1)
    up = lambda value: shift(value, axes, 1)
    down = lambda value: shift(value, axes, 3)
    upper, lower = block
    upper_1, lower_3 = up(upper), down(lower)
    swapped = swap(upper), swap(lower)
    products = multiply(weight, None, [(upper, 0, 0), (lower, 0, 1)], 0, axes)
    upper, lower, products = lax.optimization_barrier((upper, lower, products))
    upper_3, lower_1 = down(upper), up(lower)
    products = multiply(weight, products, [(swapped[0], 0, 0), (swapped[1], 0, 1)], 1, axes)
    upper_1, lower_3, products = lax.optimization_barrier((upper_1, lower_3, products))
    upper_2, lower_2 = up(upper_1), down(lower_3)
    swapped = swap(upper_1), swap(lower_3)
    products = multiply(weight, products, [(upper_1, 1, 0), (lower_3, 3, 1)], 0, axes)
    products = multiply(weight, products, [(swapped[0], 1, 0), (swapped[1], 3, 1)], 1, axes)
    upper_3, lower_1, products = lax.optimization_barrier((upper_3, lower_1, products))
    swapped = swap(upper_3), swap(lower_1)
    products = multiply(weight, products, [(upper_3, 3, 0), (lower_1, 1, 1)], 0, axes)
    products = multiply(weight, products, [(swapped[0], 3, 0), (swapped[1], 1, 1)], 1, axes)
    upper_2, lower_2, products = lax.optimization_barrier((upper_2, lower_2, products))
    swapped = swap(upper_2), swap(lower_2)
    products = multiply(weight, products, [(upper_2, 2, 0), (lower_2, 2, 1)], 0, axes)
    products = multiply(weight, products, [(swapped[0], 2, 0), (swapped[1], 2, 1)], 1, axes)

    logits, stats = join_halves(products, floor_stats, targets)
    group, before = stats, None
    for axis in ("c", "y", "z"):
        group, before = join(axis, group, before)
    terms, bits = join("x", group, before, last=(stats, totals.reshape(8, 128)))
    cumulative = finish(logits, floors, stats, terms, entries)
    return cumulative.T, bits.reshape(1024)


def solution(mesh):
    in_specs = (P(STREAM, TENSOR), P(), P(None, BOTH), P(BOTH), P(), P())
    out_specs = (P(None, BOTH), P())
    return jax.shard_map(local, mesh=mesh, in_specs=in_specs, out_specs=out_specs, check_vma=False)
```

time: 210 us -> 124 us (0.59)
  waiting for transfers between devices: 145 us -> 47.6 us
  matrix products: 21.7 us -> 0 us
  starting transfers between devices: 15.6 us -> 36.9 us
  Pallas kernels: 8.67 us -> 26.7 us
  between operations: 14.2 us -> 0.88 us
  local copies, waits for them, and re-layouts: 0.21 us -> 12 us
  other arithmetic: 4.77 us -> 0 us
    all_gather x2 -> x0, waiting for transfers between devices: 138 us -> none  [the longest x1 111 us: local(): everyone = lax.all_gather(normed, STREAM, axis=0, tiled=True)]
    ppermute x10 -> x34, waiting for transfers between devices: 5.95 us -> 47.6 us  [shift(): return lax.ppermute(value, BOTH, pairs)]
    pallas_call x5 -> x18, Pallas kernels: 3.39 us -> 26.7 us  [call(): pl.pallas_call(body, out_shape=out_shape, in_specs=[VMEM] * len(inputs),...]
    dot_general x1 -> x0, matrix products: 21.7 us -> none  [local(): lax.dot_general(head_weight, everyone, (((0,), (1,)), ((), ())), preferre...]
    ppermute x10 -> x34, starting transfers between devices: 15.5 us -> 36.9 us  [shift(): return lax.ppermute(value, BOTH, pairs)]
    unnamed x6 -> x16, local copies, waits for them, and re-layouts: 0.02 us -> 12 us
    pallas_call x2 -> x0, Pallas kernels: 5.28 us -> none  [the longest x1 3.07 us: finish(): pl.pallas_call(body, grid=(-(-entries // block),), out_shape=jax.ShapeDty...]
    convert_element_type x3 -> x0, other arithmetic: 3.24 us -> none  [the longest x1 2.51 us: normalize(): return (widened * lax.rsqrt(mean_square + epsilon) * norm_gain.astype(jnp...]
  transfers between devices with their start and end apart: 12 -> 34, of which waited for: 7 -> 18; matrix products, arithmetic and copies ran while one was open for 0% -> 0% of each run, Pallas kernels for 1% -> 14%
where the time goes in v2:
time: 124 us
  waiting for transfers between devices  47.6 us (38%)
  starting transfers between devices  36.9 us (30%)
  Pallas kernels  26.7 us (22%)
  local copies, waits for them, and re-layouts  12 us (10%)
    ppermute x34, waiting for transfers between devices, shift(): return lax.ppermute(value, BOTH, pairs)  47.6 us
    ppermute x34, starting transfers between devices, shift(): return lax.ppermute(value, BOTH, pairs)  36.9 us
    pallas_call x18, Pallas kernels, call(): pl.pallas_call(body, out_shape=out_shape, in_specs=[VMEM] * len(inputs),...  26.7 us
    unnamed x16, local copies, waits for them, and re-layouts  12 us
  transfers between devices with their start and end apart: 34, of which 18 were waited for; matrix products, arithmetic and copies ran while one was open for 0% of the time, Pallas kernels for 14%

profile of v2, /device:TPU:0, one launch (start us, length us, event | category | flops | bytes accessed | tf_op | source)
XLA Modules:
  0.0 124.2 jit_solution(11125877989487120000)
XLA Ops:
  0.6 3.2 %collective-permute-start.1 = (bf16[64,1024]{1,0:T(8,128)(2,1)}, bf16[64,1024]{1,0:T(8,128)(2,1)S(1)}, u32[]{:S(2)}, u32[]{:S(2)}) collective-permute-start(bf16[64,1024]{1,0:T(8,128)(2,1)} %refs_0_.1), channel_id=1, source_target_pairs={{0,6},{1,7},{2,0},{3,1},{4,2},{5,3},{6,4},{7,5},{8,14},{9,15},{10,... | collective-permute-start | bytes 393224 | tf_op jit(solution)/shard_map/ppermute | solution.py:29
  6.9 6.1 %collective-permute-done.refs_1_ = bf16[64,1024]{1,0:T(8,128)(2,1)S(1)} collective-permute-done((bf16[64,1024]{1,0:T(8,128)(2,1)}, bf16[64,1024]{1,0:T(8,128)(2,1)S(1)}, u32[]{:S(2)}, u32[]{:S(2)}) %collective-permute-start) | collective-permute-done | bytes 131104 | tf_op jit(solution)/shard_map/ppermute | solution.py:29
  22.5 2.3 %collective-permute-done.4.refs_2_ = bf16[32,4096]{1,0:T(8,128)(2,1)S(1)} collective-permute-done((bf16[32,4096]{1,0:T(8,128)(2,1)S(1)}, bf16[32,4096]{1,0:T(8,128)(2,1)S(1)}, u32[]{:S(2)}, u32[]{:S(2)}) %collective-permute-start.4) | collective-permute-done | bytes 262176 | tf_op jit(solution)/shard_map/ppermute | solution.py:29
  25.1 3.0 %collective-permute-start.9 = (bf16[32,4096]{1,0:T(8,128)(2,1)S(1)}, bf16[32,4096]{1,0:T(8,128)(2,1)S(1)}, u32[]{:S(2)}, u32[]{:S(2)}) collective-permute-start(bf16[32,4096]{1,0:T(8,128)(2,1)S(1)} %collective-permute-done.5.refs_3_), channel_id=1, source_target_pairs={{0,96},{1,25},{2,98},{3,27},{4,100},{5,29},{6,102},{7,31},{8,104},... | collective-permute-start | bytes 786440 | tf_op jit(solution)/shard_map/ppermute | solution.py:29
  29.6 2.8 %collective-permute-done.8.refs_6_ = bf16[32,4096]{1,0:T(8,128)(2,1)S(1)} collective-permute-done((bf16[32,4096]{1,0:T(8,128)(2,1)S(1)}, bf16[32,4096]{1,0:T(8,128)(2,1)S(1)}, u32[]{:S(2)}, u32[]{:S(2)}) %collective-permute-start.8) | collective-permute-done | bytes 262176 | tf_op jit(solution)/shard_map/ppermute | solution.py:29
  37.2 5.7 %copy-done = bf16[8192,1002]{0,1:T(8,128)(2,1)S(1)} copy-done((bf16[8192,1002]{0,1:T(8,128)(2,1)S(1)}, bf16[8192,1002]{0,1:T(8,128)(2,1)}, u32[]{:S(2)}) %copy-start) | copy-done | bytes 16416792
  42.9 2.3 %multiply.8.refs_1_ = f32[2,4,1002,256]{3,2,1,0:T(8,128)S(1)} custom-call(bf16[1002,8192]{1,0:T(8,128)(2,1)S(1)} %bitcast.6, bf16[128,4096]{1,0:T(8,128)(2,1)S(1)} %get-tuple-element.43.refs_1_, bf16[128,4096]{1,0:T(8,128)(2,1)S(1)} %get-tuple-element.44.refs_2_), custom_call_target="tpu_custom_call" | custom-call | flops 2101346304 | bytes 4194304 | tf_op jit(solution)/shard_map/multiply/pallas_call | solution.py:33
  45.3 3.3 %copy-done.1 = bf16[8192,1002]{0,1:T(8,128)(2,1)S(1)} copy-done((bf16[8192,1002]{0,1:T(8,128)(2,1)S(1)}, bf16[8192,1002]{0,1:T(8,128)(2,1)}, u32[]{:S(2)}) %copy-start.1) | copy-done | bytes 16416792
  48.6 2.3 %multiply.9.refs_1_ = f32[2,4,1002,256]{3,2,1,0:T(8,128)S(1)} custom-call(bf16[1002,8192]{1,0:T(8,128)(2,1)S(1)} %bitcast.7, f32[2,4,1002,256]{3,2,1,0:T(8,128)S(1)} %multiply.8.refs_1_, bf16[128,4096]{1,0:T(8,128)(2,1)S(1)} %collective-permute-done.12.refs_2_, bf16[128,4096]{1,0:T(8,128)(2,1)S(1)} %collective-permute-done.13.refs_3_), custom_call_target="tpu_custom_call", output_to_operand_aliasing={{}: (1, {})} | custom-call | flops 2101346304 | bytes 4194304 | tf_op jit(solution)/shard_map/multiply/pallas_call | solution.py:33
  51.6 2.6 %collective-permute-start.16 = (bf16[128,4096]{1,0:T(8,128)(2,1)S(1)}, bf16[128,4096]{1,0:T(8,128)(2,1)S(1)}, u32[]{:S(2)}, u32[]{:S(2)}) collective-permute-start(bf16[128,4096]{1,0:T(8,128)(2,1)S(1)} %get-tuple-element.43.refs_1_), channel_id=1, source_target_pairs={{0,24},{1,97},{2,26},{3,99},{4,28},{5,101},{6,30},{7,103},{8,0},{9... | collective-permute-start | bytes 3145736 | tf_op jit(solution)/shard_map/ppermute | solution.py:29
  54.2 2.3 %multiply.10.refs_1_ = f32[2,4,1002,256]{3,2,1,0:T(8,128)S(1)} custom-call(bf16[1002,8192]{1,0:T(8,128)(2,1)S(1)} %bitcast.8, f32[2,4,1002,256]{3,2,1,0:T(8,128)S(1)} %multiply.9.refs_1_, bf16[128,4096]{1,0:T(8,128)(2,1)S(1)} %collective-permute-done.10.refs_2_, bf16[128,4096]{1,0:T(8,128)(2,1)S(1)} %collective-permute-done.11.refs_3_), custom_call_target="tpu_custom_call", output_to_operand_aliasing={{}: (1, {})} | custom-call | flops 2101346304 | bytes 4194304 | tf_op jit(solution)/shard_map/multiply/pallas_call | solution.py:33
  56.5 2.3 %multiply.11.refs_1_ = f32[2,4,1002,256]{3,2,1,0:T(8,128)S(1)} custom-call(bf16[1002,8192]{1,0:T(8,128)(2,1)S(1)} %bitcast.9, f32[2,4,1002,256]{3,2,1,0:T(8,128)S(1)} %multiply.10.refs_1_, bf16[128,4096]{1,0:T(8,128)(2,1)S(1)} %collective-permute-done.18.refs_2_, bf16[128,4096]{1,0:T(8,128)(2,1)S(1)} %collective-permute-done.19.refs_3_), custom_call_target="tpu_custom_call", output_to_operand_aliasing={{}: (1, {})} | custom-call | flops 2101346304 | bytes 4194304 | tf_op jit(solution)/shard_map/multiply/pallas_call | solution.py:33
  58.9 7.6 %collective-permute-done.16.refs_2_ = bf16[128,4096]{1,0:T(8,128)(2,1)S(1)} collective-permute-done((bf16[128,4096]{1,0:T(8,128)(2,1)S(1)}, bf16[128,4096]{1,0:T(8,128)(2,1)S(1)}, u32[]{:S(2)}, u32[]{:S(2)}) %collective-permute-start.16) | collective-permute-done | bytes 1048608 | tf_op jit(solution)/shard_map/ppermute | solution.py:29
  66.5 3.7 %collective-permute-done.17.refs_3_ = bf16[128,4096]{1,0:T(8,128)(2,1)S(1)} collective-permute-done((bf16[128,4096]{1,0:T(8,128)(2,1)S(1)}, bf16[128,4096]{1,0:T(8,128)(2,1)S(1)}, u32[]{:S(2)}, u32[]{:S(2)}) %collective-permute-start.17) | collective-permute-done | bytes 1048608 | tf_op jit(solution)/shard_map/ppermute | solution.py:29
  70.7 3.2 %collective-permute-start.15 = (bf16[128,4096]{1,0:T(8,128)(2,1)S(1)}, bf16[128,4096]{1,0:T(8,128)(2,1)S(1)}, u32[]{:S(2)}, u32[]{:S(2)}) collective-permute-start(bf16[128,4096]{1,0:T(8,128)(2,1)S(1)} %collective-permute-done.11.refs_3_), channel_id=1, source_target_pairs={{0,24},{1,97},{2,26},{3,99},{4,28},{5,101},{6,30},{7,103},{8,0},{9... | collective-permute-start | bytes 3145736 | tf_op jit(solution)/shard_map/ppermute | solution.py:29
  73.9 2.3 %multiply.12.refs_1_ = f32[2,4,1002,256]{3,2,1,0:T(8,128)S(1)} custom-call(bf16[1002,8192]{1,0:T(8,128)(2,1)S(1)} %bitcast.10, f32[2,4,1002,256]{3,2,1,0:T(8,128)S(1)} %multiply.11.refs_1_, bf16[128,4096]{1,0:T(8,128)(2,1)S(1)} %collective-permute-done.16.refs_2_, bf16[128,4096]{1,0:T(8,128)(2,1)S(1)} %collective-permute-done.17.refs_3_), custom_call_target="tpu_custom_call", output_to_operand_aliasing={{}: (1, {})} | custom-call | flops 2101346304 | bytes 4194304 | tf_op jit(solution)/shard_map/multiply/pallas_call | solution.py:33
  76.3 2.3 %multiply.13.refs_1_ = f32[2,4,1002,256]{3,2,1,0:T(8,128)S(1)} custom-call(bf16[1002,8192]{1,0:T(8,128)(2,1)S(1)} %bitcast.11, f32[2,4,1002,256]{3,2,1,0:T(8,128)S(1)} %multiply.12.refs_1_, bf16[128,4096]{1,0:T(8,128)(2,1)S(1)} %collective-permute-done.20.refs_2_, bf16[128,4096]{1,0:T(8,128)(2,1)S(1)} %collective-permute-done.21.refs_3_), custom_call_target="tpu_custom_call", output_to_operand_aliasing={{}: (1, {})} | custom-call | flops 2101346304 | bytes 4194304 | tf_op jit(solution)/shard_map/multiply/pallas_call | solution.py:33
  78.6 8.1 %collective-permute-done.14.refs_2_ = bf16[128,4096]{1,0:T(8,128)(2,1)S(1)} collective-permute-done((bf16[128,4096]{1,0:T(8,128)(2,1)S(1)}, bf16[128,4096]{1,0:T(8,128)(2,1)S(1)}, u32[]{:S(2)}, u32[]{:S(2)}) %collective-permute-start.14) | collective-permute-done | bytes 1048608 | tf_op jit(solution)/shard_map/ppermute | solution.py:29
  87.2 2.3 %multiply.14.refs_1_ = f32[2,4,1002,256]{3,2,1,0:T(8,128)S(1)} custom-call(bf16[1002,8192]{1,0:T(8,128)(2,1)S(1)} %bitcast.12, f32[2,4,1002,256]{3,2,1,0:T(8,128)S(1)} %multiply.13.refs_1_, bf16[128,4096]{1,0:T(8,128)(2,1)S(1)} %collective-permute-done.14.refs_2_, bf16[128,4096]{1,0:T(8,128)(2,1)S(1)} %collective-permute-done.15.refs_3_), custom_call_target="tpu_custom_call", output_to_operand_aliasing={{}: (1, {})} | custom-call | flops 2101346304 | bytes 4194304 | tf_op jit(solution)/shard_map/multiply/pallas_call | solution.py:33
  90.9 2.3 %multiply.15.products_ref = f32[2,4,1002,256]{3,2,1,0:T(8,128)S(1)} custom-call(bf16[1002,8192]{1,0:T(8,128)(2,1)S(1)} %bitcast.13, f32[2,4,1002,256]{3,2,1,0:T(8,128)S(1)} %multiply.14.refs_1_, bf16[128,4096]{1,0:T(8,128)(2,1)S(1)} %collective-permute-done.22.refs_2_, ...), custom_call_target="tpu_custom_call", output_to_operand_aliasing={{}: (1, {})} | custom-call | flops 2101346304 | bytes 4194304 | tf_op jit(solution)/shard_map/multiply/pallas_call | solution.py:33
  93.2 2.4 %join_halves.1 = (f32[1024,1024]{1,0:T(8,128)S(1)}, f32[40,128]{1,0:T(8,128)S(1)}) custom-call(f32[2,4,1002,256]{3,2,1,0:T(8,128)S(1)} %multiply.15.products_ref, f32[16,128]{1,0:T(8,128)S(1)} %get-tuple-element.52.floors_ref, s32[8,128]{1,0:T(8,128)S(1)} %bitcast.15), custom_call_target="tpu_custom_call" | custom-call | tf_op jit(solution)/shard_map/join_halves/pallas_call | solution.py:33
  99.7 2.6 %collective-permute-done.27.refs_3_ = f32[40,128]{1,0:T(8,128)S(1)} collective-permute-done((f32[40,128]{1,0:T(8,128)S(1)}, f32[40,128]{1,0:T(8,128)S(1)}, u32[]{:S(2)}, u32[]{:S(2)}) %collective-permute-start.27) | collective-permute-done | bytes 20512 | tf_op jit(solution)/shard_map/ppermute | solution.py:29
  117.5 2.2 %collective-permute-done.31.refs_1_ = f32[40,128]{1,0:T(8,128)S(1)} collective-permute-done((f32[40,128]{1,0:T(8,128)S(1)}, f32[40,128]{1,0:T(8,128)S(1)}, u32[]{:S(2)}, u32[]{:S(2)}) %collective-permute-start.31) | collective-permute-done | bytes 20512 | tf_op jit(solution)/shard_map/ppermute | solution.py:29
  120.4 3.8 %finish.1 = f32[1002,1024]{1,0:T(8,128)} custom-call(f32[1024,1024]{1,0:T(8,128)S(1)} %get-tuple-element.53.logits_ref, f32[1024,128]{1,0:T(8,128)S(1)} %get-tuple-element.54.floors_ref, f32[40,128]{1,0:T(8,128)S(1)} %get-tuple-element.55.refs_0_.refs_5_.stats_ref, f32[24,128]{1,0:T(8,128)S(1)} %get-tuple-element.62.terms_ref), custom_call_target="tpu_custom_call" | custom-call | tf_op jit(solution)/shard_map/finish/pallas_call | solution.py:33
  (78 shorter events, 42.0 us)
Async XLA Ops:
  0.6 6.2 %collective-permute-start.1 = (bf16[64,1024]{1,0:T(8,128)(2,1)}, bf16[64,1024]{1,0:T(8,128)(2,1)S(1)}, u32[]{:S(2)}, u32[]{:S(2)}) collective-permute-start(bf16[64,1024]{1,0:T(8,128)(2,1)} %refs_0_.1), channel_id=1, source_target_pairs={{0,6},{1,7},{2,0},{3,1},{4,2},{5,3},{6,4},{7,5},{8,14},{9,15},{10,... | collective-permute-start | bytes 393224 | tf_op jit(solution)/shard_map/ppermute | solution.py:29
  3.8 9.2 %collective-permute-start = (bf16[64,1024]{1,0:T(8,128)(2,1)}, bf16[64,1024]{1,0:T(8,128)(2,1)S(1)}, u32[]{:S(2)}, u32[]{:S(2)}) collective-permute-start(bf16[64,1024]{1,0:T(8,128)(2,1)} %refs_0_.1), channel_id=1, source_target_pairs={{0,2},{1,3},{2,4},{3,5},{4,6},{5,7},{6,0},{7,1},{8,10},{9,11},{10,... | collective-permute-start | bytes 393224 | tf_op jit(solution)/shard_map/ppermute | solution.py:29
  3.8 9.2 %collective-permute-start.2 = (bf16[64,1024]{1,0:T(8,128)(2,1)}, bf16[64,1024]{1,0:T(8,128)(2,1)S(1)}, u32[]{:S(2)}, u32[]{:S(2)}) collective-permute-start(bf16[64,1024]{1,0:T(8,128)(2,1)} %refs_0_.1), channel_id=1, source_target_pairs={{0,4},{1,5},{2,6},{3,7},{4,0},{5,1},{6,2},{7,3},{8,12},{9,13},{10,... | collective-permute-start | bytes 393224 | tf_op jit(solution)/shard_map/ppermute | solution.py:29
  17.1 7.7 %collective-permute-start.4 = (bf16[32,4096]{1,0:T(8,128)(2,1)S(1)}, bf16[32,4096]{1,0:T(8,128)(2,1)S(1)}, u32[]{:S(2)}, u32[]{:S(2)}) collective-permute-start(bf16[32,4096]{1,0:T(8,128)(2,1)S(1)} %get-tuple-element.36.refs_0_), channel_id=1, source_target_pairs={{0,32},{1,9},{2,34},{3,11},{4,36},{5,13},{6,38},{7,15},{8,40},{9,1... | collective-permute-start | bytes 786440 | tf_op jit(solution)/shard_map/ppermute | solution.py:29
  18.7 6.4 %collective-permute-start.5 = (bf16[32,4096]{1,0:T(8,128)(2,1)S(1)}, bf16[32,4096]{1,0:T(8,128)(2,1)S(1)}, u32[]{:S(2)}, u32[]{:S(2)}) collective-permute-start(bf16[32,4096]{1,0:T(8,128)(2,1)S(1)} %get-tuple-element.37.refs_1_), channel_id=1, source_target_pairs={{0,96},{1,25},{2,98},{3,27},{4,100},{5,29},{6,102},{7,31},{8,104},... | collective-permute-start | bytes 786440 | tf_op jit(solution)/shard_map/ppermute | solution.py:29
  20.4 7.6 %collective-permute-start.6 = (bf16[32,4096]{1,0:T(8,128)(2,1)S(1)}, bf16[32,4096]{1,0:T(8,128)(2,1)S(1)}, u32[]{:S(2)}, u32[]{:S(2)}) collective-permute-start(bf16[32,4096]{1,0:T(8,128)(2,1)S(1)} %get-tuple-element.36.refs_0_), channel_id=1, source_target_pairs={{0,96},{1,25},{2,98},{3,27},{4,100},{5,29},{6,102},{7,31},{8,104},... | collective-permute-start | bytes 786440 | tf_op jit(solution)/shard_map/ppermute | solution.py:29
  22.0 7.6 %collective-permute-start.7 = (bf16[32,4096]{1,0:T(8,128)(2,1)S(1)}, bf16[32,4096]{1,0:T(8,128)(2,1)S(1)}, u32[]{:S(2)}, u32[]{:S(2)}) collective-permute-start(bf16[32,4096]{1,0:T(8,128)(2,1)S(1)} %get-tuple-element.37.refs_1_), channel_id=1, source_target_pairs={{0,32},{1,9},{2,34},{3,11},{4,36},{5,13},{6,38},{7,15},{8,40},{9,1... | collective-permute-start | bytes 786440 | tf_op jit(solution)/shard_map/ppermute | solution.py:29
  24.8 7.6 %collective-permute-start.8 = (bf16[32,4096]{1,0:T(8,128)(2,1)S(1)}, bf16[32,4096]{1,0:T(8,128)(2,1)S(1)}, u32[]{:S(2)}, u32[]{:S(2)}) collective-permute-start(bf16[32,4096]{1,0:T(8,128)(2,1)S(1)} %collective-permute-done.4.refs_2_), channel_id=1, source_target_pairs={{0,32},{1,9},{2,34},{3,11},{4,36},{5,13},{6,38},{7,15},{8,40},{9,1... | collective-permute-start | bytes 786440 | tf_op jit(solution)/shard_map/ppermute | solution.py:29
  25.1 7.3 %collective-permute-start.9 = (bf16[32,4096]{1,0:T(8,128)(2,1)S(1)}, bf16[32,4096]{1,0:T(8,128)(2,1)S(1)}, u32[]{:S(2)}, u32[]{:S(2)}) collective-permute-start(bf16[32,4096]{1,0:T(8,128)(2,1)S(1)} %collective-permute-done.5.refs_3_), channel_id=1, source_target_pairs={{0,96},{1,25},{2,98},{3,27},{4,100},{5,29},{6,102},{7,31},{8,104},... | collective-permute-start | bytes 786440 | tf_op jit(solution)/shard_map/ppermute | solution.py:29
  32.6 12.7 %collective-permute-start.12 = (bf16[128,4096]{1,0:T(8,128)(2,1)S(1)}, bf16[128,4096]{1,0:T(8,128)(2,1)S(1)}, u32[]{:S(2)}, u32[]{:S(2)}) collective-permute-start(bf16[128,4096]{1,0:T(8,128)(2,1)S(1)} %get-tuple-element.43.refs_1_), channel_id=1, source_target_pairs={{0,1},{1,0},{2,3},{3,2},{4,5},{5,4},{6,7},{7,6},{8,9},{9,8},{10,11... | collective-permute-start | bytes 3145736 | tf_op jit(solution)/shard_map/ppermute | solution.py:29
  32.8 12.5 %collective-permute-start.13 = (bf16[128,4096]{1,0:T(8,128)(2,1)S(1)}, bf16[128,4096]{1,0:T(8,128)(2,1)S(1)}, u32[]{:S(2)}, u32[]{:S(2)}) collective-permute-start(bf16[128,4096]{1,0:T(8,128)(2,1)S(1)} %get-tuple-element.44.refs_2_), channel_id=1, source_target_pairs={{0,1},{1,0},{2,3},{3,2},{4,5},{5,4},{6,7},{7,6},{8,9},{9,8},{10,11... | collective-permute-start | bytes 3145736 | tf_op jit(solution)/shard_map/ppermute | solution.py:29
  33.2 17.8 %collective-permute-start.10 = (bf16[128,4096]{1,0:T(8,128)(2,1)S(1)}, bf16[128,4096]{1,0:T(8,128)(2,1)S(1)}, u32[]{:S(2)}, u32[]{:S(2)}) collective-permute-start(bf16[128,4096]{1,0:T(8,128)(2,1)S(1)} %get-tuple-element.43.refs_1_), channel_id=1, source_target_pairs={{0,8},{1,33},{2,10},{3,35},{4,12},{5,37},{6,14},{7,39},{8,16},{9,4... | collective-permute-start | bytes 3145736 | tf_op jit(solution)/shard_map/ppermute | solution.py:29
  35.1 15.9 %collective-permute-start.11 = (bf16[128,4096]{1,0:T(8,128)(2,1)S(1)}, bf16[128,4096]{1,0:T(8,128)(2,1)S(1)}, u32[]{:S(2)}, u32[]{:S(2)}) collective-permute-start(bf16[128,4096]{1,0:T(8,128)(2,1)S(1)} %get-tuple-element.44.refs_2_), channel_id=1, source_target_pairs={{0,24},{1,97},{2,26},{3,99},{4,28},{5,101},{6,30},{7,103},{8,0},{9... | collective-permute-start | bytes 3145736 | tf_op jit(solution)/shard_map/ppermute | solution.py:29
  51.0 5.5 %collective-permute-start.18 = (bf16[128,4096]{1,0:T(8,128)(2,1)S(1)}, bf16[128,4096]{1,0:T(8,128)(2,1)S(1)}, u32[]{:S(2)}, u32[]{:S(2)}) collective-permute-start(bf16[128,4096]{1,0:T(8,128)(2,1)S(1)} %collective-permute-done.10.refs_2_), channel_id=1, source_target_pairs={{0,1},{1,0},{2,3},{3,2},{4,5},{5,4},{6,7},{7,6},{8,9},{9,8},{10,11... | collective-permute-start | bytes 3145736 | tf_op jit(solution)/shard_map/ppermute | solution.py:29
  51.1 5.5 %collective-permute-start.19 = (bf16[128,4096]{1,0:T(8,128)(2,1)S(1)}, bf16[128,4096]{1,0:T(8,128)(2,1)S(1)}, u32[]{:S(2)}, u32[]{:S(2)}) collective-permute-start(bf16[128,4096]{1,0:T(8,128)(2,1)S(1)} %collective-permute-done.11.refs_3_), channel_id=1, source_target_pairs={{0,1},{1,0},{2,3},{3,2},{4,5},{5,4},{6,7},{7,6},{8,9},{9,8},{10,11... | collective-permute-start | bytes 3145736 | tf_op jit(solution)/shard_map/ppermute | solution.py:29
  51.6 14.9 %collective-permute-start.16 = (bf16[128,4096]{1,0:T(8,128)(2,1)S(1)}, bf16[128,4096]{1,0:T(8,128)(2,1)S(1)}, u32[]{:S(2)}, u32[]{:S(2)}) collective-permute-start(bf16[128,4096]{1,0:T(8,128)(2,1)S(1)} %get-tuple-element.43.refs_1_), channel_id=1, source_target_pairs={{0,24},{1,97},{2,26},{3,99},{4,28},{5,101},{6,30},{7,103},{8,0},{9... | collective-permute-start | bytes 3145736 | tf_op jit(solution)/shard_map/ppermute | solution.py:29
  54.2 16.0 %collective-permute-start.17 = (bf16[128,4096]{1,0:T(8,128)(2,1)S(1)}, bf16[128,4096]{1,0:T(8,128)(2,1)S(1)}, u32[]{:S(2)}, u32[]{:S(2)}) collective-permute-start(bf16[128,4096]{1,0:T(8,128)(2,1)S(1)} %get-tuple-element.44.refs_2_), channel_id=1, source_target_pairs={{0,8},{1,33},{2,10},{3,35},{4,12},{5,37},{6,14},{7,39},{8,16},{9,4... | collective-permute-start | bytes 3145736 | tf_op jit(solution)/shard_map/ppermute | solution.py:29
  70.2 6.1 %collective-permute-start.20 = (bf16[128,4096]{1,0:T(8,128)(2,1)S(1)}, bf16[128,4096]{1,0:T(8,128)(2,1)S(1)}, u32[]{:S(2)}, u32[]{:S(2)}) collective-permute-start(bf16[128,4096]{1,0:T(8,128)(2,1)S(1)} %collective-permute-done.16.refs_2_), channel_id=1, source_target_pairs={{0,1},{1,0},{2,3},{3,2},{4,5},{5,4},{6,7},{7,6},{8,9},{9,8},{10,11... | collective-permute-start | bytes 3145736 | tf_op jit(solution)/shard_map/ppermute | solution.py:29
  70.2 6.1 %collective-permute-start.21 = (bf16[128,4096]{1,0:T(8,128)(2,1)S(1)}, bf16[128,4096]{1,0:T(8,128)(2,1)S(1)}, u32[]{:S(2)}, u32[]{:S(2)}) collective-permute-start(bf16[128,4096]{1,0:T(8,128)(2,1)S(1)} %collective-permute-done.17.refs_3_), channel_id=1, source_target_pairs={{0,1},{1,0},{2,3},{3,2},{4,5},{5,4},{6,7},{7,6},{8,9},{9,8},{10,11... | collective-permute-start | bytes 3145736 | tf_op jit(solution)/shard_map/ppermute | solution.py:29
  70.7 16.0 %collective-permute-start.14 = (bf16[128,4096]{1,0:T(8,128)(2,1)S(1)}, bf16[128,4096]{1,0:T(8,128)(2,1)S(1)}, u32[]{:S(2)}, u32[]{:S(2)}) collective-permute-start(bf16[128,4096]{1,0:T(8,128)(2,1)S(1)} %collective-permute-done.10.refs_2_), channel_id=1, source_target_pairs={{0,8},{1,33},{2,10},{3,35},{4,12},{5,37},{6,14},{7,39},{8,16},{9,4... | collective-permute-start | bytes 3145736 | tf_op jit(solution)/shard_map/ppermute | solution.py:29
  70.7 16.0 %collective-permute-start.15 = (bf16[128,4096]{1,0:T(8,128)(2,1)S(1)}, bf16[128,4096]{1,0:T(8,128)(2,1)S(1)}, u32[]{:S(2)}, u32[]{:S(2)}) collective-permute-start(bf16[128,4096]{1,0:T(8,128)(2,1)S(1)} %collective-permute-done.11.refs_3_), channel_id=1, source_target_pairs={{0,24},{1,97},{2,26},{3,99},{4,28},{5,101},{6,30},{7,103},{8,0},{9... | collective-permute-start | bytes 3145736 | tf_op jit(solution)/shard_map/ppermute | solution.py:29
  96.9 5.4 %collective-permute-start.27 = (f32[40,128]{1,0:T(8,128)S(1)}, f32[40,128]{1,0:T(8,128)S(1)}, u32[]{:S(2)}, u32[]{:S(2)}) collective-permute-start(f32[40,128]{1,0:T(8,128)S(1)} %get-tuple-element.56.refs_0_), channel_id=1, source_target_pairs={{0,4},{1,5},{2,6},{3,7},{4,0},{5,1},{6,2},{7,3},{8,12},{9,13},{10,... | collective-permute-start | bytes 61448 | tf_op jit(solution)/shard_map/ppermute | solution.py:29
  103.4 5.5 %collective-permute-start.30 = (f32[40,128]{1,0:T(8,128)S(1)}, f32[40,128]{1,0:T(8,128)S(1)}, u32[]{:S(2)}, u32[]{:S(2)}) collective-permute-start(f32[40,128]{1,0:T(8,128)S(1)} %get-tuple-element.58.refs_0_), channel_id=1, source_target_pairs={{0,16},{1,17},{2,18},{3,19},{4,20},{5,21},{6,22},{7,23},{8,24},{9,... | collective-permute-start | bytes 61448 | tf_op jit(solution)/shard_map/ppermute | solution.py:29
  111.8 5.4 %collective-permute-start.33 = (f32[40,128]{1,0:T(8,128)S(1)}, f32[40,128]{1,0:T(8,128)S(1)}, u32[]{:S(2)}, u32[]{:S(2)}) collective-permute-start(f32[40,128]{1,0:T(8,128)S(1)} %get-tuple-element.60.refs_0_), channel_id=1, source_target_pairs={{0,64},{1,65},{2,66},{3,67},{4,68},{5,69},{6,70},{7,71},{8,72},{9,... | collective-permute-start | bytes 61448 | tf_op jit(solution)/shard_map/ppermute | solution.py:29
  (18 other events, 84.1 us)

commit v3 on v2

--- a/solution.py
+++ b/solution.py
@@ -42,10 +42,26 @@
     )(*inputs)
 
 
-def prepare(floor_counts, gain, targets):
-    entries = floor_counts.shape[1]
-
-    def body(floors_ref, gain_ref, targets_ref, columns_ref, gain_out_ref, stats_ref, row):
+def prepare(weight, hidden, floor_counts, gain, targets):
+    entries = weight.shape[0]
+
+    def body(weight_hbm, hidden_hbm, floors_hbm, gain_hbm, targets_hbm,
+             weight_ref, hidden_ref, columns_ref, gain_out_ref, stats_ref,
+             row, floors_ref, gain_ref, targets_ref, sems):
+        copies = [
+            pltpu.make_async_copy(source, target, sems.at[i])
+            for i, (source, target) in enumerate((
+                (floors_hbm, floors_ref),
+                (targets_hbm, targets_ref),
+                (gain_hbm, gain_ref),
+                (hidden_hbm, hidden_ref),
+                (weight_hbm, weight_ref),
+            ))
+        ]
+        for copy in copies:
+            copy.start()
+        for copy in copies[:3]:
+            copy.wait()
         row[...] = jnp.zeros_like(row)
         row[:, 0:entries] = jnp.broadcast_to(floors_ref[...].astype(jnp.float32), (8, entries))
         total = jnp.zeros((1, 128), jnp.float32)
@@ -61,20 +77,32 @@
         stats_ref[0:8] = jnp.concatenate(picked, axis=0)
         stats_ref[8:16] = jnp.broadcast_to(total, (8, 128))
         gain_out_ref[...] = gain_ref[...].astype(jnp.float32).reshape(1, 8192)
-
-    return call(
-        body,
-        (
-            jax.ShapeDtypeStruct((1024, 128), jnp.float32),
-            jax.ShapeDtypeStruct((1, 8192), jnp.float32),
-            jax.ShapeDtypeStruct((16, 128), jnp.float32),
+        for copy in copies[3:]:
+            copy.wait()
+
+    anywhere = pl.BlockSpec(memory_space=pltpu.HBM)
+    operands = (weight, hidden, floor_counts, gain, targets)
+    return pl.pallas_call(
+        body,
+        out_shape=(
+            pltpu.VMEM(weight.shape, jnp.bfloat16),
+            pltpu.VMEM(hidden.shape, jnp.bfloat16),
+            pltpu.VMEM((1024, 128), jnp.float32),
+            pltpu.VMEM((1, 8192), jnp.float32),
+            pltpu.VMEM((16, 128), jnp.float32),
         ),
-        "prepare",
-        (floor_counts, gain, targets),
-        vmem_mib=4,
-        scratch=[pltpu.VMEM((8, 1024), jnp.float32)],
-        out_specs=(VMEM, VMEM, VMEM),
-    )
+        in_specs=[anywhere] * 5,
+        out_specs=(VMEM,) * 5,
+        scratch_shapes=[
+            pltpu.VMEM((8, 1024), jnp.float32),
+            pltpu.VMEM((1, entries), jnp.int32),
+            pltpu.VMEM((8192,), jnp.bfloat16),
+            pltpu.VMEM((8, 128), jnp.int32),
+            pltpu.SemaphoreType.DMA((5,)),
+        ],
+        compiler_params=pltpu.CompilerParams(vmem_limit_bytes=2 << 20),
+        name="prepare",
+    )(*(pltpu.with_memory_space_constraint(operand, pltpu.HBM) for operand in operands))
 
 
 def first_entry(entries):
@@ -306,13 +334,13 @@
     )
 
 
-def multiply(weight, products, pieces, side, axes):
+def multiply(weight, products, pieces, side, axes, keep=False):
     entries = weight.shape[0]
     arrays = [pieces[0][0]] if pieces[0][0] is pieces[1][0] else [piece[0] for piece in pieces]
     inputs = [weight] + ([] if products is None else [products]) + arrays
 
     def body(*refs):
-        weight_ref, out_ref = refs[0], refs[-1]
+        weight_ref, out_ref = refs[0], refs[len(inputs)]
         token_refs = refs[len(inputs) - len(arrays):len(inputs)]
         core = lax.rem(lax.axis_index(TENSOR), 2)
         features = core if side == 0 else 1 - core
@@ -322,6 +350,8 @@
             far = pl.ds(pl.multiple_of((y * 2 + features) * 1024, 1024), 1024)
             value = [ref[:, y * 1024:(y + 1) * 1024] for ref in token_refs]
             value = value[0] if len(value) == 1 else jnp.concatenate(value, axis=0)
+            if keep:
+                refs[-1][:, y * 1024:(y + 1) * 1024] = value
             product = lax.dot_general(
                 weight_ref[:, far], value, (((1,), (1,)), ((), ())), preferred_element_type=jnp.float32
             )
@@ -330,12 +360,14 @@
             place = lax.rem(mine + (4 - hops), 4)
             out_ref[side, place, :, half * 128:half * 128 + 128] = total[:, i * 128:i * 128 + 128]
 
-    return call(
-        body,
-        jax.ShapeDtypeStruct((2, 4, entries, 256), jnp.float32),
+    shape = jax.ShapeDtypeStruct((2, 4, entries, 256), jnp.float32)
+    return call(
+        body,
+        (shape, jax.ShapeDtypeStruct((256, 4096), jnp.bfloat16)) if keep else shape,
         "multiply",
         inputs,
         vmem_mib=6,
+        out_specs=(VMEM, VMEM) if keep else VMEM,
         input_output_aliases={} if products is None else {1: 0},
         cost_estimate=pl.CostEstimate(flops=2 * entries * 4096 * 256, bytes_accessed=4 << 20, transcendentals=0),
     )
@@ -351,7 +383,10 @@
     targets = targets.reshape(8, 128)
 
     beside = [shift(hidden, "y", k) for k in (1, 3, 2)]
-    floors, gain, floor_stats = prepare(floor_counts.reshape(1, entries), norm_gain, targets)
+    weight, hidden, floors, gain, floor_stats = prepare(
+        weight, hidden, floor_counts.reshape(1, entries), norm_gain, targets
+    )
+    weight, *beside = lax.optimization_barrier((weight, *beside))
     raw, own = square_sums([hidden] + beside)
     upper, lower = normalize(raw, own, shift(own, "c", 1), gain)
     axes = "xz"
@@ -367,25 +402,25 @@
     up = lambda value: shift(value, axes, 1)
     down = lambda value: shift(value, axes, 3)
     upper, lower = block
+    hold = lax.optimization_barrier
     upper_1, lower_3 = up(upper), down(lower)
     swapped = swap(upper), swap(lower)
     products = multiply(weight, None, [(upper, 0, 0), (lower, 0, 1)], 0, axes)
-    upper, lower, products = lax.optimization_barrier((upper, lower, products))
+    upper, lower, products = hold((upper, lower, products))
     upper_3, lower_1 = down(upper), up(lower)
     products = multiply(weight, products, [(swapped[0], 0, 0), (swapped[1], 0, 1)], 1, axes)
-    upper_1, lower_3, products = lax.optimization_barrier((upper_1, lower_3, products))
+    upper_1, lower_3, products = hold((upper_1, lower_3, products))
     upper_2, lower_2 = up(upper_1), down(lower_3)
-    swapped = swap(upper_1), swap(lower_3)
+    swapped_1 = swap(upper_1), swap(lower_3)
     products = multiply(weight, products, [(upper_1, 1, 0), (lower_3, 3, 1)], 0, axes)
-    products = multiply(weight, products, [(swapped[0], 1, 0), (swapped[1], 3, 1)], 1, axes)
-    upper_3, lower_1, products = lax.optimization_barrier((upper_3, lower_1, products))
-    swapped = swap(upper_3), swap(lower_1)
     products = multiply(weight, products, [(upper_3, 3, 0), (lower_1, 1, 1)], 0, axes)
-    products = multiply(weight, products, [(swapped[0], 3, 0), (swapped[1], 1, 1)], 1, axes)
-    upper_2, lower_2, products = lax.optimization_barrier((upper_2, lower_2, products))
-    swapped = swap(upper_2), swap(lower_2)
+    upper_2, lower_2, upper_3, lower_1, products = hold((upper_2, lower_2, upper_3, lower_1, products))
+    swapped_3 = swap(upper_3), swap(lower_1)
+    swapped_2 = swap(upper_2), swap(lower_2)
     products = multiply(weight, products, [(upper_2, 2, 0), (lower_2, 2, 1)], 0, axes)
-    products = multiply(weight, products, [(swapped[0], 2, 0), (swapped[1], 2, 1)], 1, axes)
+    products = multiply(weight, products, [(swapped_1[0], 1, 0), (swapped_1[1], 3, 1)], 1, axes)
+    products = multiply(weight, products, [(swapped_3[0], 3, 0), (swapped_3[1], 1, 1)], 1, axes)
+    products = multiply(weight, products, [(swapped_2[0], 2, 0), (swapped_2[1], 2, 1)], 1, axes)
 
     logits, stats = join_halves(products, floor_stats, targets)
     group, before = stats, None

time: 124 us -> 115 us (0.927)
  local copies, waits for them, and re-layouts: 12 us -> 0.01 us
  Pallas kernels: 26.7 us -> 32 us
  waiting for transfers between devices: 47.6 us -> 42.6 us
  starting transfers between devices: 36.9 us -> 39.1 us
    unnamed x16 -> x4, local copies, waits for them, and re-layouts: 12 us -> 0.01 us
    pallas_call x0 -> x1, Pallas kernels: none -> 5.87 us  [prepare(): pl.pallas_call(body, out_shape=(pltpu.VMEM(weight.shape, jnp.bfloat16), p...]
    ppermute x34, waiting for transfers between devices: 47.6 us -> 42.6 us  [shift(): return lax.ppermute(value, BOTH, pairs)]
    ppermute x34, starting transfers between devices: 36.9 us -> 39.1 us  [shift(): return lax.ppermute(value, BOTH, pairs)]
    pallas_call x18 -> x17, Pallas kernels: 26.7 us -> 26.1 us  [call(): pl.pallas_call(body, out_shape=out_shape, in_specs=[VMEM] * len(inputs),...]
  transfers between devices with their start and end apart: 34 -> 34, of which waited for: 18 -> 17; matrix products, arithmetic and copies ran while one was open for 0% -> 0% of each run, Pallas kernels for 14% -> 19%
where the time goes in v3:
time: 115 us
  waiting for transfers between devices  42.6 us (37%)
  starting transfers between devices  39.1 us (34%)
  Pallas kernels  32 us (28%)
    ppermute x34, waiting for transfers between devices, shift(): return lax.ppermute(value, BOTH, pairs)  42.6 us
    ppermute x34, starting transfers between devices, shift(): return lax.ppermute(value, BOTH, pairs)  39.1 us
    pallas_call x17, Pallas kernels, call(): pl.pallas_call(body, out_shape=out_shape, in_specs=[VMEM] * len(inputs),...  26.1 us
    pallas_call x1, Pallas kernels, prepare(): pl.pallas_call(body, out_shape=(pltpu.VMEM(weight.shape, jnp.bfloat16), p...  5.87 us
  transfers between devices with their start and end apart: 34, of which 17 were waited for; matrix products, arithmetic and copies ran while one was open for 0% of the time, Pallas kernels for 19%

profile of v3, /device:TPU:0, one launch (start us, length us, event | category | flops | bytes accessed | tf_op | source)
XLA Modules:
  0.0 114.6 jit_solution(7285065956063132816)
XLA Ops:
  2.4 2.9 %collective-permute-start.2 = (bf16[64,1024]{1,0:T(8,128)(2,1)}, bf16[64,1024]{1,0:T(8,128)(2,1)S(1)}, u32[]{:S(2)}, u32[]{:S(2)}) collective-permute-start(bf16[64,1024]{1,0:T(8,128)(2,1)} %hidden_hbm.1), channel_id=1, source_target_pairs={{0,4},{1,5},{2,6},{3,7},{4,0},{5,1},{6,2},{7,3},{8,12},{9,13},{10,... | collective-permute-start | bytes 393224 | tf_op jit(solution)/shard_map/ppermute | solution.py:29
  6.6 5.9 %prepare.1 = (bf16[1002,8192]{1,0:T(8,128)(2,1)S(1)}, bf16[64,1024]{1,0:T(8,128)(2,1)S(1)}, f32[1024,128]{1,0:T(8,128)S(1)}, f32[1,8192]{1,0:T(1,128)S(1)}, f32[16,128]{1,0:T(8,128)S(1)}) custom-call(bf16[1002,8192]{1,0:T(8,128)(2,1)} %bitcast.9, bf16[64,1024]{1,0:T(8,128)(2,1)} %hidden_hbm.1, s32[1,1002]{1,0:T(1,128)} %bitcast.11, ...), custom_call_target="tpu_custom_call" | custom-call | tf_op jit(solution)/shard_map/prepare/pallas_call | solution.py:85
  19.6 2.3 %collective-permute-done.4.refs_2_ = bf16[32,4096]{1,0:T(8,128)(2,1)S(1)} collective-permute-done((bf16[32,4096]{1,0:T(8,128)(2,1)S(1)}, bf16[32,4096]{1,0:T(8,128)(2,1)S(1)}, u32[]{:S(2)}, u32[]{:S(2)}) %collective-permute-start.4) | collective-permute-done | bytes 262176 | tf_op jit(solution)/shard_map/ppermute | solution.py:29
  22.2 3.0 %collective-permute-start.9 = (bf16[32,4096]{1,0:T(8,128)(2,1)S(1)}, bf16[32,4096]{1,0:T(8,128)(2,1)S(1)}, u32[]{:S(2)}, u32[]{:S(2)}) collective-permute-start(bf16[32,4096]{1,0:T(8,128)(2,1)S(1)} %collective-permute-done.5.refs_3_), channel_id=1, source_target_pairs={{0,96},{1,25},{2,98},{3,27},{4,100},{5,29},{6,102},{7,31},{8,104},... | collective-permute-start | bytes 786440 | tf_op jit(solution)/shard_map/ppermute | solution.py:29
  26.7 2.8 %collective-permute-done.8.refs_6_ = bf16[32,4096]{1,0:T(8,128)(2,1)S(1)} collective-permute-done((bf16[32,4096]{1,0:T(8,128)(2,1)S(1)}, bf16[32,4096]{1,0:T(8,128)(2,1)S(1)}, u32[]{:S(2)}, u32[]{:S(2)}) %collective-permute-start.8) | collective-permute-done | bytes 262176 | tf_op jit(solution)/shard_map/ppermute | solution.py:29
  32.2 2.1 %collective-permute-start.11 = (bf16[128,4096]{1,0:T(8,128)(2,1)S(1)}, bf16[128,4096]{1,0:T(8,128)(2,1)S(1)}, u32[]{:S(2)}, u32[]{:S(2)}) collective-permute-start(bf16[128,4096]{1,0:T(8,128)(2,1)S(1)} %get-tuple-element.55.refs_2_), channel_id=1, source_target_pairs={{0,24},{1,97},{2,26},{3,99},{4,28},{5,101},{6,30},{7,103},{8,0},{9... | collective-permute-start | bytes 3145736 | tf_op jit(solution)/shard_map/ppermute | solution.py:29
  34.3 2.3 %multiply.8.refs_1_ = f32[2,4,1002,256]{3,2,1,0:T(8,128)S(1)} custom-call(bf16[1002,8192]{1,0:T(8,128)(2,1)S(1)} %get-tuple-element.39.refs_0_, bf16[128,4096]{1,0:T(8,128)(2,1)S(1)} %get-tuple-element.54.refs_1_, bf16[128,4096]{1,0:T(8,128)(2,1)S(1)} %get-tuple-element.55.refs_2_), custom_call_target="tpu_custom_call" | custom-call | flops 2101346304 | bytes 4194304 | tf_op jit(solution)/shard_map/multiply/pallas_call | solution.py:33
  36.7 2.1 %collective-permute-start.16 = (bf16[128,4096]{1,0:T(8,128)(2,1)S(1)}, bf16[128,4096]{1,0:T(8,128)(2,1)S(1)}, u32[]{:S(2)}, u32[]{:S(2)}) collective-permute-start(bf16[128,4096]{1,0:T(8,128)(2,1)S(1)} %get-tuple-element.54.refs_1_), channel_id=1, source_target_pairs={{0,24},{1,97},{2,26},{3,99},{4,28},{5,101},{6,30},{7,103},{8,0},{9... | collective-permute-start | bytes 3145736 | tf_op jit(solution)/shard_map/ppermute | solution.py:29
  38.8 2.3 %multiply.9.refs_1_ = f32[2,4,1002,256]{3,2,1,0:T(8,128)S(1)} custom-call(bf16[1002,8192]{1,0:T(8,128)(2,1)S(1)} %get-tuple-element.39.refs_0_, f32[2,4,1002,256]{3,2,1,0:T(8,128)S(1)} %multiply.8.refs_1_, bf16[128,4096]{1,0:T(8,128)(2,1)S(1)} %collective-permute-done.12.refs_2_, ...), custom_call_target="tpu_custom_call", output_to_operand_aliasing={{}: (1, {})} | custom-call | flops 2101346304 | bytes 4194304 | tf_op jit(solution)/shard_map/multiply/pallas_call | solution.py:33
  41.1 6.0 %collective-permute-done.10.refs_2_ = bf16[128,4096]{1,0:T(8,128)(2,1)S(1)} collective-permute-done((bf16[128,4096]{1,0:T(8,128)(2,1)S(1)}, bf16[128,4096]{1,0:T(8,128)(2,1)S(1)}, u32[]{:S(2)}, u32[]{:S(2)}) %collective-permute-start.10) | collective-permute-done | bytes 1048608 | tf_op jit(solution)/shard_map/ppermute | solution.py:29
  50.4 2.3 %multiply.10.refs_1_ = f32[2,4,1002,256]{3,2,1,0:T(8,128)S(1)} custom-call(bf16[1002,8192]{1,0:T(8,128)(2,1)S(1)} %get-tuple-element.39.refs_0_, f32[2,4,1002,256]{3,2,1,0:T(8,128)S(1)} %multiply.9.refs_1_, bf16[128,4096]{1,0:T(8,128)(2,1)S(1)} %collective-permute-done.10.refs_2_, ...), custom_call_target="tpu_custom_call", output_to_operand_aliasing={{}: (1, {})} | custom-call | flops 2101346304 | bytes 4194304 | tf_op jit(solution)/shard_map/multiply/pallas_call | solution.py:33
  52.7 5.6 %collective-permute-done.16.refs_2_ = bf16[128,4096]{1,0:T(8,128)(2,1)S(1)} collective-permute-done((bf16[128,4096]{1,0:T(8,128)(2,1)S(1)}, bf16[128,4096]{1,0:T(8,128)(2,1)S(1)}, u32[]{:S(2)}, u32[]{:S(2)}) %collective-permute-start.16) | collective-permute-done | bytes 1048608 | tf_op jit(solution)/shard_map/ppermute | solution.py:29
  58.3 2.3 %multiply.11.refs_1_ = f32[2,4,1002,256]{3,2,1,0:T(8,128)S(1)} custom-call(bf16[1002,8192]{1,0:T(8,128)(2,1)S(1)} %get-tuple-element.39.refs_0_, f32[2,4,1002,256]{3,2,1,0:T(8,128)S(1)} %multiply.10.refs_1_, bf16[128,4096]{1,0:T(8,128)(2,1)S(1)} %collective-permute-done.16.refs_2_, ...), custom_call_target="tpu_custom_call", output_to_operand_aliasing={{}: (1, {})} | custom-call | flops 2101346304 | bytes 4194304 | tf_op jit(solution)/shard_map/multiply/pallas_call | solution.py:33
  60.7 8.9 %collective-permute-done.14.refs_2_ = bf16[128,4096]{1,0:T(8,128)(2,1)S(1)} collective-permute-done((bf16[128,4096]{1,0:T(8,128)(2,1)S(1)}, bf16[128,4096]{1,0:T(8,128)(2,1)S(1)}, u32[]{:S(2)}, u32[]{:S(2)}) %collective-permute-start.14) | collective-permute-done | bytes 1048608 | tf_op jit(solution)/shard_map/ppermute | solution.py:29
  70.6 2.3 %multiply.12.refs_1_ = f32[2,4,1002,256]{3,2,1,0:T(8,128)S(1)} custom-call(bf16[1002,8192]{1,0:T(8,128)(2,1)S(1)} %get-tuple-element.39.refs_0_, f32[2,4,1002,256]{3,2,1,0:T(8,128)S(1)} %multiply.11.refs_1_, bf16[128,4096]{1,0:T(8,128)(2,1)S(1)} %collective-permute-done.14.refs_2_, ...), custom_call_target="tpu_custom_call", output_to_operand_aliasing={{}: (1, {})} | custom-call | flops 2101346304 | bytes 4194304 | tf_op jit(solution)/shard_map/multiply/pallas_call | solution.py:33
  73.0 2.3 %multiply.13.refs_1_ = f32[2,4,1002,256]{3,2,1,0:T(8,128)S(1)} custom-call(bf16[1002,8192]{1,0:T(8,128)(2,1)S(1)} %get-tuple-element.39.refs_0_, f32[2,4,1002,256]{3,2,1,0:T(8,128)S(1)} %multiply.12.refs_1_, bf16[128,4096]{1,0:T(8,128)(2,1)S(1)} %collective-permute-done.18.refs_2_, ...), custom_call_target="tpu_custom_call", output_to_operand_aliasing={{}: (1, {})} | custom-call | flops 2101346304 | bytes 4194304 | tf_op jit(solution)/shard_map/multiply/pallas_call | solution.py:33
  75.3 2.3 %multiply.14.refs_1_ = f32[2,4,1002,256]{3,2,1,0:T(8,128)S(1)} custom-call(bf16[1002,8192]{1,0:T(8,128)(2,1)S(1)} %get-tuple-element.39.refs_0_, f32[2,4,1002,256]{3,2,1,0:T(8,128)S(1)} %multiply.13.refs_1_, bf16[128,4096]{1,0:T(8,128)(2,1)S(1)} %collective-permute-done.20.refs_2_, ...), custom_call_target="tpu_custom_call", output_to_operand_aliasing={{}: (1, {})} | custom-call | flops 2101346304 | bytes 4194304 | tf_op jit(solution)/shard_map/multiply/pallas_call | solution.py:33
  77.7 2.3 %multiply.15.products_ref = f32[2,4,1002,256]{3,2,1,0:T(8,128)S(1)} custom-call(bf16[1002,8192]{1,0:T(8,128)(2,1)S(1)} %get-tuple-element.39.refs_0_, f32[2,4,1002,256]{3,2,1,0:T(8,128)S(1)} %multiply.14.refs_1_, bf16[128,4096]{1,0:T(8,128)(2,1)S(1)} %collective-permute-done.22.refs_2_, ...), custom_call_target="tpu_custom_call", output_to_operand_aliasing={{}: (1, {})} | custom-call | flops 2101346304 | bytes 4194304 | tf_op jit(solution)/shard_map/multiply/pallas_call | solution.py:33
  80.0 2.4 %join_halves.1 = (f32[1024,1024]{1,0:T(8,128)S(1)}, f32[40,128]{1,0:T(8,128)S(1)}) custom-call(f32[2,4,1002,256]{3,2,1,0:T(8,128)S(1)} %multiply.15.products_ref, f32[16,128]{1,0:T(8,128)S(1)} %get-tuple-element.62.floors_ref, s32[8,128]{1,0:T(8,128)S(1)} %bitcast.7), custom_call_target="tpu_custom_call" | custom-call | tf_op jit(solution)/shard_map/join_halves/pallas_call | solution.py:33
  89.1 3.0 %collective-permute-done.25.refs_1_ = f32[40,128]{1,0:T(8,128)S(1)} collective-permute-done((f32[40,128]{1,0:T(8,128)S(1)}, f32[40,128]{1,0:T(8,128)S(1)}, u32[]{:S(2)}, u32[]{:S(2)}) %collective-permute-start.25) | collective-permute-done | bytes 20512 | tf_op jit(solution)/shard_map/ppermute | solution.py:29
  92.2 3.6 %collective-permute-start.30 = (f32[40,128]{1,0:T(8,128)S(1)}, f32[40,128]{1,0:T(8,128)S(1)}, u32[]{:S(2)}, u32[]{:S(2)}) collective-permute-start(f32[40,128]{1,0:T(8,128)S(1)} %get-tuple-element.68.refs_0_), channel_id=1, source_target_pairs={{0,16},{1,17},{2,18},{3,19},{4,20},{5,21},{6,22},{7,23},{8,24},{9,... | collective-permute-start | bytes 61448 | tf_op jit(solution)/shard_map/ppermute | solution.py:29
  99.5 2.2 %collective-permute-done.28.refs_1_ = f32[40,128]{1,0:T(8,128)S(1)} collective-permute-done((f32[40,128]{1,0:T(8,128)S(1)}, f32[40,128]{1,0:T(8,128)S(1)}, u32[]{:S(2)}, u32[]{:S(2)}) %collective-permute-start.28) | collective-permute-done | bytes 20512 | tf_op jit(solution)/shard_map/ppermute | solution.py:29
  107.9 2.2 %collective-permute-done.31.refs_1_ = f32[40,128]{1,0:T(8,128)S(1)} collective-permute-done((f32[40,128]{1,0:T(8,128)S(1)}, f32[40,128]{1,0:T(8,128)S(1)}, u32[]{:S(2)}, u32[]{:S(2)}) %collective-permute-start.31) | collective-permute-done | bytes 20512 | tf_op jit(solution)/shard_map/ppermute | solution.py:29
  110.8 3.8 %finish.1 = f32[1002,1024]{1,0:T(8,128)} custom-call(f32[1024,1024]{1,0:T(8,128)S(1)} %get-tuple-element.63.logits_ref, f32[1024,128]{1,0:T(8,128)S(1)} %get-tuple-element.64.floors_ref, f32[40,128]{1,0:T(8,128)S(1)} %get-tuple-element.65.refs_0_.refs_5_.stats_ref, f32[24,128]{1,0:T(8,128)S(1)} %get-tuple-element.72.terms_ref), custom_call_target="tpu_custom_call" | custom-call | tf_op jit(solution)/shard_map/finish/pallas_call | solution.py:33
  (66 shorter events, 36.4 us)
Async XLA Ops:
  0.6 11.9 %collective-permute-start = (bf16[64,1024]{1,0:T(8,128)(2,1)}, bf16[64,1024]{1,0:T(8,128)(2,1)S(1)}, u32[]{:S(2)}, u32[]{:S(2)}) collective-permute-start(bf16[64,1024]{1,0:T(8,128)(2,1)} %hidden_hbm.1), channel_id=1, source_target_pairs={{0,2},{1,3},{2,4},{3,5},{4,6},{5,7},{6,0},{7,1},{8,10},{9,11},{10,... | collective-permute-start | bytes 393224 | tf_op jit(solution)/shard_map/ppermute | solution.py:29
  2.4 10.1 %collective-permute-start.2 = (bf16[64,1024]{1,0:T(8,128)(2,1)}, bf16[64,1024]{1,0:T(8,128)(2,1)S(1)}, u32[]{:S(2)}, u32[]{:S(2)}) collective-permute-start(bf16[64,1024]{1,0:T(8,128)(2,1)} %hidden_hbm.1), channel_id=1, source_target_pairs={{0,4},{1,5},{2,6},{3,7},{4,0},{5,1},{6,2},{7,3},{8,12},{9,13},{10,... | collective-permute-start | bytes 393224 | tf_op jit(solution)/shard_map/ppermute | solution.py:29
  5.3 7.2 %collective-permute-start.1 = (bf16[64,1024]{1,0:T(8,128)(2,1)}, bf16[64,1024]{1,0:T(8,128)(2,1)S(1)}, u32[]{:S(2)}, u32[]{:S(2)}) collective-permute-start(bf16[64,1024]{1,0:T(8,128)(2,1)} %hidden_hbm.1), channel_id=1, source_target_pairs={{0,6},{1,7},{2,0},{3,1},{4,2},{5,3},{6,4},{7,5},{8,14},{9,15},{10,... | collective-permute-start | bytes 393224 | tf_op jit(solution)/shard_map/ppermute | solution.py:29
  14.2 7.7 %collective-permute-start.4 = (bf16[32,4096]{1,0:T(8,128)(2,1)S(1)}, bf16[32,4096]{1,0:T(8,128)(2,1)S(1)}, u32[]{:S(2)}, u32[]{:S(2)}) collective-permute-start(bf16[32,4096]{1,0:T(8,128)(2,1)S(1)} %get-tuple-element.47.refs_0_), channel_id=1, source_target_pairs={{0,32},{1,9},{2,34},{3,11},{4,36},{5,13},{6,38},{7,15},{8,40},{9,1... | collective-permute-start | bytes 786440 | tf_op jit(solution)/shard_map/ppermute | solution.py:29
  15.8 6.4 %collective-permute-start.5 = (bf16[32,4096]{1,0:T(8,128)(2,1)S(1)}, bf16[32,4096]{1,0:T(8,128)(2,1)S(1)}, u32[]{:S(2)}, u32[]{:S(2)}) collective-permute-start(bf16[32,4096]{1,0:T(8,128)(2,1)S(1)} %get-tuple-element.48.refs_1_), channel_id=1, source_target_pairs={{0,96},{1,25},{2,98},{3,27},{4,100},{5,29},{6,102},{7,31},{8,104},... | collective-permute-start | bytes 786440 | tf_op jit(solution)/shard_map/ppermute | solution.py:29
  17.5 7.6 %collective-permute-start.6 = (bf16[32,4096]{1,0:T(8,128)(2,1)S(1)}, bf16[32,4096]{1,0:T(8,128)(2,1)S(1)}, u32[]{:S(2)}, u32[]{:S(2)}) collective-permute-start(bf16[32,4096]{1,0:T(8,128)(2,1)S(1)} %get-tuple-element.47.refs_0_), channel_id=1, source_target_pairs={{0,96},{1,25},{2,98},{3,27},{4,100},{5,29},{6,102},{7,31},{8,104},... | collective-permute-start | bytes 786440 | tf_op jit(solution)/shard_map/ppermute | solution.py:29
  19.1 7.6 %collective-permute-start.7 = (bf16[32,4096]{1,0:T(8,128)(2,1)S(1)}, bf16[32,4096]{1,0:T(8,128)(2,1)S(1)}, u32[]{:S(2)}, u32[]{:S(2)}) collective-permute-start(bf16[32,4096]{1,0:T(8,128)(2,1)S(1)} %get-tuple-element.48.refs_1_), channel_id=1, source_target_pairs={{0,32},{1,9},{2,34},{3,11},{4,36},{5,13},{6,38},{7,15},{8,40},{9,1... | collective-permute-start | bytes 786440 | tf_op jit(solution)/shard_map/ppermute | solution.py:29
  21.9 7.6 %collective-permute-start.8 = (bf16[32,4096]{1,0:T(8,128)(2,1)S(1)}, bf16[32,4096]{1,0:T(8,128)(2,1)S(1)}, u32[]{:S(2)}, u32[]{:S(2)}) collective-permute-start(bf16[32,4096]{1,0:T(8,128)(2,1)S(1)} %collective-permute-done.4.refs_2_), channel_id=1, source_target_pairs={{0,32},{1,9},{2,34},{3,11},{4,36},{5,13},{6,38},{7,15},{8,40},{9,1... | collective-permute-start | bytes 786440 | tf_op jit(solution)/shard_map/ppermute | solution.py:29
  22.2 7.3 %collective-permute-start.9 = (bf16[32,4096]{1,0:T(8,128)(2,1)S(1)}, bf16[32,4096]{1,0:T(8,128)(2,1)S(1)}, u32[]{:S(2)}, u32[]{:S(2)}) collective-permute-start(bf16[32,4096]{1,0:T(8,128)(2,1)S(1)} %collective-permute-done.5.refs_3_), channel_id=1, source_target_pairs={{0,96},{1,25},{2,98},{3,27},{4,100},{5,29},{6,102},{7,31},{8,104},... | collective-permute-start | bytes 786440 | tf_op jit(solution)/shard_map/ppermute | solution.py:29
  29.7 9.1 %collective-permute-start.12 = (bf16[128,4096]{1,0:T(8,128)(2,1)S(1)}, bf16[128,4096]{1,0:T(8,128)(2,1)S(1)}, u32[]{:S(2)}, u32[]{:S(2)}) collective-permute-start(bf16[128,4096]{1,0:T(8,128)(2,1)S(1)} %get-tuple-element.54.refs_1_), channel_id=1, source_target_pairs={{0,1},{1,0},{2,3},{3,2},{4,5},{5,4},{6,7},{7,6},{8,9},{9,8},{10,11... | collective-permute-start | bytes 3145736 | tf_op jit(solution)/shard_map/ppermute | solution.py:29
  29.8 9.0 %collective-permute-start.13 = (bf16[128,4096]{1,0:T(8,128)(2,1)S(1)}, bf16[128,4096]{1,0:T(8,128)(2,1)S(1)}, u32[]{:S(2)}, u32[]{:S(2)}) collective-permute-start(bf16[128,4096]{1,0:T(8,128)(2,1)S(1)} %get-tuple-element.55.refs_2_), channel_id=1, source_target_pairs={{0,1},{1,0},{2,3},{3,2},{4,5},{5,4},{6,7},{7,6},{8,9},{9,8},{10,11... | collective-permute-start | bytes 3145736 | tf_op jit(solution)/shard_map/ppermute | solution.py:29
  30.3 16.8 %collective-permute-start.10 = (bf16[128,4096]{1,0:T(8,128)(2,1)S(1)}, bf16[128,4096]{1,0:T(8,128)(2,1)S(1)}, u32[]{:S(2)}, u32[]{:S(2)}) collective-permute-start(bf16[128,4096]{1,0:T(8,128)(2,1)S(1)} %get-tuple-element.54.refs_1_), channel_id=1, source_target_pairs={{0,8},{1,33},{2,10},{3,35},{4,12},{5,37},{6,14},{7,39},{8,16},{9,4... | collective-permute-start | bytes 3145736 | tf_op jit(solution)/shard_map/ppermute | solution.py:29
  32.2 14.9 %collective-permute-start.11 = (bf16[128,4096]{1,0:T(8,128)(2,1)S(1)}, bf16[128,4096]{1,0:T(8,128)(2,1)S(1)}, u32[]{:S(2)}, u32[]{:S(2)}) collective-permute-start(bf16[128,4096]{1,0:T(8,128)(2,1)S(1)} %get-tuple-element.55.refs_2_), channel_id=1, source_target_pairs={{0,24},{1,97},{2,26},{3,99},{4,28},{5,101},{6,30},{7,103},{8,0},{9... | collective-permute-start | bytes 3145736 | tf_op jit(solution)/shard_map/ppermute | solution.py:29
  36.7 21.6 %collective-permute-start.16 = (bf16[128,4096]{1,0:T(8,128)(2,1)S(1)}, bf16[128,4096]{1,0:T(8,128)(2,1)S(1)}, u32[]{:S(2)}, u32[]{:S(2)}) collective-permute-start(bf16[128,4096]{1,0:T(8,128)(2,1)S(1)} %get-tuple-element.54.refs_1_), channel_id=1, source_target_pairs={{0,24},{1,97},{2,26},{3,99},{4,28},{5,101},{6,30},{7,103},{8,0},{9... | collective-permute-start | bytes 3145736 | tf_op jit(solution)/shard_map/ppermute | solution.py:29
  38.8 19.6 %collective-permute-start.17 = (bf16[128,4096]{1,0:T(8,128)(2,1)S(1)}, bf16[128,4096]{1,0:T(8,128)(2,1)S(1)}, u32[]{:S(2)}, u32[]{:S(2)}) collective-permute-start(bf16[128,4096]{1,0:T(8,128)(2,1)S(1)} %get-tuple-element.55.refs_2_), channel_id=1, source_target_pairs={{0,8},{1,33},{2,10},{3,35},{4,12},{5,37},{6,14},{7,39},{8,16},{9,4... | collective-permute-start | bytes 3145736 | tf_op jit(solution)/shard_map/ppermute | solution.py:29
  47.1 22.5 %collective-permute-start.14 = (bf16[128,4096]{1,0:T(8,128)(2,1)S(1)}, bf16[128,4096]{1,0:T(8,128)(2,1)S(1)}, u32[]{:S(2)}, u32[]{:S(2)}) collective-permute-start(bf16[128,4096]{1,0:T(8,128)(2,1)S(1)} %collective-permute-done.10.refs_2_), channel_id=1, source_target_pairs={{0,8},{1,33},{2,10},{3,35},{4,12},{5,37},{6,14},{7,39},{8,16},{9,4... | collective-permute-start | bytes 3145736 | tf_op jit(solution)/shard_map/ppermute | solution.py:29
  48.9 20.6 %collective-permute-start.15 = (bf16[128,4096]{1,0:T(8,128)(2,1)S(1)}, bf16[128,4096]{1,0:T(8,128)(2,1)S(1)}, u32[]{:S(2)}, u32[]{:S(2)}) collective-permute-start(bf16[128,4096]{1,0:T(8,128)(2,1)S(1)} %collective-permute-done.11.refs_3_), channel_id=1, source_target_pairs={{0,24},{1,97},{2,26},{3,99},{4,28},{5,101},{6,30},{7,103},{8,0},{9... | collective-permute-start | bytes 3145736 | tf_op jit(solution)/shard_map/ppermute | solution.py:29
  50.4 19.8 %collective-permute-start.18 = (bf16[128,4096]{1,0:T(8,128)(2,1)S(1)}, bf16[128,4096]{1,0:T(8,128)(2,1)S(1)}, u32[]{:S(2)}, u32[]{:S(2)}) collective-permute-start(bf16[128,4096]{1,0:T(8,128)(2,1)S(1)} %collective-permute-done.10.refs_2_), channel_id=1, source_target_pairs={{0,1},{1,0},{2,3},{3,2},{4,5},{5,4},{6,7},{7,6},{8,9},{9,8},{10,11... | collective-permute-start | bytes 3145736 | tf_op jit(solution)/shard_map/ppermute | solution.py:29
  58.2 14.7 %collective-permute-start.19 = (bf16[128,4096]{1,0:T(8,128)(2,1)S(1)}, bf16[128,4096]{1,0:T(8,128)(2,1)S(1)}, u32[]{:S(2)}, u32[]{:S(2)}) collective-permute-start(bf16[128,4096]{1,0:T(8,128)(2,1)S(1)} %collective-permute-done.11.refs_3_), channel_id=1, source_target_pairs={{0,1},{1,0},{2,3},{3,2},{4,5},{5,4},{6,7},{7,6},{8,9},{9,8},{10,11... | collective-permute-start | bytes 3145736 | tf_op jit(solution)/shard_map/ppermute | solution.py:29
  69.6 5.7 %collective-permute-start.20 = (bf16[128,4096]{1,0:T(8,128)(2,1)S(1)}, bf16[128,4096]{1,0:T(8,128)(2,1)S(1)}, u32[]{:S(2)}, u32[]{:S(2)}) collective-permute-start(bf16[128,4096]{1,0:T(8,128)(2,1)S(1)} %collective-permute-done.16.refs_2_), channel_id=1, source_target_pairs={{0,1},{1,0},{2,3},{3,2},{4,5},{5,4},{6,7},{7,6},{8,9},{9,8},{10,11... | collective-permute-start | bytes 3145736 | tf_op jit(solution)/shard_map/ppermute | solution.py:29
  69.6 5.7 %collective-permute-start.21 = (bf16[128,4096]{1,0:T(8,128)(2,1)S(1)}, bf16[128,4096]{1,0:T(8,128)(2,1)S(1)}, u32[]{:S(2)}, u32[]{:S(2)}) collective-permute-start(bf16[128,4096]{1,0:T(8,128)(2,1)S(1)} %collective-permute-done.17.refs_3_), channel_id=1, source_target_pairs={{0,1},{1,0},{2,3},{3,2},{4,5},{5,4},{6,7},{7,6},{8,9},{9,8},{10,11... | collective-permute-start | bytes 3145736 | tf_op jit(solution)/shard_map/ppermute | solution.py:29
  70.1 7.5 %collective-permute-start.22 = (bf16[128,4096]{1,0:T(8,128)(2,1)S(1)}, bf16[128,4096]{1,0:T(8,128)(2,1)S(1)}, u32[]{:S(2)}, u32[]{:S(2)}) collective-permute-start(bf16[128,4096]{1,0:T(8,128)(2,1)S(1)} %collective-permute-done.14.refs_2_), channel_id=1, source_target_pairs={{0,1},{1,0},{2,3},{3,2},{4,5},{5,4},{6,7},{7,6},{8,9},{9,8},{10,11... | collective-permute-start | bytes 3145736 | tf_op jit(solution)/shard_map/ppermute | solution.py:29
  70.1 7.6 %collective-permute-start.23 = (bf16[128,4096]{1,0:T(8,128)(2,1)S(1)}, bf16[128,4096]{1,0:T(8,128)(2,1)S(1)}, u32[]{:S(2)}, u32[]{:S(2)}) collective-permute-start(bf16[128,4096]{1,0:T(8,128)(2,1)S(1)} %collective-permute-done.15.refs_3_), channel_id=1, source_target_pairs={{0,1},{1,0},{2,3},{3,2},{4,5},{5,4},{6,7},{7,6},{8,9},{9,8},{10,11... | collective-permute-start | bytes 3145736 | tf_op jit(solution)/shard_map/ppermute | solution.py:29
  92.2 5.6 %collective-permute-start.30 = (f32[40,128]{1,0:T(8,128)S(1)}, f32[40,128]{1,0:T(8,128)S(1)}, u32[]{:S(2)}, u32[]{:S(2)}) collective-permute-start(f32[40,128]{1,0:T(8,128)S(1)} %get-tuple-element.68.refs_0_), channel_id=1, source_target_pairs={{0,16},{1,17},{2,18},{3,19},{4,20},{5,21},{6,22},{7,23},{8,24},{9,... | collective-permute-start | bytes 61448 | tf_op jit(solution)/shard_map/ppermute | solution.py:29
  (12 other events, 72.6 us)

commit v4 on v3

--- a/solution.py
+++ b/solution.py
@@ -112,12 +112,12 @@
 def join_halves(products, floor_stats, targets):
     entries = products.shape[2]
 
-    def body(products_ref, floors_ref, targets_ref, logits_ref, stats_ref):
+    def body(products_ref, floors_ref, targets_ref, weights_ref, stats_ref):
         core = lax.rem(lax.axis_index(TENSOR), 2)
         first = first_entry(entries)
         rows = lax.broadcasted_iota(jnp.int32, (entries, 128), 0)
         left = lax.broadcasted_iota(jnp.int32, (entries, 128), 1) < 64
-        logits_ref[1000:1024, :] = jnp.full((24, 1024), -jnp.inf, jnp.float32)
+        weights_ref[1000:1024, :] = jnp.zeros((24, 1024), jnp.float32)
         for j in range(ROWS):
             x, z = j // 2, j % 2 * 2
             near = slice(x // 2 * 128, x // 2 * 128 + 128)
@@ -127,9 +127,9 @@
             else:
                 one = pltpu.roll(one, 64, 1)
             tile = products_ref[1 - core, x, :, z * 64:z * 64 + 128] + jnp.where(left, one, two)
-            logits_ref[0:entries, j * 128:(j + 1) * 128] = tile
             peak = jnp.max(tile, axis=0, keepdims=True)
             exponent = jnp.exp(tile - peak)
+            weights_ref[0:entries, j * 128:(j + 1) * 128] = exponent
             hit = rows == targets_ref[j:j + 1, :] - first
             stats_ref[j:j + 1, :] = peak
             stats_ref[8 + j:9 + j, :] = jnp.sum(exponent, axis=0, keepdims=True)
@@ -211,50 +211,67 @@
     )
 
 
-def finish(logits, floors, stats, terms, entries):
+def running_sums(weights, floors):
     block = 256
 
-    def body(logits_ref, floors_ref, stats_ref, terms_ref, out_ref, carry_ref, floor_carry_ref):
-        i = pl.program_id(0)
-
-        @pl.when(i == 0)
-        def _():
-            carry_ref[...] = jnp.zeros_like(carry_ref)
-            floor_carry_ref[...] = jnp.zeros_like(floor_carry_ref)
-
-        rows = pl.ds(pl.multiple_of(i * block, block), block)
+    def body(weights_ref, floors_ref, sums_ref, floor_sums_ref):
         below = lax.broadcasted_iota(jnp.int32, (block, block), 1)
         lower = (below < lax.broadcasted_iota(jnp.int32, (block, block), 0)).astype(jnp.bfloat16)
-        floors = floors_ref[rows, :]
-        floor_sums = floor_carry_ref[0:1, :] + jnp.dot(
-            lower, floors.astype(jnp.bfloat16), preferred_element_type=jnp.float32
-        )
-        floor_carry_ref[0:1, :] += jnp.sum(floors, axis=0, keepdims=True)
-        for j in range(0, ROWS, 2):
-            lanes = slice(j * 128, (j + 2) * 128)
-            peak, scale, inverse, offset = (
-                jnp.concatenate([ref[at + j:at + j + 1, :], ref[at + j + 1:at + j + 2, :]], axis=1)
-                for ref, at in ((stats_ref, 0), (terms_ref, 0), (terms_ref, 8), (terms_ref, 16))
+        carry = [jnp.zeros((1, 256), jnp.float32)] * (ROWS // 2)
+        floor_carry = jnp.zeros((1, 128), jnp.float32)
+        for b in range(1024 // block):
+            rows = slice(b * block, (b + 1) * block)
+            floors = floors_ref[rows, :]
+            floor_sums_ref[rows, :] = floor_carry + jnp.dot(
+                lower, floors.astype(jnp.bfloat16), preferred_element_type=jnp.float32
             )
-            value = jnp.exp(logits_ref[rows, lanes] - peak)
-            high = value.astype(jnp.bfloat16)
-            low = (value - high.astype(jnp.float32)).astype(jnp.bfloat16)
-            sums = jnp.dot(lower, high, preferred_element_type=jnp.float32)
-            sums = sums + jnp.dot(lower, low, preferred_element_type=jnp.float32)
-            sums = sums + carry_ref[0:1, lanes]
-            carry_ref[0:1, lanes] += jnp.sum(value, axis=0, keepdims=True)
-            wide = jnp.concatenate([floor_sums, floor_sums], axis=1)
-            out_ref[:, lanes] = sums * scale + wide * inverse + offset
+            floor_carry = floor_carry + jnp.sum(floors, axis=0, keepdims=True)
+            for j in range(ROWS // 2):
+                lanes = slice(j * 256, (j + 1) * 256)
+                value = weights_ref[rows, lanes]
+                high = value.astype(jnp.bfloat16)
+                low = (value - high.astype(jnp.float32)).astype(jnp.bfloat16)
+                sums = jnp.dot(lower, high, preferred_element_type=jnp.float32)
+                sums = sums + jnp.dot(lower, low, preferred_element_type=jnp.float32)
+                sums_ref[rows, lanes] = sums + carry[j]
+                carry[j] = carry[j] + jnp.sum(value, axis=0, keepdims=True)
+
+    return call(
+        body,
+        (
+            jax.ShapeDtypeStruct((1024, 1024), jnp.float32),
+            jax.ShapeDtypeStruct((1024, 128), jnp.float32),
+        ),
+        "running_sums",
+        (weights, floors),
+        vmem_mib=4,
+        out_specs=(VMEM, VMEM),
+    )
+
+
+def finish(sums, floor_sums, terms, entries):
+    def body(sums_ref, floors_ref, terms_ref, out_hbm, out_ref, sems):
+        copies = []
+        for j in range(ROWS):
+            lanes = slice(j * 128, (j + 1) * 128)
+            out_ref[:, lanes] = (
+                sums_ref[0:entries, lanes] * terms_ref[j:j + 1, :]
+                + floors_ref[0:entries, :] * terms_ref[8 + j:9 + j, :]
+                + terms_ref[16 + j:17 + j, :]
+            )
+            copies.append(pltpu.make_async_copy(out_ref.at[:, lanes], out_hbm.at[:, lanes], sems.at[j]))
+            copies[-1].start()
+        for copy in copies:
+            copy.wait()
 
     return call(
         body,
         jax.ShapeDtypeStruct((entries, 1024), jnp.float32),
         "finish",
-        (logits, floors, stats, terms),
+        (sums, floor_sums, terms),
         vmem_mib=8,
-        grid=(-(-entries // block),),
-        scratch=[pltpu.VMEM((8, 1024), jnp.float32), pltpu.VMEM((8, 128), jnp.float32)],
-        out_specs=pl.BlockSpec((block, 1024), lambda i: (i, 0)),
+        scratch=[pltpu.VMEM((entries, 1024), jnp.float32), pltpu.SemaphoreType.DMA((ROWS,))],
+        out_specs=pl.BlockSpec(memory_space=pltpu.HBM),
     )
 
 
@@ -316,6 +333,7 @@
         mine = own_coordinate(axes)
         for (side, hops, _), ref in zip(pieces, refs):
             place = lax.rem(mine + (4 - hops), 4)
+            refs[-3][pl.ds(pl.multiple_of(place * rows + side * half, half), half), :] = ref[...]
             for i, out_ref in enumerate(refs[-2:]):
 
                 @pl.when(place // 2 == i)
@@ -323,14 +341,15 @@
                     at = pl.multiple_of((place - 2 * i) * rows + side * half, half)
                     out_ref[pl.ds(at, half), :] = ref[...]
 
+    whole = jax.ShapeDtypeStruct((4 * rows, 4096), jnp.bfloat16)
     shape = jax.ShapeDtypeStruct((2 * rows, 4096), jnp.bfloat16)
     return call(
         body,
-        (shape, shape),
+        (whole, shape, shape),
         "stack",
         [piece[2] for piece in pieces],
         vmem_mib=4,
-        out_specs=(VMEM, VMEM),
+        out_specs=(VMEM, VMEM, VMEM),
     )
 
 
@@ -395,20 +414,19 @@
     upper_2, lower_2 = shift(upper_1, axes, 1), shift(lower_3, axes, 3)
     pieces = [(0, 0, upper), (1, 0, lower), (0, 1, upper_1), (1, 3, lower_3)]
     pieces += [(0, 3, upper_3), (1, 1, lower_1), (0, 2, upper_2), (1, 2, lower_2)]
-    block = stack(pieces, axes)
+    block, upper, lower = stack(pieces, axes)
 
     axes = "zx"
     swap = lambda value: shift(value, "c", 1)
     up = lambda value: shift(value, axes, 1)
     down = lambda value: shift(value, axes, 3)
-    upper, lower = block
     hold = lax.optimization_barrier
     upper_1, lower_3 = up(upper), down(lower)
-    swapped = swap(upper), swap(lower)
-    products = multiply(weight, None, [(upper, 0, 0), (lower, 0, 1)], 0, axes)
+    swapped = swap(block)
+    products = multiply(weight, None, [(block, 0, 0), (block, 0, 1)], 0, axes)
     upper, lower, products = hold((upper, lower, products))
     upper_3, lower_1 = down(upper), up(lower)
-    products = multiply(weight, products, [(swapped[0], 0, 0), (swapped[1], 0, 1)], 1, axes)
+    products = multiply(weight, products, [(swapped, 0, 0), (swapped, 0, 1)], 1, axes)
     upper_1, lower_3, products = hold((upper_1, lower_3, products))
     upper_2, lower_2 = up(upper_1), down(lower_3)
     swapped_1 = swap(upper_1), swap(lower_3)
@@ -422,12 +440,13 @@
     products = multiply(weight, products, [(swapped_3[0], 3, 0), (swapped_3[1], 1, 1)], 1, axes)
     products = multiply(weight, products, [(swapped_2[0], 2, 0), (swapped_2[1], 2, 1)], 1, axes)
 
-    logits, stats = join_halves(products, floor_stats, targets)
+    weights, stats = join_halves(products, floor_stats, targets)
+    sums, floor_sums = running_sums(weights, floors)
     group, before = stats, None
     for axis in ("c", "y", "z"):
         group, before = join(axis, group, before)
     terms, bits = join("x", group, before, last=(stats, totals.reshape(8, 128)))
-    cumulative = finish(logits, floors, stats, terms, entries)
+    cumulative = finish(sums, floor_sums, terms, entries)
     return cumulative.T, bits.reshape(1024)
 
 

time: 115 us -> 113 us (0.983)
  waiting for transfers between devices: 42.6 us -> 41.2 us
    ppermute x34 -> x33, waiting for transfers between devices: 42.6 us -> 41.2 us  [shift(): return lax.ppermute(value, BOTH, pairs)]
    ppermute x34 -> x33, starting transfers between devices: 39.1 us -> 38.8 us  [shift(): return lax.ppermute(value, BOTH, pairs)]
    pallas_call x17 -> x18, Pallas kernels: 26.1 us -> 26.3 us  [call(): pl.pallas_call(body, out_shape=out_shape, in_specs=[VMEM] * len(inputs),...]
  transfers between devices with their start and end apart: 34 -> 33, of which waited for: 17 -> 15; matrix products, arithmetic and copies ran while one was open for 0% -> 0% of each run, Pallas kernels for 19% -> 21%
where the time goes in v4:
time: 113 us
  waiting for transfers between devices  41.2 us (36%)
  starting transfers between devices  38.8 us (34%)
  Pallas kernels  32.1 us (28%)
    ppermute x33, waiting for transfers between devices, shift(): return lax.ppermute(value, BOTH, pairs)  41.2 us
    ppermute x33, starting transfers between devices, shift(): return lax.ppermute(value, BOTH, pairs)  38.8 us
    pallas_call x18, Pallas kernels, call(): pl.pallas_call(body, out_shape=out_shape, in_specs=[VMEM] * len(inputs),...  26.3 us
    pallas_call x1, Pallas kernels, prepare(): pl.pallas_call(body, out_shape=(pltpu.VMEM(weight.shape, jnp.bfloat16), p...  5.87 us
  transfers between devices with their start and end apart: 33, of which 15 were waited for; matrix products, arithmetic and copies ran while one was open for 0% of the time, Pallas kernels for 21%

profile of v4, /device:TPU:0, one launch (start us, length us, event | category | flops | bytes accessed | tf_op | source)
XLA Modules:
  0.0 113.2 jit_solution(13498069577062490146)
XLA Ops:
  2.4 2.9 %collective-permute-start.2 = (bf16[64,1024]{1,0:T(8,128)(2,1)}, bf16[64,1024]{1,0:T(8,128)(2,1)S(1)}, u32[]{:S(2)}, u32[]{:S(2)}) collective-permute-start(bf16[64,1024]{1,0:T(8,128)(2,1)} %hidden_hbm.1), channel_id=1, source_target_pairs={{0,4},{1,5},{2,6},{3,7},{4,0},{5,1},{6,2},{7,3},{8,12},{9,13},{10,... | collective-permute-start | bytes 393224 | tf_op jit(solution)/shard_map/ppermute | solution.py:29
  6.6 5.9 %prepare.1 = (bf16[1002,8192]{1,0:T(8,128)(2,1)S(1)}, bf16[64,1024]{1,0:T(8,128)(2,1)S(1)}, f32[1024,128]{1,0:T(8,128)S(1)}, f32[1,8192]{1,0:T(1,128)S(1)}, f32[16,128]{1,0:T(8,128)S(1)}) custom-call(bf16[1002,8192]{1,0:T(8,128)(2,1)} %bitcast.9, bf16[64,1024]{1,0:T(8,128)(2,1)} %hidden_hbm.1, s32[1,1002]{1,0:T(1,128)} %bitcast.11, ...), custom_call_target="tpu_custom_call" | custom-call | tf_op jit(solution)/shard_map/prepare/pallas_call | solution.py:85
  19.6 2.3 %collective-permute-done.4.refs_2_ = bf16[32,4096]{1,0:T(8,128)(2,1)S(1)} collective-permute-done((bf16[32,4096]{1,0:T(8,128)(2,1)S(1)}, bf16[32,4096]{1,0:T(8,128)(2,1)S(1)}, u32[]{:S(2)}, u32[]{:S(2)}) %collective-permute-start.4) | collective-permute-done | bytes 262176 | tf_op jit(solution)/shard_map/ppermute | solution.py:29
  22.2 3.0 %collective-permute-start.9 = (bf16[32,4096]{1,0:T(8,128)(2,1)S(1)}, bf16[32,4096]{1,0:T(8,128)(2,1)S(1)}, u32[]{:S(2)}, u32[]{:S(2)}) collective-permute-start(bf16[32,4096]{1,0:T(8,128)(2,1)S(1)} %collective-permute-done.5.refs_3_), channel_id=1, source_target_pairs={{0,96},{1,25},{2,98},{3,27},{4,100},{5,29},{6,102},{7,31},{8,104},... | collective-permute-start | bytes 786440 | tf_op jit(solution)/shard_map/ppermute | solution.py:29
  26.7 2.8 %collective-permute-done.8.refs_6_ = bf16[32,4096]{1,0:T(8,128)(2,1)S(1)} collective-permute-done((bf16[32,4096]{1,0:T(8,128)(2,1)S(1)}, bf16[32,4096]{1,0:T(8,128)(2,1)S(1)}, u32[]{:S(2)}, u32[]{:S(2)}) %collective-permute-start.8) | collective-permute-done | bytes 262176 | tf_op jit(solution)/shard_map/ppermute | solution.py:29
  31.9 2.2 %collective-permute-start.11 = (bf16[128,4096]{1,0:T(8,128)(2,1)S(1)}, bf16[128,4096]{1,0:T(8,128)(2,1)S(1)}, u32[]{:S(2)}, u32[]{:S(2)}) collective-permute-start(bf16[128,4096]{1,0:T(8,128)(2,1)S(1)} %get-tuple-element.59), channel_id=1, source_target_pairs={{0,24},{1,97},{2,26},{3,99},{4,28},{5,101},{6,30},{7,103},{8,0},{9... | collective-permute-start | bytes 3145736 | tf_op jit(solution)/shard_map/ppermute | solution.py:29
  34.1 2.3 %multiply.8.refs_1_ = f32[2,4,1002,256]{3,2,1,0:T(8,128)S(1)} custom-call(bf16[1002,8192]{1,0:T(8,128)(2,1)S(1)} %get-tuple-element.42.refs_0_, bf16[256,4096]{1,0:T(8,128)(2,1)S(1)} %get-tuple-element.54.refs_1_), custom_call_target="tpu_custom_call" | custom-call | flops 2101346304 | bytes 4194304 | tf_op jit(solution)/shard_map/multiply/pallas_call | solution.py:33
  36.5 2.0 %collective-permute-start.15 = (bf16[128,4096]{1,0:T(8,128)(2,1)S(1)}, bf16[128,4096]{1,0:T(8,128)(2,1)S(1)}, u32[]{:S(2)}, u32[]{:S(2)}) collective-permute-start(bf16[128,4096]{1,0:T(8,128)(2,1)S(1)} %get-tuple-element.58), channel_id=1, source_target_pairs={{0,24},{1,97},{2,26},{3,99},{4,28},{5,101},{6,30},{7,103},{8,0},{9... | collective-permute-start | bytes 3145736 | tf_op jit(solution)/shard_map/ppermute | solution.py:29
  38.6 2.3 %multiply.9.refs_1_ = f32[2,4,1002,256]{3,2,1,0:T(8,128)S(1)} custom-call(bf16[1002,8192]{1,0:T(8,128)(2,1)S(1)} %get-tuple-element.42.refs_0_, f32[2,4,1002,256]{3,2,1,0:T(8,128)S(1)} %multiply.8.refs_1_, bf16[256,4096]{1,0:T(8,128)(2,1)S(1)} %collective-permute-done.12.refs_2_), custom_call_target="tpu_custom_call", output_to_operand_aliasing={{}: (1, {})} | custom-call | flops 2101346304 | bytes 4194304 | tf_op jit(solution)/shard_map/multiply/pallas_call | solution.py:33
  40.9 5.9 %collective-permute-done.10.refs_2_ = bf16[128,4096]{1,0:T(8,128)(2,1)S(1)} collective-permute-done((bf16[128,4096]{1,0:T(8,128)(2,1)S(1)}, bf16[128,4096]{1,0:T(8,128)(2,1)S(1)}, u32[]{:S(2)}, u32[]{:S(2)}) %collective-permute-start.10) | collective-permute-done | bytes 1048608 | tf_op jit(solution)/shard_map/ppermute | solution.py:29
  50.1 2.3 %multiply.10.refs_1_ = f32[2,4,1002,256]{3,2,1,0:T(8,128)S(1)} custom-call(bf16[1002,8192]{1,0:T(8,128)(2,1)S(1)} %get-tuple-element.42.refs_0_, f32[2,4,1002,256]{3,2,1,0:T(8,128)S(1)} %multiply.9.refs_1_, bf16[128,4096]{1,0:T(8,128)(2,1)S(1)} %collective-permute-done.10.refs_2_, ...), custom_call_target="tpu_custom_call", output_to_operand_aliasing={{}: (1, {})} | custom-call | flops 2101346304 | bytes 4194304 | tf_op jit(solution)/shard_map/multiply/pallas_call | solution.py:33
  52.5 5.5 %collective-permute-done.15.refs_2_ = bf16[128,4096]{1,0:T(8,128)(2,1)S(1)} collective-permute-done((bf16[128,4096]{1,0:T(8,128)(2,1)S(1)}, bf16[128,4096]{1,0:T(8,128)(2,1)S(1)}, u32[]{:S(2)}, u32[]{:S(2)}) %collective-permute-start.15) | collective-permute-done | bytes 1048608 | tf_op jit(solution)/shard_map/ppermute | solution.py:29
  58.1 2.3 %multiply.11.refs_1_ = f32[2,4,1002,256]{3,2,1,0:T(8,128)S(1)} custom-call(bf16[1002,8192]{1,0:T(8,128)(2,1)S(1)} %get-tuple-element.42.refs_0_, f32[2,4,1002,256]{3,2,1,0:T(8,128)S(1)} %multiply.10.refs_1_, bf16[128,4096]{1,0:T(8,128)(2,1)S(1)} %collective-permute-done.15.refs_2_, ...), custom_call_target="tpu_custom_call", output_to_operand_aliasing={{}: (1, {})} | custom-call | flops 2101346304 | bytes 4194304 | tf_op jit(solution)/shard_map/multiply/pallas_call | solution.py:33
  60.4 8.9 %collective-permute-done.13.refs_2_ = bf16[128,4096]{1,0:T(8,128)(2,1)S(1)} collective-permute-done((bf16[128,4096]{1,0:T(8,128)(2,1)S(1)}, bf16[128,4096]{1,0:T(8,128)(2,1)S(1)}, u32[]{:S(2)}, u32[]{:S(2)}) %collective-permute-start.13) | collective-permute-done | bytes 1048608 | tf_op jit(solution)/shard_map/ppermute | solution.py:29
  70.3 2.3 %multiply.12.refs_1_ = f32[2,4,1002,256]{3,2,1,0:T(8,128)S(1)} custom-call(bf16[1002,8192]{1,0:T(8,128)(2,1)S(1)} %get-tuple-element.42.refs_0_, f32[2,4,1002,256]{3,2,1,0:T(8,128)S(1)} %multiply.11.refs_1_, bf16[128,4096]{1,0:T(8,128)(2,1)S(1)} %collective-permute-done.13.refs_2_, ...), custom_call_target="tpu_custom_call", output_to_operand_aliasing={{}: (1, {})} | custom-call | flops 2101346304 | bytes 4194304 | tf_op jit(solution)/shard_map/multiply/pallas_call | solution.py:33
  72.7 2.3 %multiply.13.refs_1_ = f32[2,4,1002,256]{3,2,1,0:T(8,128)S(1)} custom-call(bf16[1002,8192]{1,0:T(8,128)(2,1)S(1)} %get-tuple-element.42.refs_0_, f32[2,4,1002,256]{3,2,1,0:T(8,128)S(1)} %multiply.12.refs_1_, bf16[128,4096]{1,0:T(8,128)(2,1)S(1)} %collective-permute-done.17.refs_2_, ...), custom_call_target="tpu_custom_call", output_to_operand_aliasing={{}: (1, {})} | custom-call | flops 2101346304 | bytes 4194304 | tf_op jit(solution)/shard_map/multiply/pallas_call | solution.py:33
  75.0 2.3 %multiply.14.refs_1_ = f32[2,4,1002,256]{3,2,1,0:T(8,128)S(1)} custom-call(bf16[1002,8192]{1,0:T(8,128)(2,1)S(1)} %get-tuple-element.42.refs_0_, f32[2,4,1002,256]{3,2,1,0:T(8,128)S(1)} %multiply.13.refs_1_, bf16[128,4096]{1,0:T(8,128)(2,1)S(1)} %collective-permute-done.19.refs_2_, ...), custom_call_target="tpu_custom_call", output_to_operand_aliasing={{}: (1, {})} | custom-call | flops 2101346304 | bytes 4194304 | tf_op jit(solution)/shard_map/multiply/pallas_call | solution.py:33
  77.4 2.3 %multiply.15.products_ref = f32[2,4,1002,256]{3,2,1,0:T(8,128)S(1)} custom-call(bf16[1002,8192]{1,0:T(8,128)(2,1)S(1)} %get-tuple-element.42.refs_0_, f32[2,4,1002,256]{3,2,1,0:T(8,128)S(1)} %multiply.14.refs_1_, bf16[128,4096]{1,0:T(8,128)(2,1)S(1)} %collective-permute-done.21.refs_2_, ...), custom_call_target="tpu_custom_call", output_to_operand_aliasing={{}: (1, {})} | custom-call | flops 2101346304 | bytes 4194304 | tf_op jit(solution)/shard_map/multiply/pallas_call | solution.py:33
  79.7 2.5 %join_halves.1 = (f32[1024,1024]{1,0:T(8,128)S(1)}, f32[40,128]{1,0:T(8,128)S(1)}) custom-call(f32[2,4,1002,256]{3,2,1,0:T(8,128)S(1)} %multiply.15.products_ref, f32[16,128]{1,0:T(8,128)S(1)} %get-tuple-element.66.floors_ref, s32[8,128]{1,0:T(8,128)S(1)} %bitcast.7), custom_call_target="tpu_custom_call" | custom-call | tf_op jit(solution)/shard_map/join_halves/pallas_call | solution.py:33
  88.9 3.0 %collective-permute-done.24.refs_1_ = f32[40,128]{1,0:T(8,128)S(1)} collective-permute-done((f32[40,128]{1,0:T(8,128)S(1)}, f32[40,128]{1,0:T(8,128)S(1)}, u32[]{:S(2)}, u32[]{:S(2)}) %collective-permute-start.24) | collective-permute-done | bytes 20512 | tf_op jit(solution)/shard_map/ppermute | solution.py:29
  92.0 3.6 %collective-permute-start.29 = (f32[40,128]{1,0:T(8,128)S(1)}, f32[40,128]{1,0:T(8,128)S(1)}, u32[]{:S(2)}, u32[]{:S(2)}) collective-permute-start(f32[40,128]{1,0:T(8,128)S(1)} %get-tuple-element.74.refs_0_), channel_id=1, source_target_pairs={{0,16},{1,17},{2,18},{3,19},{4,20},{5,21},{6,22},{7,23},{8,24},{9,... | collective-permute-start | bytes 61448 | tf_op jit(solution)/shard_map/ppermute | solution.py:29
  99.3 2.2 %collective-permute-done.27.refs_1_ = f32[40,128]{1,0:T(8,128)S(1)} collective-permute-done((f32[40,128]{1,0:T(8,128)S(1)}, f32[40,128]{1,0:T(8,128)S(1)}, u32[]{:S(2)}, u32[]{:S(2)}) %collective-permute-start.27) | collective-permute-done | bytes 20512 | tf_op jit(solution)/shard_map/ppermute | solution.py:29
  107.7 2.5 %collective-permute-done.30.refs_1_ = f32[40,128]{1,0:T(8,128)S(1)} collective-permute-done((f32[40,128]{1,0:T(8,128)S(1)}, f32[40,128]{1,0:T(8,128)S(1)}, u32[]{:S(2)}, u32[]{:S(2)}) %collective-permute-start.30) | collective-permute-done | bytes 20512 | tf_op jit(solution)/shard_map/ppermute | solution.py:29
  110.8 2.2 %finish.1 = f32[1002,1024]{1,0:T(8,128)} custom-call(f32[1024,1024]{1,0:T(8,128)S(1)} %get-tuple-element.69.sums_ref, f32[1024,128]{1,0:T(8,128)S(1)} %get-tuple-element.70.floors_ref, f32[24,128]{1,0:T(8,128)S(1)} %get-tuple-element.78.terms_ref), custom_call_target="tpu_custom_call" | custom-call | tf_op jit(solution)/shard_map/finish/pallas_call | solution.py:33
  (65 shorter events, 36.2 us)
Async XLA Ops:
  0.6 11.9 %collective-permute-start = (bf16[64,1024]{1,0:T(8,128)(2,1)}, bf16[64,1024]{1,0:T(8,128)(2,1)S(1)}, u32[]{:S(2)}, u32[]{:S(2)}) collective-permute-start(bf16[64,1024]{1,0:T(8,128)(2,1)} %hidden_hbm.1), channel_id=1, source_target_pairs={{0,2},{1,3},{2,4},{3,5},{4,6},{5,7},{6,0},{7,1},{8,10},{9,11},{10,... | collective-permute-start | bytes 393224 | tf_op jit(solution)/shard_map/ppermute | solution.py:29
  2.4 10.1 %collective-permute-start.2 = (bf16[64,1024]{1,0:T(8,128)(2,1)}, bf16[64,1024]{1,0:T(8,128)(2,1)S(1)}, u32[]{:S(2)}, u32[]{:S(2)}) collective-permute-start(bf16[64,1024]{1,0:T(8,128)(2,1)} %hidden_hbm.1), channel_id=1, source_target_pairs={{0,4},{1,5},{2,6},{3,7},{4,0},{5,1},{6,2},{7,3},{8,12},{9,13},{10,... | collective-permute-start | bytes 393224 | tf_op jit(solution)/shard_map/ppermute | solution.py:29
  5.3 7.2 %collective-permute-start.1 = (bf16[64,1024]{1,0:T(8,128)(2,1)}, bf16[64,1024]{1,0:T(8,128)(2,1)S(1)}, u32[]{:S(2)}, u32[]{:S(2)}) collective-permute-start(bf16[64,1024]{1,0:T(8,128)(2,1)} %hidden_hbm.1), channel_id=1, source_target_pairs={{0,6},{1,7},{2,0},{3,1},{4,2},{5,3},{6,4},{7,5},{8,14},{9,15},{10,... | collective-permute-start | bytes 393224 | tf_op jit(solution)/shard_map/ppermute | solution.py:29
  14.2 7.7 %collective-permute-start.4 = (bf16[32,4096]{1,0:T(8,128)(2,1)S(1)}, bf16[32,4096]{1,0:T(8,128)(2,1)S(1)}, u32[]{:S(2)}, u32[]{:S(2)}) collective-permute-start(bf16[32,4096]{1,0:T(8,128)(2,1)S(1)} %get-tuple-element.50.refs_0_), channel_id=1, source_target_pairs={{0,32},{1,9},{2,34},{3,11},{4,36},{5,13},{6,38},{7,15},{8,40},{9,1... | collective-permute-start | bytes 786440 | tf_op jit(solution)/shard_map/ppermute | solution.py:29
  15.8 6.4 %collective-permute-start.5 = (bf16[32,4096]{1,0:T(8,128)(2,1)S(1)}, bf16[32,4096]{1,0:T(8,128)(2,1)S(1)}, u32[]{:S(2)}, u32[]{:S(2)}) collective-permute-start(bf16[32,4096]{1,0:T(8,128)(2,1)S(1)} %get-tuple-element.51.refs_1_), channel_id=1, source_target_pairs={{0,96},{1,25},{2,98},{3,27},{4,100},{5,29},{6,102},{7,31},{8,104},... | collective-permute-start | bytes 786440 | tf_op jit(solution)/shard_map/ppermute | solution.py:29
  17.5 7.6 %collective-permute-start.6 = (bf16[32,4096]{1,0:T(8,128)(2,1)S(1)}, bf16[32,4096]{1,0:T(8,128)(2,1)S(1)}, u32[]{:S(2)}, u32[]{:S(2)}) collective-permute-start(bf16[32,4096]{1,0:T(8,128)(2,1)S(1)} %get-tuple-element.50.refs_0_), channel_id=1, source_target_pairs={{0,96},{1,25},{2,98},{3,27},{4,100},{5,29},{6,102},{7,31},{8,104},... | collective-permute-start | bytes 786440 | tf_op jit(solution)/shard_map/ppermute | solution.py:29
  19.1 7.6 %collective-permute-start.7 = (bf16[32,4096]{1,0:T(8,128)(2,1)S(1)}, bf16[32,4096]{1,0:T(8,128)(2,1)S(1)}, u32[]{:S(2)}, u32[]{:S(2)}) collective-permute-start(bf16[32,4096]{1,0:T(8,128)(2,1)S(1)} %get-tuple-element.51.refs_1_), channel_id=1, source_target_pairs={{0,32},{1,9},{2,34},{3,11},{4,36},{5,13},{6,38},{7,15},{8,40},{9,1... | collective-permute-start | bytes 786440 | tf_op jit(solution)/shard_map/ppermute | solution.py:29
  21.9 7.6 %collective-permute-start.8 = (bf16[32,4096]{1,0:T(8,128)(2,1)S(1)}, bf16[32,4096]{1,0:T(8,128)(2,1)S(1)}, u32[]{:S(2)}, u32[]{:S(2)}) collective-permute-start(bf16[32,4096]{1,0:T(8,128)(2,1)S(1)} %collective-permute-done.4.refs_2_), channel_id=1, source_target_pairs={{0,32},{1,9},{2,34},{3,11},{4,36},{5,13},{6,38},{7,15},{8,40},{9,1... | collective-permute-start | bytes 786440 | tf_op jit(solution)/shard_map/ppermute | solution.py:29
  22.2 7.3 %collective-permute-start.9 = (bf16[32,4096]{1,0:T(8,128)(2,1)S(1)}, bf16[32,4096]{1,0:T(8,128)(2,1)S(1)}, u32[]{:S(2)}, u32[]{:S(2)}) collective-permute-start(bf16[32,4096]{1,0:T(8,128)(2,1)S(1)} %collective-permute-done.5.refs_3_), channel_id=1, source_target_pairs={{0,96},{1,25},{2,98},{3,27},{4,100},{5,29},{6,102},{7,31},{8,104},... | collective-permute-start | bytes 786440 | tf_op jit(solution)/shard_map/ppermute | solution.py:29
  29.8 8.7 %collective-permute-start.12 = (bf16[256,4096]{1,0:T(8,128)(2,1)S(1)}, bf16[256,4096]{1,0:T(8,128)(2,1)S(1)}, u32[]{:S(2)}, u32[]{:S(2)}) collective-permute-start(bf16[256,4096]{1,0:T(8,128)(2,1)S(1)} %get-tuple-element.54.refs_1_), channel_id=1, source_target_pairs={{0,1},{1,0},{2,3},{3,2},{4,5},{5,4},{6,7},{7,6},{8,9},{9,8},{10,11... | collective-permute-start | bytes 6291464 | tf_op jit(solution)/shard_map/ppermute | solution.py:29
  29.9 16.9 %collective-permute-start.10 = (bf16[128,4096]{1,0:T(8,128)(2,1)S(1)}, bf16[128,4096]{1,0:T(8,128)(2,1)S(1)}, u32[]{:S(2)}, u32[]{:S(2)}) collective-permute-start(bf16[128,4096]{1,0:T(8,128)(2,1)S(1)} %get-tuple-element.58), channel_id=1, source_target_pairs={{0,8},{1,33},{2,10},{3,35},{4,12},{5,37},{6,14},{7,39},{8,16},{9,4... | collective-permute-start | bytes 3145736 | tf_op jit(solution)/shard_map/ppermute | solution.py:29
  31.9 14.9 %collective-permute-start.11 = (bf16[128,4096]{1,0:T(8,128)(2,1)S(1)}, bf16[128,4096]{1,0:T(8,128)(2,1)S(1)}, u32[]{:S(2)}, u32[]{:S(2)}) collective-permute-start(bf16[128,4096]{1,0:T(8,128)(2,1)S(1)} %get-tuple-element.59), channel_id=1, source_target_pairs={{0,24},{1,97},{2,26},{3,99},{4,28},{5,101},{6,30},{7,103},{8,0},{9... | collective-permute-start | bytes 3145736 | tf_op jit(solution)/shard_map/ppermute | solution.py:29
  36.5 21.5 %collective-permute-start.15 = (bf16[128,4096]{1,0:T(8,128)(2,1)S(1)}, bf16[128,4096]{1,0:T(8,128)(2,1)S(1)}, u32[]{:S(2)}, u32[]{:S(2)}) collective-permute-start(bf16[128,4096]{1,0:T(8,128)(2,1)S(1)} %get-tuple-element.58), channel_id=1, source_target_pairs={{0,24},{1,97},{2,26},{3,99},{4,28},{5,101},{6,30},{7,103},{8,0},{9... | collective-permute-start | bytes 3145736 | tf_op jit(solution)/shard_map/ppermute | solution.py:29
  38.5 19.6 %collective-permute-start.16 = (bf16[128,4096]{1,0:T(8,128)(2,1)S(1)}, bf16[128,4096]{1,0:T(8,128)(2,1)S(1)}, u32[]{:S(2)}, u32[]{:S(2)}) collective-permute-start(bf16[128,4096]{1,0:T(8,128)(2,1)S(1)} %get-tuple-element.59), channel_id=1, source_target_pairs={{0,8},{1,33},{2,10},{3,35},{4,12},{5,37},{6,14},{7,39},{8,16},{9,4... | collective-permute-start | bytes 3145736 | tf_op jit(solution)/shard_map/ppermute | solution.py:29
  46.8 22.5 %collective-permute-start.13 = (bf16[128,4096]{1,0:T(8,128)(2,1)S(1)}, bf16[128,4096]{1,0:T(8,128)(2,1)S(1)}, u32[]{:S(2)}, u32[]{:S(2)}) collective-permute-start(bf16[128,4096]{1,0:T(8,128)(2,1)S(1)} %collective-permute-done.10.refs_2_), channel_id=1, source_target_pairs={{0,8},{1,33},{2,10},{3,35},{4,12},{5,37},{6,14},{7,39},{8,16},{9,4... | collective-permute-start | bytes 3145736 | tf_op jit(solution)/shard_map/ppermute | solution.py:29
  48.6 20.7 %collective-permute-start.14 = (bf16[128,4096]{1,0:T(8,128)(2,1)S(1)}, bf16[128,4096]{1,0:T(8,128)(2,1)S(1)}, u32[]{:S(2)}, u32[]{:S(2)}) collective-permute-start(bf16[128,4096]{1,0:T(8,128)(2,1)S(1)} %collective-permute-done.11.refs_3_), channel_id=1, source_target_pairs={{0,24},{1,97},{2,26},{3,99},{4,28},{5,101},{6,30},{7,103},{8,0},{9... | collective-permute-start | bytes 3145736 | tf_op jit(solution)/shard_map/ppermute | solution.py:29
  50.1 19.7 %collective-permute-start.17 = (bf16[128,4096]{1,0:T(8,128)(2,1)S(1)}, bf16[128,4096]{1,0:T(8,128)(2,1)S(1)}, u32[]{:S(2)}, u32[]{:S(2)}) collective-permute-start(bf16[128,4096]{1,0:T(8,128)(2,1)S(1)} %collective-permute-done.10.refs_2_), channel_id=1, source_target_pairs={{0,1},{1,0},{2,3},{3,2},{4,5},{5,4},{6,7},{7,6},{8,9},{9,8},{10,11... | collective-permute-start | bytes 3145736 | tf_op jit(solution)/shard_map/ppermute | solution.py:29
  58.0 14.7 %collective-permute-start.18 = (bf16[128,4096]{1,0:T(8,128)(2,1)S(1)}, bf16[128,4096]{1,0:T(8,128)(2,1)S(1)}, u32[]{:S(2)}, u32[]{:S(2)}) collective-permute-start(bf16[128,4096]{1,0:T(8,128)(2,1)S(1)} %collective-permute-done.11.refs_3_), channel_id=1, source_target_pairs={{0,1},{1,0},{2,3},{3,2},{4,5},{5,4},{6,7},{7,6},{8,9},{9,8},{10,11... | collective-permute-start | bytes 3145736 | tf_op jit(solution)/shard_map/ppermute | solution.py:29
  69.3 5.7 %collective-permute-start.19 = (bf16[128,4096]{1,0:T(8,128)(2,1)S(1)}, bf16[128,4096]{1,0:T(8,128)(2,1)S(1)}, u32[]{:S(2)}, u32[]{:S(2)}) collective-permute-start(bf16[128,4096]{1,0:T(8,128)(2,1)S(1)} %collective-permute-done.15.refs_2_), channel_id=1, source_target_pairs={{0,1},{1,0},{2,3},{3,2},{4,5},{5,4},{6,7},{7,6},{8,9},{9,8},{10,11... | collective-permute-start | bytes 3145736 | tf_op jit(solution)/shard_map/ppermute | solution.py:29
  69.3 5.7 %collective-permute-start.20 = (bf16[128,4096]{1,0:T(8,128)(2,1)S(1)}, bf16[128,4096]{1,0:T(8,128)(2,1)S(1)}, u32[]{:S(2)}, u32[]{:S(2)}) collective-permute-start(bf16[128,4096]{1,0:T(8,128)(2,1)S(1)} %collective-permute-done.16.refs_3_), channel_id=1, source_target_pairs={{0,1},{1,0},{2,3},{3,2},{4,5},{5,4},{6,7},{7,6},{8,9},{9,8},{10,11... | collective-permute-start | bytes 3145736 | tf_op jit(solution)/shard_map/ppermute | solution.py:29
  69.8 7.6 %collective-permute-start.21 = (bf16[128,4096]{1,0:T(8,128)(2,1)S(1)}, bf16[128,4096]{1,0:T(8,128)(2,1)S(1)}, u32[]{:S(2)}, u32[]{:S(2)}) collective-permute-start(bf16[128,4096]{1,0:T(8,128)(2,1)S(1)} %collective-permute-done.13.refs_2_), channel_id=1, source_target_pairs={{0,1},{1,0},{2,3},{3,2},{4,5},{5,4},{6,7},{7,6},{8,9},{9,8},{10,11... | collective-permute-start | bytes 3145736 | tf_op jit(solution)/shard_map/ppermute | solution.py:29
  69.8 7.6 %collective-permute-start.22 = (bf16[128,4096]{1,0:T(8,128)(2,1)S(1)}, bf16[128,4096]{1,0:T(8,128)(2,1)S(1)}, u32[]{:S(2)}, u32[]{:S(2)}) collective-permute-start(bf16[128,4096]{1,0:T(8,128)(2,1)S(1)} %collective-permute-done.14.refs_3_), channel_id=1, source_target_pairs={{0,1},{1,0},{2,3},{3,2},{4,5},{5,4},{6,7},{7,6},{8,9},{9,8},{10,11... | collective-permute-start | bytes 3145736 | tf_op jit(solution)/shard_map/ppermute | solution.py:29
  92.0 5.6 %collective-permute-start.29 = (f32[40,128]{1,0:T(8,128)S(1)}, f32[40,128]{1,0:T(8,128)S(1)}, u32[]{:S(2)}, u32[]{:S(2)}) collective-permute-start(f32[40,128]{1,0:T(8,128)S(1)} %get-tuple-element.74.refs_0_), channel_id=1, source_target_pairs={{0,16},{1,17},{2,18},{3,19},{4,20},{5,21},{6,22},{7,23},{8,24},{9,... | collective-permute-start | bytes 61448 | tf_op jit(solution)/shard_map/ppermute | solution.py:29
  101.6 5.6 %collective-permute-start.32 = (f32[40,128]{1,0:T(8,128)S(1)}, f32[40,128]{1,0:T(8,128)S(1)}, u32[]{:S(2)}, u32[]{:S(2)}) collective-permute-start(f32[40,128]{1,0:T(8,128)S(1)} %get-tuple-element.76.refs_0_), channel_id=1, source_target_pairs={{0,64},{1,65},{2,66},{3,67},{4,68},{5,69},{6,70},{7,71},{8,72},{9,... | collective-permute-start | bytes 61448 | tf_op jit(solution)/shard_map/ppermute | solution.py:29
  (11 other events, 67.6 us)

commit v5 on v4

--- a/solution.py
+++ b/solution.py
@@ -19,13 +19,14 @@
     return lax.rem(lax.div(index, STRIDES[axis]), SIZES[axis])
 
 
-def shift(value, axis, hops):
+def shift(value, axis, hops, cross=False):
     pairs = []
     for source in range(128):
         name = axis[source % len(axis)]
         size, stride = SIZES[name], STRIDES[name]
         place = source // stride % size
-        pairs.append((source, source + ((place + hops) % size - place) * stride))
+        target = source + ((place + hops) % size - place) * stride
+        pairs.append((source, target ^ 1 if cross else target))
     return lax.ppermute(value, BOTH, pairs)
 
 
@@ -152,7 +153,7 @@
 def join(axis, stats, before, last=None):
     size = SIZES[axis]
     hops = [0, 1] if size == 2 else [0, 1, 3, 2]
-    pieces = [stats] + [shift(stats, axis, k) for k in hops[1:]]
+    pieces = [stats] + [shift(stats, axis, k, axis != "c") for k in hops[1:]]
 
     def body(*refs):
         piece_refs, rest = refs[:size], refs[size:]

time: 113 us -> 112 us (level); the launches traced: 113 us -> 111 us
  starting transfers between devices: 38.8 us -> 37.5 us
  waiting for transfers between devices: 41.2 us -> 40 us
    ppermute x33, starting transfers between devices: 38.8 us -> 37.5 us  [shift(): return lax.ppermute(value, BOTH, pairs)]
    ppermute x33, waiting for transfers between devices: 41.2 us -> 40 us  [shift(): return lax.ppermute(value, BOTH, pairs)]
where the time goes in v5:
time: 112 us; the launch traced here: 111 us
  waiting for transfers between devices  40 us (36%)
  starting transfers between devices  37.5 us (33%)
  Pallas kernels  32.1 us (29%)
    ppermute x33, waiting for transfers between devices, shift(): return lax.ppermute(value, BOTH, pairs)  40 us
    ppermute x33, starting transfers between devices, shift(): return lax.ppermute(value, BOTH, pairs)  37.5 us
    pallas_call x18, Pallas kernels, call(): pl.pallas_call(body, out_shape=out_shape, in_specs=[VMEM] * len(inputs),...  26.3 us
    pallas_call x1, Pallas kernels, prepare(): pl.pallas_call(body, out_shape=(pltpu.VMEM(weight.shape, jnp.bfloat16), p...  5.87 us
  transfers between devices with their start and end apart: 33, of which 15 were waited for; matrix products, arithmetic and copies ran while one was open for 0% of the time, Pallas kernels for 21%

profile of v5, /device:TPU:0, one launch (start us, length us, event | category | flops | bytes accessed | tf_op | source)
XLA Modules:
  0.0 110.7 jit_solution(558715720449933129)
XLA Ops:
  2.4 2.9 %collective-permute-start.2 = (bf16[64,1024]{1,0:T(8,128)(2,1)}, bf16[64,1024]{1,0:T(8,128)(2,1)S(1)}, u32[]{:S(2)}, u32[]{:S(2)}) collective-permute-start(bf16[64,1024]{1,0:T(8,128)(2,1)} %hidden_hbm.1), channel_id=1, source_target_pairs={{0,4},{1,5},{2,6},{3,7},{4,0},{5,1},{6,2},{7,3},{8,12},{9,13},{10,... | collective-permute-start | bytes 393224 | tf_op jit(solution)/shard_map/ppermute | solution.py:30
  6.6 5.9 %prepare.1 = (bf16[1002,8192]{1,0:T(8,128)(2,1)S(1)}, bf16[64,1024]{1,0:T(8,128)(2,1)S(1)}, f32[1024,128]{1,0:T(8,128)S(1)}, f32[1,8192]{1,0:T(1,128)S(1)}, f32[16,128]{1,0:T(8,128)S(1)}) custom-call(bf16[1002,8192]{1,0:T(8,128)(2,1)} %bitcast.9, bf16[64,1024]{1,0:T(8,128)(2,1)} %hidden_hbm.1, s32[1,1002]{1,0:T(1,128)} %bitcast.11, ...), custom_call_target="tpu_custom_call" | custom-call | tf_op jit(solution)/shard_map/prepare/pallas_call | solution.py:86
  19.6 2.3 %collective-permute-done.4.refs_2_ = bf16[32,4096]{1,0:T(8,128)(2,1)S(1)} collective-permute-done((bf16[32,4096]{1,0:T(8,128)(2,1)S(1)}, bf16[32,4096]{1,0:T(8,128)(2,1)S(1)}, u32[]{:S(2)}, u32[]{:S(2)}) %collective-permute-start.4) | collective-permute-done | bytes 262176 | tf_op jit(solution)/shard_map/ppermute | solution.py:30
  22.2 3.0 %collective-permute-start.9 = (bf16[32,4096]{1,0:T(8,128)(2,1)S(1)}, bf16[32,4096]{1,0:T(8,128)(2,1)S(1)}, u32[]{:S(2)}, u32[]{:S(2)}) collective-permute-start(bf16[32,4096]{1,0:T(8,128)(2,1)S(1)} %collective-permute-done.5.refs_3_), channel_id=1, source_target_pairs={{0,96},{1,25},{2,98},{3,27},{4,100},{5,29},{6,102},{7,31},{8,104},... | collective-permute-start | bytes 786440 | tf_op jit(solution)/shard_map/ppermute | solution.py:30
  26.7 2.8 %collective-permute-done.8.refs_6_ = bf16[32,4096]{1,0:T(8,128)(2,1)S(1)} collective-permute-done((bf16[32,4096]{1,0:T(8,128)(2,1)S(1)}, bf16[32,4096]{1,0:T(8,128)(2,1)S(1)}, u32[]{:S(2)}, u32[]{:S(2)}) %collective-permute-start.8) | collective-permute-done | bytes 262176 | tf_op jit(solution)/shard_map/ppermute | solution.py:30
  31.9 2.2 %collective-permute-start.11 = (bf16[128,4096]{1,0:T(8,128)(2,1)S(1)}, bf16[128,4096]{1,0:T(8,128)(2,1)S(1)}, u32[]{:S(2)}, u32[]{:S(2)}) collective-permute-start(bf16[128,4096]{1,0:T(8,128)(2,1)S(1)} %get-tuple-element.59), channel_id=1, source_target_pairs={{0,24},{1,97},{2,26},{3,99},{4,28},{5,101},{6,30},{7,103},{8,0},{9... | collective-permute-start | bytes 3145736 | tf_op jit(solution)/shard_map/ppermute | solution.py:30
  34.1 2.3 %multiply.8.refs_1_ = f32[2,4,1002,256]{3,2,1,0:T(8,128)S(1)} custom-call(bf16[1002,8192]{1,0:T(8,128)(2,1)S(1)} %get-tuple-element.42.refs_0_, bf16[256,4096]{1,0:T(8,128)(2,1)S(1)} %get-tuple-element.54.refs_1_), custom_call_target="tpu_custom_call" | custom-call | flops 2101346304 | bytes 4194304 | tf_op jit(solution)/shard_map/multiply/pallas_call | solution.py:34
  36.5 2.0 %collective-permute-start.15 = (bf16[128,4096]{1,0:T(8,128)(2,1)S(1)}, bf16[128,4096]{1,0:T(8,128)(2,1)S(1)}, u32[]{:S(2)}, u32[]{:S(2)}) collective-permute-start(bf16[128,4096]{1,0:T(8,128)(2,1)S(1)} %get-tuple-element.58), channel_id=1, source_target_pairs={{0,24},{1,97},{2,26},{3,99},{4,28},{5,101},{6,30},{7,103},{8,0},{9... | collective-permute-start | bytes 3145736 | tf_op jit(solution)/shard_map/ppermute | solution.py:30
  38.6 2.3 %multiply.9.refs_1_ = f32[2,4,1002,256]{3,2,1,0:T(8,128)S(1)} custom-call(bf16[1002,8192]{1,0:T(8,128)(2,1)S(1)} %get-tuple-element.42.refs_0_, f32[2,4,1002,256]{3,2,1,0:T(8,128)S(1)} %multiply.8.refs_1_, bf16[256,4096]{1,0:T(8,128)(2,1)S(1)} %collective-permute-done.12.refs_2_), custom_call_target="tpu_custom_call", output_to_operand_aliasing={{}: (1, {})} | custom-call | flops 2101346304 | bytes 4194304 | tf_op jit(solution)/shard_map/multiply/pallas_call | solution.py:34
  40.9 5.9 %collective-permute-done.10.refs_2_ = bf16[128,4096]{1,0:T(8,128)(2,1)S(1)} collective-permute-done((bf16[128,4096]{1,0:T(8,128)(2,1)S(1)}, bf16[128,4096]{1,0:T(8,128)(2,1)S(1)}, u32[]{:S(2)}, u32[]{:S(2)}) %collective-permute-start.10) | collective-permute-done | bytes 1048608 | tf_op jit(solution)/shard_map/ppermute | solution.py:30
  50.1 2.3 %multiply.10.refs_1_ = f32[2,4,1002,256]{3,2,1,0:T(8,128)S(1)} custom-call(bf16[1002,8192]{1,0:T(8,128)(2,1)S(1)} %get-tuple-element.42.refs_0_, f32[2,4,1002,256]{3,2,1,0:T(8,128)S(1)} %multiply.9.refs_1_, bf16[128,4096]{1,0:T(8,128)(2,1)S(1)} %collective-permute-done.10.refs_2_, ...), custom_call_target="tpu_custom_call", output_to_operand_aliasing={{}: (1, {})} | custom-call | flops 2101346304 | bytes 4194304 | tf_op jit(solution)/shard_map/multiply/pallas_call | solution.py:34
  52.5 5.5 %collective-permute-done.15.refs_2_ = bf16[128,4096]{1,0:T(8,128)(2,1)S(1)} collective-permute-done((bf16[128,4096]{1,0:T(8,128)(2,1)S(1)}, bf16[128,4096]{1,0:T(8,128)(2,1)S(1)}, u32[]{:S(2)}, u32[]{:S(2)}) %collective-permute-start.15) | collective-permute-done | bytes 1048608 | tf_op jit(solution)/shard_map/ppermute | solution.py:30
  58.1 2.3 %multiply.11.refs_1_ = f32[2,4,1002,256]{3,2,1,0:T(8,128)S(1)} custom-call(bf16[1002,8192]{1,0:T(8,128)(2,1)S(1)} %get-tuple-element.42.refs_0_, f32[2,4,1002,256]{3,2,1,0:T(8,128)S(1)} %multiply.10.refs_1_, bf16[128,4096]{1,0:T(8,128)(2,1)S(1)} %collective-permute-done.15.refs_2_, ...), custom_call_target="tpu_custom_call", output_to_operand_aliasing={{}: (1, {})} | custom-call | flops 2101346304 | bytes 4194304 | tf_op jit(solution)/shard_map/multiply/pallas_call | solution.py:34
  60.4 8.9 %collective-permute-done.13.refs_2_ = bf16[128,4096]{1,0:T(8,128)(2,1)S(1)} collective-permute-done((bf16[128,4096]{1,0:T(8,128)(2,1)S(1)}, bf16[128,4096]{1,0:T(8,128)(2,1)S(1)}, u32[]{:S(2)}, u32[]{:S(2)}) %collective-permute-start.13) | collective-permute-done | bytes 1048608 | tf_op jit(solution)/shard_map/ppermute | solution.py:30
  70.3 2.3 %multiply.12.refs_1_ = f32[2,4,1002,256]{3,2,1,0:T(8,128)S(1)} custom-call(bf16[1002,8192]{1,0:T(8,128)(2,1)S(1)} %get-tuple-element.42.refs_0_, f32[2,4,1002,256]{3,2,1,0:T(8,128)S(1)} %multiply.11.refs_1_, bf16[128,4096]{1,0:T(8,128)(2,1)S(1)} %collective-permute-done.13.refs_2_, ...), custom_call_target="tpu_custom_call", output_to_operand_aliasing={{}: (1, {})} | custom-call | flops 2101346304 | bytes 4194304 | tf_op jit(solution)/shard_map/multiply/pallas_call | solution.py:34
  72.7 2.3 %multiply.13.refs_1_ = f32[2,4,1002,256]{3,2,1,0:T(8,128)S(1)} custom-call(bf16[1002,8192]{1,0:T(8,128)(2,1)S(1)} %get-tuple-element.42.refs_0_, f32[2,4,1002,256]{3,2,1,0:T(8,128)S(1)} %multiply.12.refs_1_, bf16[128,4096]{1,0:T(8,128)(2,1)S(1)} %collective-permute-done.17.refs_2_, ...), custom_call_target="tpu_custom_call", output_to_operand_aliasing={{}: (1, {})} | custom-call | flops 2101346304 | bytes 4194304 | tf_op jit(solution)/shard_map/multiply/pallas_call | solution.py:34
  75.0 2.3 %multiply.14.refs_1_ = f32[2,4,1002,256]{3,2,1,0:T(8,128)S(1)} custom-call(bf16[1002,8192]{1,0:T(8,128)(2,1)S(1)} %get-tuple-element.42.refs_0_, f32[2,4,1002,256]{3,2,1,0:T(8,128)S(1)} %multiply.13.refs_1_, bf16[128,4096]{1,0:T(8,128)(2,1)S(1)} %collective-permute-done.19.refs_2_, ...), custom_call_target="tpu_custom_call", output_to_operand_aliasing={{}: (1, {})} | custom-call | flops 2101346304 | bytes 4194304 | tf_op jit(solution)/shard_map/multiply/pallas_call | solution.py:34
  77.4 2.3 %multiply.15.products_ref = f32[2,4,1002,256]{3,2,1,0:T(8,128)S(1)} custom-call(bf16[1002,8192]{1,0:T(8,128)(2,1)S(1)} %get-tuple-element.42.refs_0_, f32[2,4,1002,256]{3,2,1,0:T(8,128)S(1)} %multiply.14.refs_1_, bf16[128,4096]{1,0:T(8,128)(2,1)S(1)} %collective-permute-done.21.refs_2_, ...), custom_call_target="tpu_custom_call", output_to_operand_aliasing={{}: (1, {})} | custom-call | flops 2101346304 | bytes 4194304 | tf_op jit(solution)/shard_map/multiply/pallas_call | solution.py:34
  79.7 2.5 %join_halves.1 = (f32[1024,1024]{1,0:T(8,128)S(1)}, f32[40,128]{1,0:T(8,128)S(1)}) custom-call(f32[2,4,1002,256]{3,2,1,0:T(8,128)S(1)} %multiply.15.products_ref, f32[16,128]{1,0:T(8,128)S(1)} %get-tuple-element.66.floors_ref, s32[8,128]{1,0:T(8,128)S(1)} %bitcast.7), custom_call_target="tpu_custom_call" | custom-call | tf_op jit(solution)/shard_map/join_halves/pallas_call | solution.py:34
  88.3 2.8 %collective-permute-done.24.refs_1_ = f32[40,128]{1,0:T(8,128)S(1)} collective-permute-done((f32[40,128]{1,0:T(8,128)S(1)}, f32[40,128]{1,0:T(8,128)S(1)}, u32[]{:S(2)}, u32[]{:S(2)}) %collective-permute-start.24) | collective-permute-done | bytes 20512 | tf_op jit(solution)/shard_map/ppermute | solution.py:30
  91.1 3.3 %collective-permute-start.29 = (f32[40,128]{1,0:T(8,128)S(1)}, f32[40,128]{1,0:T(8,128)S(1)}, u32[]{:S(2)}, u32[]{:S(2)}) collective-permute-start(f32[40,128]{1,0:T(8,128)S(1)} %get-tuple-element.74.refs_0_), channel_id=1, source_target_pairs={{0,17},{1,16},{2,19},{3,18},{4,21},{5,20},{6,23},{7,22},{8,25},{9,... | collective-permute-start | bytes 61448 | tf_op jit(solution)/shard_map/ppermute | solution.py:30
  97.7 2.2 %collective-permute-done.27.refs_1_ = f32[40,128]{1,0:T(8,128)S(1)} collective-permute-done((f32[40,128]{1,0:T(8,128)S(1)}, f32[40,128]{1,0:T(8,128)S(1)}, u32[]{:S(2)}, u32[]{:S(2)}) %collective-permute-start.27) | collective-permute-done | bytes 20512 | tf_op jit(solution)/shard_map/ppermute | solution.py:30
  105.5 2.1 %collective-permute-done.30.refs_1_ = f32[40,128]{1,0:T(8,128)S(1)} collective-permute-done((f32[40,128]{1,0:T(8,128)S(1)}, f32[40,128]{1,0:T(8,128)S(1)}, u32[]{:S(2)}, u32[]{:S(2)}) %collective-permute-start.30) | collective-permute-done | bytes 20512 | tf_op jit(solution)/shard_map/ppermute | solution.py:30
  108.3 2.2 %finish.1 = f32[1002,1024]{1,0:T(8,128)} custom-call(f32[1024,1024]{1,0:T(8,128)S(1)} %get-tuple-element.69.sums_ref, f32[1024,128]{1,0:T(8,128)S(1)} %get-tuple-element.70.floors_ref, f32[24,128]{1,0:T(8,128)S(1)} %get-tuple-element.78.terms_ref), custom_call_target="tpu_custom_call" | custom-call | tf_op jit(solution)/shard_map/finish/pallas_call | solution.py:34
  (65 shorter events, 34.6 us)
Async XLA Ops:
  0.6 11.9 %collective-permute-start = (bf16[64,1024]{1,0:T(8,128)(2,1)}, bf16[64,1024]{1,0:T(8,128)(2,1)S(1)}, u32[]{:S(2)}, u32[]{:S(2)}) collective-permute-start(bf16[64,1024]{1,0:T(8,128)(2,1)} %hidden_hbm.1), channel_id=1, source_target_pairs={{0,2},{1,3},{2,4},{3,5},{4,6},{5,7},{6,0},{7,1},{8,10},{9,11},{10,... | collective-permute-start | bytes 393224 | tf_op jit(solution)/shard_map/ppermute | solution.py:30
  2.4 10.1 %collective-permute-start.2 = (bf16[64,1024]{1,0:T(8,128)(2,1)}, bf16[64,1024]{1,0:T(8,128)(2,1)S(1)}, u32[]{:S(2)}, u32[]{:S(2)}) collective-permute-start(bf16[64,1024]{1,0:T(8,128)(2,1)} %hidden_hbm.1), channel_id=1, source_target_pairs={{0,4},{1,5},{2,6},{3,7},{4,0},{5,1},{6,2},{7,3},{8,12},{9,13},{10,... | collective-permute-start | bytes 393224 | tf_op jit(solution)/shard_map/ppermute | solution.py:30
  5.3 7.2 %collective-permute-start.1 = (bf16[64,1024]{1,0:T(8,128)(2,1)}, bf16[64,1024]{1,0:T(8,128)(2,1)S(1)}, u32[]{:S(2)}, u32[]{:S(2)}) collective-permute-start(bf16[64,1024]{1,0:T(8,128)(2,1)} %hidden_hbm.1), channel_id=1, source_target_pairs={{0,6},{1,7},{2,0},{3,1},{4,2},{5,3},{6,4},{7,5},{8,14},{9,15},{10,... | collective-permute-start | bytes 393224 | tf_op jit(solution)/shard_map/ppermute | solution.py:30
  14.2 7.7 %collective-permute-start.4 = (bf16[32,4096]{1,0:T(8,128)(2,1)S(1)}, bf16[32,4096]{1,0:T(8,128)(2,1)S(1)}, u32[]{:S(2)}, u32[]{:S(2)}) collective-permute-start(bf16[32,4096]{1,0:T(8,128)(2,1)S(1)} %get-tuple-element.50.refs_0_), channel_id=1, source_target_pairs={{0,32},{1,9},{2,34},{3,11},{4,36},{5,13},{6,38},{7,15},{8,40},{9,1... | collective-permute-start | bytes 786440 | tf_op jit(solution)/shard_map/ppermute | solution.py:30
  15.8 6.4 %collective-permute-start.5 = (bf16[32,4096]{1,0:T(8,128)(2,1)S(1)}, bf16[32,4096]{1,0:T(8,128)(2,1)S(1)}, u32[]{:S(2)}, u32[]{:S(2)}) collective-permute-start(bf16[32,4096]{1,0:T(8,128)(2,1)S(1)} %get-tuple-element.51.refs_1_), channel_id=1, source_target_pairs={{0,96},{1,25},{2,98},{3,27},{4,100},{5,29},{6,102},{7,31},{8,104},... | collective-permute-start | bytes 786440 | tf_op jit(solution)/shard_map/ppermute | solution.py:30
  17.5 7.6 %collective-permute-start.6 = (bf16[32,4096]{1,0:T(8,128)(2,1)S(1)}, bf16[32,4096]{1,0:T(8,128)(2,1)S(1)}, u32[]{:S(2)}, u32[]{:S(2)}) collective-permute-start(bf16[32,4096]{1,0:T(8,128)(2,1)S(1)} %get-tuple-element.50.refs_0_), channel_id=1, source_target_pairs={{0,96},{1,25},{2,98},{3,27},{4,100},{5,29},{6,102},{7,31},{8,104},... | collective-permute-start | bytes 786440 | tf_op jit(solution)/shard_map/ppermute | solution.py:30
  19.1 7.6 %collective-permute-start.7 = (bf16[32,4096]{1,0:T(8,128)(2,1)S(1)}, bf16[32,4096]{1,0:T(8,128)(2,1)S(1)}, u32[]{:S(2)}, u32[]{:S(2)}) collective-permute-start(bf16[32,4096]{1,0:T(8,128)(2,1)S(1)} %get-tuple-element.51.refs_1_), channel_id=1, source_target_pairs={{0,32},{1,9},{2,34},{3,11},{4,36},{5,13},{6,38},{7,15},{8,40},{9,1... | collective-permute-start | bytes 786440 | tf_op jit(solution)/shard_map/ppermute | solution.py:30
  21.9 7.6 %collective-permute-start.8 = (bf16[32,4096]{1,0:T(8,128)(2,1)S(1)}, bf16[32,4096]{1,0:T(8,128)(2,1)S(1)}, u32[]{:S(2)}, u32[]{:S(2)}) collective-permute-start(bf16[32,4096]{1,0:T(8,128)(2,1)S(1)} %collective-permute-done.4.refs_2_), channel_id=1, source_target_pairs={{0,32},{1,9},{2,34},{3,11},{4,36},{5,13},{6,38},{7,15},{8,40},{9,1... | collective-permute-start | bytes 786440 | tf_op jit(solution)/shard_map/ppermute | solution.py:30
  22.2 7.3 %collective-permute-start.9 = (bf16[32,4096]{1,0:T(8,128)(2,1)S(1)}, bf16[32,4096]{1,0:T(8,128)(2,1)S(1)}, u32[]{:S(2)}, u32[]{:S(2)}) collective-permute-start(bf16[32,4096]{1,0:T(8,128)(2,1)S(1)} %collective-permute-done.5.refs_3_), channel_id=1, source_target_pairs={{0,96},{1,25},{2,98},{3,27},{4,100},{5,29},{6,102},{7,31},{8,104},... | collective-permute-start | bytes 786440 | tf_op jit(solution)/shard_map/ppermute | solution.py:30
  29.8 8.7 %collective-permute-start.12 = (bf16[256,4096]{1,0:T(8,128)(2,1)S(1)}, bf16[256,4096]{1,0:T(8,128)(2,1)S(1)}, u32[]{:S(2)}, u32[]{:S(2)}) collective-permute-start(bf16[256,4096]{1,0:T(8,128)(2,1)S(1)} %get-tuple-element.54.refs_1_), channel_id=1, source_target_pairs={{0,1},{1,0},{2,3},{3,2},{4,5},{5,4},{6,7},{7,6},{8,9},{9,8},{10,11... | collective-permute-start | bytes 6291464 | tf_op jit(solution)/shard_map/ppermute | solution.py:30
  29.9 16.9 %collective-permute-start.10 = (bf16[128,4096]{1,0:T(8,128)(2,1)S(1)}, bf16[128,4096]{1,0:T(8,128)(2,1)S(1)}, u32[]{:S(2)}, u32[]{:S(2)}) collective-permute-start(bf16[128,4096]{1,0:T(8,128)(2,1)S(1)} %get-tuple-element.58), channel_id=1, source_target_pairs={{0,8},{1,33},{2,10},{3,35},{4,12},{5,37},{6,14},{7,39},{8,16},{9,4... | collective-permute-start | bytes 3145736 | tf_op jit(solution)/shard_map/ppermute | solution.py:30
  31.9 14.9 %collective-permute-start.11 = (bf16[128,4096]{1,0:T(8,128)(2,1)S(1)}, bf16[128,4096]{1,0:T(8,128)(2,1)S(1)}, u32[]{:S(2)}, u32[]{:S(2)}) collective-permute-start(bf16[128,4096]{1,0:T(8,128)(2,1)S(1)} %get-tuple-element.59), channel_id=1, source_target_pairs={{0,24},{1,97},{2,26},{3,99},{4,28},{5,101},{6,30},{7,103},{8,0},{9... | collective-permute-start | bytes 3145736 | tf_op jit(solution)/shard_map/ppermute | solution.py:30
  36.5 21.5 %collective-permute-start.15 = (bf16[128,4096]{1,0:T(8,128)(2,1)S(1)}, bf16[128,4096]{1,0:T(8,128)(2,1)S(1)}, u32[]{:S(2)}, u32[]{:S(2)}) collective-permute-start(bf16[128,4096]{1,0:T(8,128)(2,1)S(1)} %get-tuple-element.58), channel_id=1, source_target_pairs={{0,24},{1,97},{2,26},{3,99},{4,28},{5,101},{6,30},{7,103},{8,0},{9... | collective-permute-start | bytes 3145736 | tf_op jit(solution)/shard_map/ppermute | solution.py:30
  38.5 19.6 %collective-permute-start.16 = (bf16[128,4096]{1,0:T(8,128)(2,1)S(1)}, bf16[128,4096]{1,0:T(8,128)(2,1)S(1)}, u32[]{:S(2)}, u32[]{:S(2)}) collective-permute-start(bf16[128,4096]{1,0:T(8,128)(2,1)S(1)} %get-tuple-element.59), channel_id=1, source_target_pairs={{0,8},{1,33},{2,10},{3,35},{4,12},{5,37},{6,14},{7,39},{8,16},{9,4... | collective-permute-start | bytes 3145736 | tf_op jit(solution)/shard_map/ppermute | solution.py:30
  46.8 22.5 %collective-permute-start.13 = (bf16[128,4096]{1,0:T(8,128)(2,1)S(1)}, bf16[128,4096]{1,0:T(8,128)(2,1)S(1)}, u32[]{:S(2)}, u32[]{:S(2)}) collective-permute-start(bf16[128,4096]{1,0:T(8,128)(2,1)S(1)} %collective-permute-done.10.refs_2_), channel_id=1, source_target_pairs={{0,8},{1,33},{2,10},{3,35},{4,12},{5,37},{6,14},{7,39},{8,16},{9,4... | collective-permute-start | bytes 3145736 | tf_op jit(solution)/shard_map/ppermute | solution.py:30
  48.6 20.7 %collective-permute-start.14 = (bf16[128,4096]{1,0:T(8,128)(2,1)S(1)}, bf16[128,4096]{1,0:T(8,128)(2,1)S(1)}, u32[]{:S(2)}, u32[]{:S(2)}) collective-permute-start(bf16[128,4096]{1,0:T(8,128)(2,1)S(1)} %collective-permute-done.11.refs_3_), channel_id=1, source_target_pairs={{0,24},{1,97},{2,26},{3,99},{4,28},{5,101},{6,30},{7,103},{8,0},{9... | collective-permute-start | bytes 3145736 | tf_op jit(solution)/shard_map/ppermute | solution.py:30
  50.1 19.7 %collective-permute-start.17 = (bf16[128,4096]{1,0:T(8,128)(2,1)S(1)}, bf16[128,4096]{1,0:T(8,128)(2,1)S(1)}, u32[]{:S(2)}, u32[]{:S(2)}) collective-permute-start(bf16[128,4096]{1,0:T(8,128)(2,1)S(1)} %collective-permute-done.10.refs_2_), channel_id=1, source_target_pairs={{0,1},{1,0},{2,3},{3,2},{4,5},{5,4},{6,7},{7,6},{8,9},{9,8},{10,11... | collective-permute-start | bytes 3145736 | tf_op jit(solution)/shard_map/ppermute | solution.py:30
  58.0 14.7 %collective-permute-start.18 = (bf16[128,4096]{1,0:T(8,128)(2,1)S(1)}, bf16[128,4096]{1,0:T(8,128)(2,1)S(1)}, u32[]{:S(2)}, u32[]{:S(2)}) collective-permute-start(bf16[128,4096]{1,0:T(8,128)(2,1)S(1)} %collective-permute-done.11.refs_3_), channel_id=1, source_target_pairs={{0,1},{1,0},{2,3},{3,2},{4,5},{5,4},{6,7},{7,6},{8,9},{9,8},{10,11... | collective-permute-start | bytes 3145736 | tf_op jit(solution)/shard_map/ppermute | solution.py:30
  69.3 5.7 %collective-permute-start.19 = (bf16[128,4096]{1,0:T(8,128)(2,1)S(1)}, bf16[128,4096]{1,0:T(8,128)(2,1)S(1)}, u32[]{:S(2)}, u32[]{:S(2)}) collective-permute-start(bf16[128,4096]{1,0:T(8,128)(2,1)S(1)} %collective-permute-done.15.refs_2_), channel_id=1, source_target_pairs={{0,1},{1,0},{2,3},{3,2},{4,5},{5,4},{6,7},{7,6},{8,9},{9,8},{10,11... | collective-permute-start | bytes 3145736 | tf_op jit(solution)/shard_map/ppermute | solution.py:30
  69.3 5.7 %collective-permute-start.20 = (bf16[128,4096]{1,0:T(8,128)(2,1)S(1)}, bf16[128,4096]{1,0:T(8,128)(2,1)S(1)}, u32[]{:S(2)}, u32[]{:S(2)}) collective-permute-start(bf16[128,4096]{1,0:T(8,128)(2,1)S(1)} %collective-permute-done.16.refs_3_), channel_id=1, source_target_pairs={{0,1},{1,0},{2,3},{3,2},{4,5},{5,4},{6,7},{7,6},{8,9},{9,8},{10,11... | collective-permute-start | bytes 3145736 | tf_op jit(solution)/shard_map/ppermute | solution.py:30
  69.8 7.6 %collective-permute-start.21 = (bf16[128,4096]{1,0:T(8,128)(2,1)S(1)}, bf16[128,4096]{1,0:T(8,128)(2,1)S(1)}, u32[]{:S(2)}, u32[]{:S(2)}) collective-permute-start(bf16[128,4096]{1,0:T(8,128)(2,1)S(1)} %collective-permute-done.13.refs_2_), channel_id=1, source_target_pairs={{0,1},{1,0},{2,3},{3,2},{4,5},{5,4},{6,7},{7,6},{8,9},{9,8},{10,11... | collective-permute-start | bytes 3145736 | tf_op jit(solution)/shard_map/ppermute | solution.py:30
  69.8 7.6 %collective-permute-start.22 = (bf16[128,4096]{1,0:T(8,128)(2,1)S(1)}, bf16[128,4096]{1,0:T(8,128)(2,1)S(1)}, u32[]{:S(2)}, u32[]{:S(2)}) collective-permute-start(bf16[128,4096]{1,0:T(8,128)(2,1)S(1)} %collective-permute-done.14.refs_3_), channel_id=1, source_target_pairs={{0,1},{1,0},{2,3},{3,2},{4,5},{5,4},{6,7},{7,6},{8,9},{9,8},{10,11... | collective-permute-start | bytes 3145736 | tf_op jit(solution)/shard_map/ppermute | solution.py:30
  91.1 5.1 %collective-permute-start.29 = (f32[40,128]{1,0:T(8,128)S(1)}, f32[40,128]{1,0:T(8,128)S(1)}, u32[]{:S(2)}, u32[]{:S(2)}) collective-permute-start(f32[40,128]{1,0:T(8,128)S(1)} %get-tuple-element.74.refs_0_), channel_id=1, source_target_pairs={{0,17},{1,16},{2,19},{3,18},{4,21},{5,20},{6,23},{7,22},{8,25},{9,... | collective-permute-start | bytes 61448 | tf_op jit(solution)/shard_map/ppermute | solution.py:30
  99.9 5.4 %collective-permute-start.32 = (f32[40,128]{1,0:T(8,128)S(1)}, f32[40,128]{1,0:T(8,128)S(1)}, u32[]{:S(2)}, u32[]{:S(2)}) collective-permute-start(f32[40,128]{1,0:T(8,128)S(1)} %get-tuple-element.76.refs_0_), channel_id=1, source_target_pairs={{0,65},{1,64},{2,67},{3,66},{4,69},{5,68},{6,71},{7,70},{8,73},{9,... | collective-permute-start | bytes 61448 | tf_op jit(solution)/shard_map/ppermute | solution.py:30
  (11 other events, 61.6 us)

commit v6 on v5

--- a/solution.py
+++ b/solution.py
@@ -354,7 +354,7 @@
     )
 
 
-def multiply(weight, products, pieces, side, axes, keep=False):
+def multiply(weight, products, pieces, side, axes, keep=False, cost=1):
     entries = weight.shape[0]
     arrays = [pieces[0][0]] if pieces[0][0] is pieces[1][0] else [piece[0] for piece in pieces]
     inputs = [weight] + ([] if products is None else [products]) + arrays
@@ -389,8 +389,19 @@
         vmem_mib=6,
         out_specs=(VMEM, VMEM) if keep else VMEM,
         input_output_aliases={} if products is None else {1: 0},
-        cost_estimate=pl.CostEstimate(flops=2 * entries * 4096 * 256, bytes_accessed=4 << 20, transcendentals=0),
-    )
+        cost_estimate=pl.CostEstimate(
+            flops=cost * 2 * entries * 4096 * 256, bytes_accessed=4 << 20, transcendentals=0
+        ),
+    )
+
+
+def beside_each(upper, lower):
+    def body(upper_ref, lower_ref, out_ref):
+        out_ref[0:128, :] = upper_ref[...]
+        out_ref[128:256, :] = lower_ref[...]
+
+    shape = jax.ShapeDtypeStruct((256, 4096), jnp.bfloat16)
+    return call(body, shape, "beside_each", (upper, lower), vmem_mib=2)
 
 
 def coordinate_of(core, axes):
@@ -430,14 +441,14 @@
     products = multiply(weight, products, [(swapped, 0, 0), (swapped, 0, 1)], 1, axes)
     upper_1, lower_3, products = hold((upper_1, lower_3, products))
     upper_2, lower_2 = up(upper_1), down(lower_3)
-    swapped_1 = swap(upper_1), swap(lower_3)
+    pair_1 = swap(beside_each(upper_1, lower_3))
     products = multiply(weight, products, [(upper_1, 1, 0), (lower_3, 3, 1)], 0, axes)
-    products = multiply(weight, products, [(upper_3, 3, 0), (lower_1, 1, 1)], 0, axes)
+    products = multiply(weight, products, [(upper_3, 3, 0), (lower_1, 1, 1)], 0, axes, cost=10)
+    products = multiply(weight, products, [(pair_1, 1, 0), (pair_1, 3, 1)], 1, axes)
     upper_2, lower_2, upper_3, lower_1, products = hold((upper_2, lower_2, upper_3, lower_1, products))
     swapped_3 = swap(upper_3), swap(lower_1)
     swapped_2 = swap(upper_2), swap(lower_2)
     products = multiply(weight, products, [(upper_2, 2, 0), (lower_2, 2, 1)], 0, axes)
-    products = multiply(weight, products, [(swapped_1[0], 1, 0), (swapped_1[1], 3, 1)], 1, axes)
     products = multiply(weight, products, [(swapped_3[0], 3, 0), (swapped_3[1], 1, 1)], 1, axes)
     products = multiply(weight, products, [(swapped_2[0], 2, 0), (swapped_2[1], 2, 1)], 1, axes)
 

time: 112 us -> 111 us (level)
  waiting for transfers between devices: 40 us -> 38.3 us
    ppermute x33 -> x32, waiting for transfers between devices: 40 us -> 38.3 us  [shift(): return lax.ppermute(value, BOTH, pairs)]
    ppermute x33 -> x32, starting transfers between devices: 37.5 us -> 37.9 us  [shift(): return lax.ppermute(value, BOTH, pairs)]
    pallas_call x18 -> x19, Pallas kernels: 26.3 us -> 26.4 us  [call(): pl.pallas_call(body, out_shape=out_shape, in_specs=[VMEM] * len(inputs),...]
  transfers between devices with their start and end apart: 33 -> 32, of which waited for: 15 -> 17; matrix products, arithmetic and copies ran while one was open for 0% -> 0% of each run, Pallas kernels for 21% -> 22%
where the time goes in v6:
time: 111 us; the launch traced here: 110 us
  waiting for transfers between devices  38.3 us (35%)
  starting transfers between devices  37.9 us (34%)
  Pallas kernels  32.3 us (29%)
    ppermute x32, waiting for transfers between devices, shift(): return lax.ppermute(value, BOTH, pairs)  38.3 us
    ppermute x32, starting transfers between devices, shift(): return lax.ppermute(value, BOTH, pairs)  37.9 us
    pallas_call x19, Pallas kernels, call(): pl.pallas_call(body, out_shape=out_shape, in_specs=[VMEM] * len(inputs),...  26.4 us
    pallas_call x1, Pallas kernels, prepare(): pl.pallas_call(body, out_shape=(pltpu.VMEM(weight.shape, jnp.bfloat16), p...  5.87 us
  transfers between devices with their start and end apart: 32, of which 17 were waited for; matrix products, arithmetic and copies ran while one was open for 0% of the time, Pallas kernels for 22%

profile of v6, /device:TPU:0, one launch (start us, length us, event | category | flops | bytes accessed | tf_op | source)
XLA Modules:
  0.0 109.5 jit_solution(1229816815026085643)
XLA Ops:
  2.4 2.9 %collective-permute-start.2 = (bf16[64,1024]{1,0:T(8,128)(2,1)}, bf16[64,1024]{1,0:T(8,128)(2,1)S(1)}, u32[]{:S(2)}, u32[]{:S(2)}) collective-permute-start(bf16[64,1024]{1,0:T(8,128)(2,1)} %hidden_hbm.1), channel_id=1, source_target_pairs={{0,4},{1,5},{2,6},{3,7},{4,0},{5,1},{6,2},{7,3},{8,12},{9,13},{10,... | collective-permute-start | bytes 393224 | tf_op jit(solution)/shard_map/ppermute | solution.py:30
  6.6 5.9 %prepare.1 = (bf16[1002,8192]{1,0:T(8,128)(2,1)S(1)}, bf16[64,1024]{1,0:T(8,128)(2,1)S(1)}, f32[1024,128]{1,0:T(8,128)S(1)}, f32[1,8192]{1,0:T(1,128)S(1)}, f32[16,128]{1,0:T(8,128)S(1)}) custom-call(bf16[1002,8192]{1,0:T(8,128)(2,1)} %bitcast.9, bf16[64,1024]{1,0:T(8,128)(2,1)} %hidden_hbm.1, s32[1,1002]{1,0:T(1,128)} %bitcast.11, ...), custom_call_target="tpu_custom_call" | custom-call | tf_op jit(solution)/shard_map/prepare/pallas_call | solution.py:86
  19.6 2.3 %collective-permute-done.4.refs_2_ = bf16[32,4096]{1,0:T(8,128)(2,1)S(1)} collective-permute-done((bf16[32,4096]{1,0:T(8,128)(2,1)S(1)}, bf16[32,4096]{1,0:T(8,128)(2,1)S(1)}, u32[]{:S(2)}, u32[]{:S(2)}) %collective-permute-start.4) | collective-permute-done | bytes 262176 | tf_op jit(solution)/shard_map/ppermute | solution.py:30
  22.2 3.0 %collective-permute-start.9 = (bf16[32,4096]{1,0:T(8,128)(2,1)S(1)}, bf16[32,4096]{1,0:T(8,128)(2,1)S(1)}, u32[]{:S(2)}, u32[]{:S(2)}) collective-permute-start(bf16[32,4096]{1,0:T(8,128)(2,1)S(1)} %collective-permute-done.5.refs_3_), channel_id=1, source_target_pairs={{0,96},{1,25},{2,98},{3,27},{4,100},{5,29},{6,102},{7,31},{8,104},... | collective-permute-start | bytes 786440 | tf_op jit(solution)/shard_map/ppermute | solution.py:30
  26.7 2.8 %collective-permute-done.8.refs_6_ = bf16[32,4096]{1,0:T(8,128)(2,1)S(1)} collective-permute-done((bf16[32,4096]{1,0:T(8,128)(2,1)S(1)}, bf16[32,4096]{1,0:T(8,128)(2,1)S(1)}, u32[]{:S(2)}, u32[]{:S(2)}) %collective-permute-start.8) | collective-permute-done | bytes 262176 | tf_op jit(solution)/shard_map/ppermute | solution.py:30
  29.9 2.0 %collective-permute-start.10 = (bf16[128,4096]{1,0:T(8,128)(2,1)S(1)}, bf16[128,4096]{1,0:T(8,128)(2,1)S(1)}, u32[]{:S(2)}, u32[]{:S(2)}) collective-permute-start(bf16[128,4096]{1,0:T(8,128)(2,1)S(1)} %get-tuple-element.58), channel_id=1, source_target_pairs={{0,8},{1,33},{2,10},{3,35},{4,12},{5,37},{6,14},{7,39},{8,16},{9,4... | collective-permute-start | bytes 3145736 | tf_op jit(solution)/shard_map/ppermute | solution.py:30
  31.9 2.2 %collective-permute-start.11 = (bf16[128,4096]{1,0:T(8,128)(2,1)S(1)}, bf16[128,4096]{1,0:T(8,128)(2,1)S(1)}, u32[]{:S(2)}, u32[]{:S(2)}) collective-permute-start(bf16[128,4096]{1,0:T(8,128)(2,1)S(1)} %get-tuple-element.59), channel_id=1, source_target_pairs={{0,24},{1,97},{2,26},{3,99},{4,28},{5,101},{6,30},{7,103},{8,0},{9... | collective-permute-start | bytes 3145736 | tf_op jit(solution)/shard_map/ppermute | solution.py:30
  34.1 2.3 %multiply.8.refs_1_ = f32[2,4,1002,256]{3,2,1,0:T(8,128)S(1)} custom-call(bf16[1002,8192]{1,0:T(8,128)(2,1)S(1)} %get-tuple-element.42.refs_0_, bf16[256,4096]{1,0:T(8,128)(2,1)S(1)} %get-tuple-element.54.refs_1_), custom_call_target="tpu_custom_call" | custom-call | flops 2101346304 | bytes 4194304 | tf_op jit(solution)/shard_map/multiply/pallas_call | solution.py:34
  36.5 2.0 %collective-permute-start.15 = (bf16[128,4096]{1,0:T(8,128)(2,1)S(1)}, bf16[128,4096]{1,0:T(8,128)(2,1)S(1)}, u32[]{:S(2)}, u32[]{:S(2)}) collective-permute-start(bf16[128,4096]{1,0:T(8,128)(2,1)S(1)} %get-tuple-element.58), channel_id=1, source_target_pairs={{0,24},{1,97},{2,26},{3,99},{4,28},{5,101},{6,30},{7,103},{8,0},{9... | collective-permute-start | bytes 3145736 | tf_op jit(solution)/shard_map/ppermute | solution.py:30
  38.6 2.3 %multiply.9.refs_1_ = f32[2,4,1002,256]{3,2,1,0:T(8,128)S(1)} custom-call(bf16[1002,8192]{1,0:T(8,128)(2,1)S(1)} %get-tuple-element.42.refs_0_, f32[2,4,1002,256]{3,2,1,0:T(8,128)S(1)} %multiply.8.refs_1_, bf16[256,4096]{1,0:T(8,128)(2,1)S(1)} %collective-permute-done.12.refs_2_), custom_call_target="tpu_custom_call", output_to_operand_aliasing={{}: (1, {})} | custom-call | flops 2101346304 | bytes 4194304 | tf_op jit(solution)/shard_map/multiply/pallas_call | solution.py:34
  40.9 5.9 %collective-permute-done.10.refs_2_.upper_ref = bf16[128,4096]{1,0:T(8,128)(2,1)S(1)} collective-permute-done((bf16[128,4096]{1,0:T(8,128)(2,1)S(1)}, bf16[128,4096]{1,0:T(8,128)(2,1)S(1)}, u32[]{:S(2)}, u32[]{:S(2)}) %collective-permute-start.10) | collective-permute-done | bytes 1048608 | tf_op jit(solution)/shard_map/ppermute | solution.py:30
  50.5 2.3 %multiply.10.refs_1_ = f32[2,4,1002,256]{3,2,1,0:T(8,128)S(1)} custom-call(bf16[1002,8192]{1,0:T(8,128)(2,1)S(1)} %get-tuple-element.42.refs_0_, f32[2,4,1002,256]{3,2,1,0:T(8,128)S(1)} %multiply.9.refs_1_, bf16[128,4096]{1,0:T(8,128)(2,1)S(1)} %collective-permute-done.10.refs_2_.upper_ref, ...), custom_call_target="tpu_custom_call", output_to_operand_aliasing={{}: (1, {})} | custom-call | flops 2101346304 | bytes 4194304 | tf_op jit(solution)/shard_map/multiply/pallas_call | solution.py:34
  52.9 5.1 %collective-permute-done.15.refs_2_ = bf16[128,4096]{1,0:T(8,128)(2,1)S(1)} collective-permute-done((bf16[128,4096]{1,0:T(8,128)(2,1)S(1)}, bf16[128,4096]{1,0:T(8,128)(2,1)S(1)}, u32[]{:S(2)}, u32[]{:S(2)}) %collective-permute-start.15) | collective-permute-done | bytes 1048608 | tf_op jit(solution)/shard_map/ppermute | solution.py:30
  58.1 2.3 %multiply.11.refs_1_ = f32[2,4,1002,256]{3,2,1,0:T(8,128)S(1)} custom-call(bf16[1002,8192]{1,0:T(8,128)(2,1)S(1)} %get-tuple-element.42.refs_0_, f32[2,4,1002,256]{3,2,1,0:T(8,128)S(1)} %multiply.10.refs_1_, bf16[128,4096]{1,0:T(8,128)(2,1)S(1)} %collective-permute-done.15.refs_2_, ...), custom_call_target="tpu_custom_call", output_to_operand_aliasing={{}: (1, {})} | custom-call | flops 21013463040 | bytes 4194304 | tf_op jit(solution)/shard_map/multiply/pallas_call | solution.py:34
  60.4 2.3 %multiply.12.refs_1_ = f32[2,4,1002,256]{3,2,1,0:T(8,128)S(1)} custom-call(bf16[1002,8192]{1,0:T(8,128)(2,1)S(1)} %get-tuple-element.42.refs_0_, f32[2,4,1002,256]{3,2,1,0:T(8,128)S(1)} %multiply.11.refs_1_, bf16[256,4096]{1,0:T(8,128)(2,1)S(1)} %collective-permute-done.17.refs_2_), custom_call_target="tpu_custom_call", output_to_operand_aliasing={{}: (1, {})} | custom-call | flops 2101346304 | bytes 4194304 | tf_op jit(solution)/shard_map/multiply/pallas_call | solution.py:34
  62.7 6.6 %collective-permute-done.13.refs_2_ = bf16[128,4096]{1,0:T(8,128)(2,1)S(1)} collective-permute-done((bf16[128,4096]{1,0:T(8,128)(2,1)S(1)}, bf16[128,4096]{1,0:T(8,128)(2,1)S(1)}, u32[]{:S(2)}, u32[]{:S(2)}) %collective-permute-start.13) | collective-permute-done | bytes 1048608 | tf_op jit(solution)/shard_map/ppermute | solution.py:30
  70.3 2.3 %multiply.13.refs_1_ = f32[2,4,1002,256]{3,2,1,0:T(8,128)S(1)} custom-call(bf16[1002,8192]{1,0:T(8,128)(2,1)S(1)} %get-tuple-element.42.refs_0_, f32[2,4,1002,256]{3,2,1,0:T(8,128)S(1)} %multiply.12.refs_1_, bf16[128,4096]{1,0:T(8,128)(2,1)S(1)} %collective-permute-done.13.refs_2_, ...), custom_call_target="tpu_custom_call", output_to_operand_aliasing={{}: (1, {})} | custom-call | flops 2101346304 | bytes 4194304 | tf_op jit(solution)/shard_map/multiply/pallas_call | solution.py:34
  73.5 2.3 %multiply.14.refs_1_ = f32[2,4,1002,256]{3,2,1,0:T(8,128)S(1)} custom-call(bf16[1002,8192]{1,0:T(8,128)(2,1)S(1)} %get-tuple-element.42.refs_0_, f32[2,4,1002,256]{3,2,1,0:T(8,128)S(1)} %multiply.13.refs_1_, bf16[128,4096]{1,0:T(8,128)(2,1)S(1)} %collective-permute-done.18.refs_2_, ...), custom_call_target="tpu_custom_call", output_to_operand_aliasing={{}: (1, {})} | custom-call | flops 2101346304 | bytes 4194304 | tf_op jit(solution)/shard_map/multiply/pallas_call | solution.py:34
  76.5 2.3 %multiply.15.products_ref = f32[2,4,1002,256]{3,2,1,0:T(8,128)S(1)} custom-call(bf16[1002,8192]{1,0:T(8,128)(2,1)S(1)} %get-tuple-element.42.refs_0_, f32[2,4,1002,256]{3,2,1,0:T(8,128)S(1)} %multiply.14.refs_1_, bf16[128,4096]{1,0:T(8,128)(2,1)S(1)} %collective-permute-done.20.refs_2_, ...), custom_call_target="tpu_custom_call", output_to_operand_aliasing={{}: (1, {})} | custom-call | flops 2101346304 | bytes 4194304 | tf_op jit(solution)/shard_map/multiply/pallas_call | solution.py:34
  78.8 2.5 %join_halves.1 = (f32[1024,1024]{1,0:T(8,128)S(1)}, f32[40,128]{1,0:T(8,128)S(1)}) custom-call(f32[2,4,1002,256]{3,2,1,0:T(8,128)S(1)} %multiply.15.products_ref, f32[16,128]{1,0:T(8,128)S(1)} %get-tuple-element.66.floors_ref, s32[8,128]{1,0:T(8,128)S(1)} %bitcast.7), custom_call_target="tpu_custom_call" | custom-call | tf_op jit(solution)/shard_map/join_halves/pallas_call | solution.py:34
  87.4 2.8 %collective-permute-done.23.refs_1_ = f32[40,128]{1,0:T(8,128)S(1)} collective-permute-done((f32[40,128]{1,0:T(8,128)S(1)}, f32[40,128]{1,0:T(8,128)S(1)}, u32[]{:S(2)}, u32[]{:S(2)}) %collective-permute-start.23) | collective-permute-done | bytes 20512 | tf_op jit(solution)/shard_map/ppermute | solution.py:30
  90.2 3.3 %collective-permute-start.28 = (f32[40,128]{1,0:T(8,128)S(1)}, f32[40,128]{1,0:T(8,128)S(1)}, u32[]{:S(2)}, u32[]{:S(2)}) collective-permute-start(f32[40,128]{1,0:T(8,128)S(1)} %get-tuple-element.74.refs_0_), channel_id=1, source_target_pairs={{0,17},{1,16},{2,19},{3,18},{4,21},{5,20},{6,23},{7,22},{8,25},{9,... | collective-permute-start | bytes 61448 | tf_op jit(solution)/shard_map/ppermute | solution.py:30
  96.7 2.2 %collective-permute-done.26.refs_1_ = f32[40,128]{1,0:T(8,128)S(1)} collective-permute-done((f32[40,128]{1,0:T(8,128)S(1)}, f32[40,128]{1,0:T(8,128)S(1)}, u32[]{:S(2)}, u32[]{:S(2)}) %collective-permute-start.26) | collective-permute-done | bytes 20512 | tf_op jit(solution)/shard_map/ppermute | solution.py:30
  107.2 2.2 %finish.1 = f32[1002,1024]{1,0:T(8,128)} custom-call(f32[1024,1024]{1,0:T(8,128)S(1)} %get-tuple-element.69.sums_ref, f32[1024,128]{1,0:T(8,128)S(1)} %get-tuple-element.70.floors_ref, f32[24,128]{1,0:T(8,128)S(1)} %get-tuple-element.78.terms_ref), custom_call_target="tpu_custom_call" | custom-call | tf_op jit(solution)/shard_map/finish/pallas_call | solution.py:34
  (64 shorter events, 36.3 us)
Async XLA Ops:
  0.6 11.9 %collective-permute-start = (bf16[64,1024]{1,0:T(8,128)(2,1)}, bf16[64,1024]{1,0:T(8,128)(2,1)S(1)}, u32[]{:S(2)}, u32[]{:S(2)}) collective-permute-start(bf16[64,1024]{1,0:T(8,128)(2,1)} %hidden_hbm.1), channel_id=1, source_target_pairs={{0,2},{1,3},{2,4},{3,5},{4,6},{5,7},{6,0},{7,1},{8,10},{9,11},{10,... | collective-permute-start | bytes 393224 | tf_op jit(solution)/shard_map/ppermute | solution.py:30
  2.4 10.1 %collective-permute-start.2 = (bf16[64,1024]{1,0:T(8,128)(2,1)}, bf16[64,1024]{1,0:T(8,128)(2,1)S(1)}, u32[]{:S(2)}, u32[]{:S(2)}) collective-permute-start(bf16[64,1024]{1,0:T(8,128)(2,1)} %hidden_hbm.1), channel_id=1, source_target_pairs={{0,4},{1,5},{2,6},{3,7},{4,0},{5,1},{6,2},{7,3},{8,12},{9,13},{10,... | collective-permute-start | bytes 393224 | tf_op jit(solution)/shard_map/ppermute | solution.py:30
  5.3 7.2 %collective-permute-start.1 = (bf16[64,1024]{1,0:T(8,128)(2,1)}, bf16[64,1024]{1,0:T(8,128)(2,1)S(1)}, u32[]{:S(2)}, u32[]{:S(2)}) collective-permute-start(bf16[64,1024]{1,0:T(8,128)(2,1)} %hidden_hbm.1), channel_id=1, source_target_pairs={{0,6},{1,7},{2,0},{3,1},{4,2},{5,3},{6,4},{7,5},{8,14},{9,15},{10,... | collective-permute-start | bytes 393224 | tf_op jit(solution)/shard_map/ppermute | solution.py:30
  14.2 7.7 %collective-permute-start.4 = (bf16[32,4096]{1,0:T(8,128)(2,1)S(1)}, bf16[32,4096]{1,0:T(8,128)(2,1)S(1)}, u32[]{:S(2)}, u32[]{:S(2)}) collective-permute-start(bf16[32,4096]{1,0:T(8,128)(2,1)S(1)} %get-tuple-element.50.refs_0_), channel_id=1, source_target_pairs={{0,32},{1,9},{2,34},{3,11},{4,36},{5,13},{6,38},{7,15},{8,40},{9,1... | collective-permute-start | bytes 786440 | tf_op jit(solution)/shard_map/ppermute | solution.py:30
  15.8 6.4 %collective-permute-start.5 = (bf16[32,4096]{1,0:T(8,128)(2,1)S(1)}, bf16[32,4096]{1,0:T(8,128)(2,1)S(1)}, u32[]{:S(2)}, u32[]{:S(2)}) collective-permute-start(bf16[32,4096]{1,0:T(8,128)(2,1)S(1)} %get-tuple-element.51.refs_1_), channel_id=1, source_target_pairs={{0,96},{1,25},{2,98},{3,27},{4,100},{5,29},{6,102},{7,31},{8,104},... | collective-permute-start | bytes 786440 | tf_op jit(solution)/shard_map/ppermute | solution.py:30
  17.5 7.6 %collective-permute-start.6 = (bf16[32,4096]{1,0:T(8,128)(2,1)S(1)}, bf16[32,4096]{1,0:T(8,128)(2,1)S(1)}, u32[]{:S(2)}, u32[]{:S(2)}) collective-permute-start(bf16[32,4096]{1,0:T(8,128)(2,1)S(1)} %get-tuple-element.50.refs_0_), channel_id=1, source_target_pairs={{0,96},{1,25},{2,98},{3,27},{4,100},{5,29},{6,102},{7,31},{8,104},... | collective-permute-start | bytes 786440 | tf_op jit(solution)/shard_map/ppermute | solution.py:30
  19.1 7.6 %collective-permute-start.7 = (bf16[32,4096]{1,0:T(8,128)(2,1)S(1)}, bf16[32,4096]{1,0:T(8,128)(2,1)S(1)}, u32[]{:S(2)}, u32[]{:S(2)}) collective-permute-start(bf16[32,4096]{1,0:T(8,128)(2,1)S(1)} %get-tuple-element.51.refs_1_), channel_id=1, source_target_pairs={{0,32},{1,9},{2,34},{3,11},{4,36},{5,13},{6,38},{7,15},{8,40},{9,1... | collective-permute-start | bytes 786440 | tf_op jit(solution)/shard_map/ppermute | solution.py:30
  21.9 7.6 %collective-permute-start.8 = (bf16[32,4096]{1,0:T(8,128)(2,1)S(1)}, bf16[32,4096]{1,0:T(8,128)(2,1)S(1)}, u32[]{:S(2)}, u32[]{:S(2)}) collective-permute-start(bf16[32,4096]{1,0:T(8,128)(2,1)S(1)} %collective-permute-done.4.refs_2_), channel_id=1, source_target_pairs={{0,32},{1,9},{2,34},{3,11},{4,36},{5,13},{6,38},{7,15},{8,40},{9,1... | collective-permute-start | bytes 786440 | tf_op jit(solution)/shard_map/ppermute | solution.py:30
  22.2 7.3 %collective-permute-start.9 = (bf16[32,4096]{1,0:T(8,128)(2,1)S(1)}, bf16[32,4096]{1,0:T(8,128)(2,1)S(1)}, u32[]{:S(2)}, u32[]{:S(2)}) collective-permute-start(bf16[32,4096]{1,0:T(8,128)(2,1)S(1)} %collective-permute-done.5.refs_3_), channel_id=1, source_target_pairs={{0,96},{1,25},{2,98},{3,27},{4,100},{5,29},{6,102},{7,31},{8,104},... | collective-permute-start | bytes 786440 | tf_op jit(solution)/shard_map/ppermute | solution.py:30
  29.8 8.7 %collective-permute-start.12 = (bf16[256,4096]{1,0:T(8,128)(2,1)S(1)}, bf16[256,4096]{1,0:T(8,128)(2,1)S(1)}, u32[]{:S(2)}, u32[]{:S(2)}) collective-permute-start(bf16[256,4096]{1,0:T(8,128)(2,1)S(1)} %get-tuple-element.54.refs_1_), channel_id=1, source_target_pairs={{0,1},{1,0},{2,3},{3,2},{4,5},{5,4},{6,7},{7,6},{8,9},{9,8},{10,11... | collective-permute-start | bytes 6291464 | tf_op jit(solution)/shard_map/ppermute | solution.py:30
  29.9 16.9 %collective-permute-start.10 = (bf16[128,4096]{1,0:T(8,128)(2,1)S(1)}, bf16[128,4096]{1,0:T(8,128)(2,1)S(1)}, u32[]{:S(2)}, u32[]{:S(2)}) collective-permute-start(bf16[128,4096]{1,0:T(8,128)(2,1)S(1)} %get-tuple-element.58), channel_id=1, source_target_pairs={{0,8},{1,33},{2,10},{3,35},{4,12},{5,37},{6,14},{7,39},{8,16},{9,4... | collective-permute-start | bytes 3145736 | tf_op jit(solution)/shard_map/ppermute | solution.py:30
  31.9 14.9 %collective-permute-start.11 = (bf16[128,4096]{1,0:T(8,128)(2,1)S(1)}, bf16[128,4096]{1,0:T(8,128)(2,1)S(1)}, u32[]{:S(2)}, u32[]{:S(2)}) collective-permute-start(bf16[128,4096]{1,0:T(8,128)(2,1)S(1)} %get-tuple-element.59), channel_id=1, source_target_pairs={{0,24},{1,97},{2,26},{3,99},{4,28},{5,101},{6,30},{7,103},{8,0},{9... | collective-permute-start | bytes 3145736 | tf_op jit(solution)/shard_map/ppermute | solution.py:30
  36.5 21.5 %collective-permute-start.15 = (bf16[128,4096]{1,0:T(8,128)(2,1)S(1)}, bf16[128,4096]{1,0:T(8,128)(2,1)S(1)}, u32[]{:S(2)}, u32[]{:S(2)}) collective-permute-start(bf16[128,4096]{1,0:T(8,128)(2,1)S(1)} %get-tuple-element.58), channel_id=1, source_target_pairs={{0,24},{1,97},{2,26},{3,99},{4,28},{5,101},{6,30},{7,103},{8,0},{9... | collective-permute-start | bytes 3145736 | tf_op jit(solution)/shard_map/ppermute | solution.py:30
  38.5 19.6 %collective-permute-start.16 = (bf16[128,4096]{1,0:T(8,128)(2,1)S(1)}, bf16[128,4096]{1,0:T(8,128)(2,1)S(1)}, u32[]{:S(2)}, u32[]{:S(2)}) collective-permute-start(bf16[128,4096]{1,0:T(8,128)(2,1)S(1)} %get-tuple-element.59), channel_id=1, source_target_pairs={{0,8},{1,33},{2,10},{3,35},{4,12},{5,37},{6,14},{7,39},{8,16},{9,4... | collective-permute-start | bytes 3145736 | tf_op jit(solution)/shard_map/ppermute | solution.py:30
  46.8 22.5 %collective-permute-start.13 = (bf16[128,4096]{1,0:T(8,128)(2,1)S(1)}, bf16[128,4096]{1,0:T(8,128)(2,1)S(1)}, u32[]{:S(2)}, u32[]{:S(2)}) collective-permute-start(bf16[128,4096]{1,0:T(8,128)(2,1)S(1)} %collective-permute-done.10.refs_2_.upper_ref), channel_id=1, source_target_pairs={{0,8},{1,33},{2,10},{3,35},{4,12},{5,37},{6,14},{7,39},{8,16},{9,4... | collective-permute-start | bytes 3145736 | tf_op jit(solution)/shard_map/ppermute | solution.py:30
  48.6 20.7 %collective-permute-start.14 = (bf16[128,4096]{1,0:T(8,128)(2,1)S(1)}, bf16[128,4096]{1,0:T(8,128)(2,1)S(1)}, u32[]{:S(2)}, u32[]{:S(2)}) collective-permute-start(bf16[128,4096]{1,0:T(8,128)(2,1)S(1)} %collective-permute-done.11.refs_3_.lower_ref), channel_id=1, source_target_pairs={{0,24},{1,97},{2,26},{3,99},{4,28},{5,101},{6,30},{7,103},{8,0},{9... | collective-permute-start | bytes 3145736 | tf_op jit(solution)/shard_map/ppermute | solution.py:30
  50.3 10.1 %collective-permute-start.17 = (bf16[256,4096]{1,0:T(8,128)(2,1)S(1)}, bf16[256,4096]{1,0:T(8,128)(2,1)S(1)}, u32[]{:S(2)}, u32[]{:S(2)}) collective-permute-start(bf16[256,4096]{1,0:T(8,128)(2,1)S(1)} %beside_each.1), channel_id=1, source_target_pairs={{0,1},{1,0},{2,3},{3,2},{4,5},{5,4},{6,7},{7,6},{8,9},{9,8},{10,11... | collective-permute-start | bytes 6291464 | tf_op jit(solution)/shard_map/ppermute | solution.py:30
  69.8 6.0 %collective-permute-start.20 = (bf16[128,4096]{1,0:T(8,128)(2,1)S(1)}, bf16[128,4096]{1,0:T(8,128)(2,1)S(1)}, u32[]{:S(2)}, u32[]{:S(2)}) collective-permute-start(bf16[128,4096]{1,0:T(8,128)(2,1)S(1)} %collective-permute-done.13.refs_2_), channel_id=1, source_target_pairs={{0,1},{1,0},{2,3},{3,2},{4,5},{5,4},{6,7},{7,6},{8,9},{9,8},{10,11... | collective-permute-start | bytes 3145736 | tf_op jit(solution)/shard_map/ppermute | solution.py:30
  69.8 6.6 %collective-permute-start.21 = (bf16[128,4096]{1,0:T(8,128)(2,1)S(1)}, bf16[128,4096]{1,0:T(8,128)(2,1)S(1)}, u32[]{:S(2)}, u32[]{:S(2)}) collective-permute-start(bf16[128,4096]{1,0:T(8,128)(2,1)S(1)} %collective-permute-done.14.refs_3_), channel_id=1, source_target_pairs={{0,1},{1,0},{2,3},{3,2},{4,5},{5,4},{6,7},{7,6},{8,9},{9,8},{10,11... | collective-permute-start | bytes 3145736 | tf_op jit(solution)/shard_map/ppermute | solution.py:30
  82.6 4.8 %collective-permute-start.25 = (f32[40,128]{1,0:T(8,128)S(1)}, f32[40,128]{1,0:T(8,128)S(1)}, u32[]{:S(2)}, u32[]{:S(2)}) collective-permute-start(f32[40,128]{1,0:T(8,128)S(1)} %get-tuple-element.72.refs_0_), channel_id=1, source_target_pairs={{0,5},{1,4},{2,7},{3,6},{4,1},{5,0},{6,3},{7,2},{8,13},{9,12},{10,... | collective-permute-start | bytes 61448 | tf_op jit(solution)/shard_map/ppermute | solution.py:30
  85.8 4.4 %collective-permute-start.23 = (f32[40,128]{1,0:T(8,128)S(1)}, f32[40,128]{1,0:T(8,128)S(1)}, u32[]{:S(2)}, u32[]{:S(2)}) collective-permute-start(f32[40,128]{1,0:T(8,128)S(1)} %get-tuple-element.72.refs_0_), channel_id=1, source_target_pairs={{0,3},{1,2},{2,5},{3,4},{4,7},{5,6},{6,1},{7,0},{8,11},{9,10},{10,... | collective-permute-start | bytes 61448 | tf_op jit(solution)/shard_map/ppermute | solution.py:30
  90.2 5.1 %collective-permute-start.28 = (f32[40,128]{1,0:T(8,128)S(1)}, f32[40,128]{1,0:T(8,128)S(1)}, u32[]{:S(2)}, u32[]{:S(2)}) collective-permute-start(f32[40,128]{1,0:T(8,128)S(1)} %get-tuple-element.74.refs_0_), channel_id=1, source_target_pairs={{0,17},{1,16},{2,19},{3,18},{4,21},{5,20},{6,23},{7,22},{8,25},{9,... | collective-permute-start | bytes 61448 | tf_op jit(solution)/shard_map/ppermute | solution.py:30
  94.5 4.4 %collective-permute-start.26 = (f32[40,128]{1,0:T(8,128)S(1)}, f32[40,128]{1,0:T(8,128)S(1)}, u32[]{:S(2)}, u32[]{:S(2)}) collective-permute-start(f32[40,128]{1,0:T(8,128)S(1)} %get-tuple-element.74.refs_0_), channel_id=1, source_target_pairs={{0,9},{1,8},{2,11},{3,10},{4,13},{5,12},{6,15},{7,14},{8,17},{9,16... | collective-permute-start | bytes 61448 | tf_op jit(solution)/shard_map/ppermute | solution.py:30
  98.9 5.4 %collective-permute-start.31 = (f32[40,128]{1,0:T(8,128)S(1)}, f32[40,128]{1,0:T(8,128)S(1)}, u32[]{:S(2)}, u32[]{:S(2)}) collective-permute-start(f32[40,128]{1,0:T(8,128)S(1)} %get-tuple-element.76.refs_0_), channel_id=1, source_target_pairs={{0,65},{1,64},{2,67},{3,66},{4,69},{5,68},{6,71},{7,70},{8,73},{9,... | collective-permute-start | bytes 61448 | tf_op jit(solution)/shard_map/ppermute | solution.py:30
  (10 other events, 55.9 us)

commit v7 on v6

--- a/solution.py
+++ b/solution.py
@@ -191,24 +191,24 @@
             after_ref[0:8] = mass_before
             after_ref[8:16] = total_before
         else:
-            own_ref, totals_ref, terms_ref, bits_ref = rest[:4]
+            own_ref, totals_ref, terms_ref = rest[:3]
             tokens = totals_ref[...].astype(jnp.float32)
             free = (tokens - total) / mass
             terms_ref[0:8] = jnp.exp(own_ref[0:8] - peak) * free / tokens
             terms_ref[8:16] = 1.0 / tokens
             terms_ref[16:24] = (total_before + mass_before * free) / tokens
-            bits_ref[...] = -jnp.log2((floor + target * free) / tokens)
+            terms_ref[24:32] = -jnp.log2((floor + target * free) / tokens)
 
     inputs = pieces + ([] if before is None else [before]) + ([] if last is None else list(last))
-    first, second = ((40, 128), (16, 128)) if last is None else ((24, 128), (8, 128))
-    return call(
-        body,
-        (jax.ShapeDtypeStruct(first, jnp.float32), jax.ShapeDtypeStruct(second, jnp.float32)),
+    shapes = ((40, 128), (16, 128)) if last is None else ((32, 128),)
+    return call(
+        body,
+        tuple(jax.ShapeDtypeStruct(shape, jnp.float32) for shape in shapes),
         "join_" + axis,
         inputs,
         vmem_mib=2,
         scratch=[pltpu.VMEM((size, 40, 128), jnp.float32)],
-        out_specs=(VMEM, VMEM),
+        out_specs=(VMEM,) * len(shapes),
     )
 
 
@@ -251,8 +251,9 @@
 
 
 def finish(sums, floor_sums, terms, entries):
-    def body(sums_ref, floors_ref, terms_ref, out_hbm, out_ref, sems):
-        copies = []
+    def body(sums_ref, floors_ref, terms_ref, out_hbm, bits_hbm, out_ref, sems):
+        copies = [pltpu.make_async_copy(terms_ref.at[24:32], bits_hbm, sems.at[ROWS])]
+        copies[0].start()
         for j in range(ROWS):
             lanes = slice(j * 128, (j + 1) * 128)
             out_ref[:, lanes] = (
@@ -267,12 +268,15 @@
 
     return call(
         body,
-        jax.ShapeDtypeStruct((entries, 1024), jnp.float32),
+        (
+            jax.ShapeDtypeStruct((entries, 1024), jnp.float32),
+            jax.ShapeDtypeStruct((8, 128), jnp.float32),
+        ),
         "finish",
         (sums, floor_sums, terms),
         vmem_mib=8,
-        scratch=[pltpu.VMEM((entries, 1024), jnp.float32), pltpu.SemaphoreType.DMA((ROWS,))],
-        out_specs=pl.BlockSpec(memory_space=pltpu.HBM),
+        scratch=[pltpu.VMEM((entries, 1024), jnp.float32), pltpu.SemaphoreType.DMA((ROWS + 1,))],
+        out_specs=(pl.BlockSpec(memory_space=pltpu.HBM),) * 2,
     )
 
 
@@ -354,7 +358,7 @@
     )
 
 
-def multiply(weight, products, pieces, side, axes, keep=False, cost=1):
+def multiply(weight, products, pieces, side, axes, cost=1):
     entries = weight.shape[0]
     arrays = [pieces[0][0]] if pieces[0][0] is pieces[1][0] else [piece[0] for piece in pieces]
     inputs = [weight] + ([] if products is None else [products]) + arrays
@@ -370,8 +374,6 @@
             far = pl.ds(pl.multiple_of((y * 2 + features) * 1024, 1024), 1024)
             value = [ref[:, y * 1024:(y + 1) * 1024] for ref in token_refs]
             value = value[0] if len(value) == 1 else jnp.concatenate(value, axis=0)
-            if keep:
-                refs[-1][:, y * 1024:(y + 1) * 1024] = value
             product = lax.dot_general(
                 weight_ref[:, far], value, (((1,), (1,)), ((), ())), preferred_element_type=jnp.float32
             )
@@ -383,11 +385,10 @@
     shape = jax.ShapeDtypeStruct((2, 4, entries, 256), jnp.float32)
     return call(
         body,
-        (shape, jax.ShapeDtypeStruct((256, 4096), jnp.bfloat16)) if keep else shape,
+        shape,
         "multiply",
         inputs,
         vmem_mib=6,
-        out_specs=(VMEM, VMEM) if keep else VMEM,
         input_output_aliases={} if products is None else {1: 0},
         cost_estimate=pl.CostEstimate(
             flops=cost * 2 * entries * 4096 * 256, bytes_accessed=4 << 20, transcendentals=0
@@ -457,8 +458,8 @@
     group, before = stats, None
     for axis in ("c", "y", "z"):
         group, before = join(axis, group, before)
-    terms, bits = join("x", group, before, last=(stats, totals.reshape(8, 128)))
-    cumulative = finish(sums, floor_sums, terms, entries)
+    (terms,) = join("x", group, before, last=(stats, totals.reshape(8, 128)))
+    cumulative, bits = finish(sums, floor_sums, terms, entries)
     return cumulative.T, bits.reshape(1024)
 
 

time: 111 us -> 110 us (level)
  no operation moved by 1% of the time
where the time goes in v7:
time: 110 us; the launch traced here: 109 us
  waiting for transfers between devices  38.3 us (35%)
  starting transfers between devices  37.9 us (34%)
  Pallas kernels  31.5 us (29%)
    ppermute x32, waiting for transfers between devices, shift(): return lax.ppermute(value, BOTH, pairs)  38.3 us
    ppermute x32, starting transfers between devices, shift(): return lax.ppermute(value, BOTH, pairs)  37.9 us
    pallas_call x19, Pallas kernels, call(): pl.pallas_call(body, out_shape=out_shape, in_specs=[VMEM] * len(inputs),...  25.7 us
    pallas_call x1, Pallas kernels, prepare(): pl.pallas_call(body, out_shape=(pltpu.VMEM(weight.shape, jnp.bfloat16), p...  5.87 us
  transfers between devices with their start and end apart: 32, of which 17 were waited for; matrix products, arithmetic and copies ran while one was open for 0% of the time, Pallas kernels for 22%

profile of v7, /device:TPU:0, one launch (start us, length us, event | category | flops | bytes accessed | tf_op | source)
XLA Modules:
  0.0 108.8 jit_solution(12964557521589853066)
XLA Ops:
  2.4 2.9 %collective-permute-start.2 = (bf16[64,1024]{1,0:T(8,128)(2,1)}, bf16[64,1024]{1,0:T(8,128)(2,1)S(1)}, u32[]{:S(2)}, u32[]{:S(2)}) collective-permute-start(bf16[64,1024]{1,0:T(8,128)(2,1)} %hidden_hbm.1), channel_id=1, source_target_pairs={{0,4},{1,5},{2,6},{3,7},{4,0},{5,1},{6,2},{7,3},{8,12},{9,13},{10,... | collective-permute-start | bytes 393224 | tf_op jit(solution)/shard_map/ppermute | solution.py:30
  6.6 5.9 %prepare.1 = (bf16[1002,8192]{1,0:T(8,128)(2,1)S(1)}, bf16[64,1024]{1,0:T(8,128)(2,1)S(1)}, f32[1024,128]{1,0:T(8,128)S(1)}, f32[1,8192]{1,0:T(1,128)S(1)}, f32[16,128]{1,0:T(8,128)S(1)}) custom-call(bf16[1002,8192]{1,0:T(8,128)(2,1)} %bitcast.9, bf16[64,1024]{1,0:T(8,128)(2,1)} %hidden_hbm.1, s32[1,1002]{1,0:T(1,128)} %bitcast.10, ...), custom_call_target="tpu_custom_call" | custom-call | tf_op jit(solution)/shard_map/prepare/pallas_call | solution.py:86
  19.6 2.3 %collective-permute-done.4.refs_2_ = bf16[32,4096]{1,0:T(8,128)(2,1)S(1)} collective-permute-done((bf16[32,4096]{1,0:T(8,128)(2,1)S(1)}, bf16[32,4096]{1,0:T(8,128)(2,1)S(1)}, u32[]{:S(2)}, u32[]{:S(2)}) %collective-permute-start.4) | collective-permute-done | bytes 262176 | tf_op jit(solution)/shard_map/ppermute | solution.py:30
  22.2 3.0 %collective-permute-start.9 = (bf16[32,4096]{1,0:T(8,128)(2,1)S(1)}, bf16[32,4096]{1,0:T(8,128)(2,1)S(1)}, u32[]{:S(2)}, u32[]{:S(2)}) collective-permute-start(bf16[32,4096]{1,0:T(8,128)(2,1)S(1)} %collective-permute-done.5.refs_3_), channel_id=1, source_target_pairs={{0,96},{1,25},{2,98},{3,27},{4,100},{5,29},{6,102},{7,31},{8,104},... | collective-permute-start | bytes 786440 | tf_op jit(solution)/shard_map/ppermute | solution.py:30
  26.7 2.8 %collective-permute-done.8.refs_6_ = bf16[32,4096]{1,0:T(8,128)(2,1)S(1)} collective-permute-done((bf16[32,4096]{1,0:T(8,128)(2,1)S(1)}, bf16[32,4096]{1,0:T(8,128)(2,1)S(1)}, u32[]{:S(2)}, u32[]{:S(2)}) %collective-permute-start.8) | collective-permute-done | bytes 262176 | tf_op jit(solution)/shard_map/ppermute | solution.py:30
  29.9 2.0 %collective-permute-start.10 = (bf16[128,4096]{1,0:T(8,128)(2,1)S(1)}, bf16[128,4096]{1,0:T(8,128)(2,1)S(1)}, u32[]{:S(2)}, u32[]{:S(2)}) collective-permute-start(bf16[128,4096]{1,0:T(8,128)(2,1)S(1)} %get-tuple-element.58), channel_id=1, source_target_pairs={{0,8},{1,33},{2,10},{3,35},{4,12},{5,37},{6,14},{7,39},{8,16},{9,4... | collective-permute-start | bytes 3145736 | tf_op jit(solution)/shard_map/ppermute | solution.py:30
  31.9 2.2 %collective-permute-start.11 = (bf16[128,4096]{1,0:T(8,128)(2,1)S(1)}, bf16[128,4096]{1,0:T(8,128)(2,1)S(1)}, u32[]{:S(2)}, u32[]{:S(2)}) collective-permute-start(bf16[128,4096]{1,0:T(8,128)(2,1)S(1)} %get-tuple-element.59), channel_id=1, source_target_pairs={{0,24},{1,97},{2,26},{3,99},{4,28},{5,101},{6,30},{7,103},{8,0},{9... | collective-permute-start | bytes 3145736 | tf_op jit(solution)/shard_map/ppermute | solution.py:30
  34.1 2.3 %multiply.8.refs_1_ = f32[2,4,1002,256]{3,2,1,0:T(8,128)S(1)} custom-call(bf16[1002,8192]{1,0:T(8,128)(2,1)S(1)} %get-tuple-element.42.refs_0_, bf16[256,4096]{1,0:T(8,128)(2,1)S(1)} %get-tuple-element.54.refs_1_), custom_call_target="tpu_custom_call" | custom-call | flops 2101346304 | bytes 4194304 | tf_op jit(solution)/shard_map/multiply/pallas_call | solution.py:34
  36.5 2.0 %collective-permute-start.15 = (bf16[128,4096]{1,0:T(8,128)(2,1)S(1)}, bf16[128,4096]{1,0:T(8,128)(2,1)S(1)}, u32[]{:S(2)}, u32[]{:S(2)}) collective-permute-start(bf16[128,4096]{1,0:T(8,128)(2,1)S(1)} %get-tuple-element.58), channel_id=1, source_target_pairs={{0,24},{1,97},{2,26},{3,99},{4,28},{5,101},{6,30},{7,103},{8,0},{9... | collective-permute-start | bytes 3145736 | tf_op jit(solution)/shard_map/ppermute | solution.py:30
  38.6 2.3 %multiply.9.refs_1_ = f32[2,4,1002,256]{3,2,1,0:T(8,128)S(1)} custom-call(bf16[1002,8192]{1,0:T(8,128)(2,1)S(1)} %get-tuple-element.42.refs_0_, f32[2,4,1002,256]{3,2,1,0:T(8,128)S(1)} %multiply.8.refs_1_, bf16[256,4096]{1,0:T(8,128)(2,1)S(1)} %collective-permute-done.12.refs_2_), custom_call_target="tpu_custom_call", output_to_operand_aliasing={{}: (1, {})} | custom-call | flops 2101346304 | bytes 4194304 | tf_op jit(solution)/shard_map/multiply/pallas_call | solution.py:34
  40.9 5.9 %collective-permute-done.10.refs_2_.upper_ref = bf16[128,4096]{1,0:T(8,128)(2,1)S(1)} collective-permute-done((bf16[128,4096]{1,0:T(8,128)(2,1)S(1)}, bf16[128,4096]{1,0:T(8,128)(2,1)S(1)}, u32[]{:S(2)}, u32[]{:S(2)}) %collective-permute-start.10) | collective-permute-done | bytes 1048608 | tf_op jit(solution)/shard_map/ppermute | solution.py:30
  50.5 2.3 %multiply.10.refs_1_ = f32[2,4,1002,256]{3,2,1,0:T(8,128)S(1)} custom-call(bf16[1002,8192]{1,0:T(8,128)(2,1)S(1)} %get-tuple-element.42.refs_0_, f32[2,4,1002,256]{3,2,1,0:T(8,128)S(1)} %multiply.9.refs_1_, bf16[128,4096]{1,0:T(8,128)(2,1)S(1)} %collective-permute-done.10.refs_2_.upper_ref, ...), custom_call_target="tpu_custom_call", output_to_operand_aliasing={{}: (1, {})} | custom-call | flops 2101346304 | bytes 4194304 | tf_op jit(solution)/shard_map/multiply/pallas_call | solution.py:34
  52.9 5.1 %collective-permute-done.15.refs_2_ = bf16[128,4096]{1,0:T(8,128)(2,1)S(1)} collective-permute-done((bf16[128,4096]{1,0:T(8,128)(2,1)S(1)}, bf16[128,4096]{1,0:T(8,128)(2,1)S(1)}, u32[]{:S(2)}, u32[]{:S(2)}) %collective-permute-start.15) | collective-permute-done | bytes 1048608 | tf_op jit(solution)/shard_map/ppermute | solution.py:30
  58.1 2.3 %multiply.11.refs_1_ = f32[2,4,1002,256]{3,2,1,0:T(8,128)S(1)} custom-call(bf16[1002,8192]{1,0:T(8,128)(2,1)S(1)} %get-tuple-element.42.refs_0_, f32[2,4,1002,256]{3,2,1,0:T(8,128)S(1)} %multiply.10.refs_1_, bf16[128,4096]{1,0:T(8,128)(2,1)S(1)} %collective-permute-done.15.refs_2_, ...), custom_call_target="tpu_custom_call", output_to_operand_aliasing={{}: (1, {})} | custom-call | flops 21013463040 | bytes 4194304 | tf_op jit(solution)/shard_map/multiply/pallas_call | solution.py:34
  60.4 2.3 %multiply.12.refs_1_ = f32[2,4,1002,256]{3,2,1,0:T(8,128)S(1)} custom-call(bf16[1002,8192]{1,0:T(8,128)(2,1)S(1)} %get-tuple-element.42.refs_0_, f32[2,4,1002,256]{3,2,1,0:T(8,128)S(1)} %multiply.11.refs_1_, bf16[256,4096]{1,0:T(8,128)(2,1)S(1)} %collective-permute-done.17.refs_2_), custom_call_target="tpu_custom_call", output_to_operand_aliasing={{}: (1, {})} | custom-call | flops 2101346304 | bytes 4194304 | tf_op jit(solution)/shard_map/multiply/pallas_call | solution.py:34
  62.7 6.6 %collective-permute-done.13.refs_2_ = bf16[128,4096]{1,0:T(8,128)(2,1)S(1)} collective-permute-done((bf16[128,4096]{1,0:T(8,128)(2,1)S(1)}, bf16[128,4096]{1,0:T(8,128)(2,1)S(1)}, u32[]{:S(2)}, u32[]{:S(2)}) %collective-permute-start.13) | collective-permute-done | bytes 1048608 | tf_op jit(solution)/shard_map/ppermute | solution.py:30
  70.3 2.3 %multiply.13.refs_1_ = f32[2,4,1002,256]{3,2,1,0:T(8,128)S(1)} custom-call(bf16[1002,8192]{1,0:T(8,128)(2,1)S(1)} %get-tuple-element.42.refs_0_, f32[2,4,1002,256]{3,2,1,0:T(8,128)S(1)} %multiply.12.refs_1_, bf16[128,4096]{1,0:T(8,128)(2,1)S(1)} %collective-permute-done.13.refs_2_, ...), custom_call_target="tpu_custom_call", output_to_operand_aliasing={{}: (1, {})} | custom-call | flops 2101346304 | bytes 4194304 | tf_op jit(solution)/shard_map/multiply/pallas_call | solution.py:34
  73.5 2.3 %multiply.14.refs_1_ = f32[2,4,1002,256]{3,2,1,0:T(8,128)S(1)} custom-call(bf16[1002,8192]{1,0:T(8,128)(2,1)S(1)} %get-tuple-element.42.refs_0_, f32[2,4,1002,256]{3,2,1,0:T(8,128)S(1)} %multiply.13.refs_1_, bf16[128,4096]{1,0:T(8,128)(2,1)S(1)} %collective-permute-done.18.refs_2_, ...), custom_call_target="tpu_custom_call", output_to_operand_aliasing={{}: (1, {})} | custom-call | flops 2101346304 | bytes 4194304 | tf_op jit(solution)/shard_map/multiply/pallas_call | solution.py:34
  76.5 2.3 %multiply.15.products_ref = f32[2,4,1002,256]{3,2,1,0:T(8,128)S(1)} custom-call(bf16[1002,8192]{1,0:T(8,128)(2,1)S(1)} %get-tuple-element.42.refs_0_, f32[2,4,1002,256]{3,2,1,0:T(8,128)S(1)} %multiply.14.refs_1_, bf16[128,4096]{1,0:T(8,128)(2,1)S(1)} %collective-permute-done.20.refs_2_, ...), custom_call_target="tpu_custom_call", output_to_operand_aliasing={{}: (1, {})} | custom-call | flops 2101346304 | bytes 4194304 | tf_op jit(solution)/shard_map/multiply/pallas_call | solution.py:34
  78.8 2.4 %join_halves.1 = (f32[1024,1024]{1,0:T(8,128)S(1)}, f32[40,128]{1,0:T(8,128)S(1)}) custom-call(f32[2,4,1002,256]{3,2,1,0:T(8,128)S(1)} %multiply.15.products_ref, f32[16,128]{1,0:T(8,128)S(1)} %get-tuple-element.66.floors_ref, s32[8,128]{1,0:T(8,128)S(1)} %bitcast.7), custom_call_target="tpu_custom_call" | custom-call | tf_op jit(solution)/shard_map/join_halves/pallas_call | solution.py:34
  87.3 2.8 %collective-permute-done.23.refs_1_ = f32[40,128]{1,0:T(8,128)S(1)} collective-permute-done((f32[40,128]{1,0:T(8,128)S(1)}, f32[40,128]{1,0:T(8,128)S(1)}, u32[]{:S(2)}, u32[]{:S(2)}) %collective-permute-start.23) | collective-permute-done | bytes 20512 | tf_op jit(solution)/shard_map/ppermute | solution.py:30
  90.1 3.3 %collective-permute-start.28 = (f32[40,128]{1,0:T(8,128)S(1)}, f32[40,128]{1,0:T(8,128)S(1)}, u32[]{:S(2)}, u32[]{:S(2)}) collective-permute-start(f32[40,128]{1,0:T(8,128)S(1)} %get-tuple-element.74.refs_0_), channel_id=1, source_target_pairs={{0,17},{1,16},{2,19},{3,18},{4,21},{5,20},{6,23},{7,22},{8,25},{9,... | collective-permute-start | bytes 61448 | tf_op jit(solution)/shard_map/ppermute | solution.py:30
  96.6 2.2 %collective-permute-done.26.refs_1_ = f32[40,128]{1,0:T(8,128)S(1)} collective-permute-done((f32[40,128]{1,0:T(8,128)S(1)}, f32[40,128]{1,0:T(8,128)S(1)}, u32[]{:S(2)}, u32[]{:S(2)}) %collective-permute-start.26) | collective-permute-done | bytes 20512 | tf_op jit(solution)/shard_map/ppermute | solution.py:30
  106.5 2.2 %finish.1 = (f32[1002,1024]{1,0:T(8,128)}, f32[8,128]{1,0:T(8,128)}) custom-call(f32[1024,1024]{1,0:T(8,128)S(1)} %get-tuple-element.69.sums_ref, f32[1024,128]{1,0:T(8,128)S(1)} %get-tuple-element.70.floors_ref, f32[32,128]{1,0:T(8,128)S(1)} %join_x.1.terms_ref), custom_call_target="tpu_custom_call" | custom-call | tf_op jit(solution)/shard_map/finish/pallas_call | solution.py:34
  (64 shorter events, 35.7 us)
Async XLA Ops:
  0.6 11.9 %collective-permute-start = (bf16[64,1024]{1,0:T(8,128)(2,1)}, bf16[64,1024]{1,0:T(8,128)(2,1)S(1)}, u32[]{:S(2)}, u32[]{:S(2)}) collective-permute-start(bf16[64,1024]{1,0:T(8,128)(2,1)} %hidden_hbm.1), channel_id=1, source_target_pairs={{0,2},{1,3},{2,4},{3,5},{4,6},{5,7},{6,0},{7,1},{8,10},{9,11},{10,... | collective-permute-start | bytes 393224 | tf_op jit(solution)/shard_map/ppermute | solution.py:30
  2.4 10.1 %collective-permute-start.2 = (bf16[64,1024]{1,0:T(8,128)(2,1)}, bf16[64,1024]{1,0:T(8,128)(2,1)S(1)}, u32[]{:S(2)}, u32[]{:S(2)}) collective-permute-start(bf16[64,1024]{1,0:T(8,128)(2,1)} %hidden_hbm.1), channel_id=1, source_target_pairs={{0,4},{1,5},{2,6},{3,7},{4,0},{5,1},{6,2},{7,3},{8,12},{9,13},{10,... | collective-permute-start | bytes 393224 | tf_op jit(solution)/shard_map/ppermute | solution.py:30
  5.3 7.2 %collective-permute-start.1 = (bf16[64,1024]{1,0:T(8,128)(2,1)}, bf16[64,1024]{1,0:T(8,128)(2,1)S(1)}, u32[]{:S(2)}, u32[]{:S(2)}) collective-permute-start(bf16[64,1024]{1,0:T(8,128)(2,1)} %hidden_hbm.1), channel_id=1, source_target_pairs={{0,6},{1,7},{2,0},{3,1},{4,2},{5,3},{6,4},{7,5},{8,14},{9,15},{10,... | collective-permute-start | bytes 393224 | tf_op jit(solution)/shard_map/ppermute | solution.py:30
  14.2 7.7 %collective-permute-start.4 = (bf16[32,4096]{1,0:T(8,128)(2,1)S(1)}, bf16[32,4096]{1,0:T(8,128)(2,1)S(1)}, u32[]{:S(2)}, u32[]{:S(2)}) collective-permute-start(bf16[32,4096]{1,0:T(8,128)(2,1)S(1)} %get-tuple-element.50.refs_0_), channel_id=1, source_target_pairs={{0,32},{1,9},{2,34},{3,11},{4,36},{5,13},{6,38},{7,15},{8,40},{9,1... | collective-permute-start | bytes 786440 | tf_op jit(solution)/shard_map/ppermute | solution.py:30
  15.8 6.4 %collective-permute-start.5 = (bf16[32,4096]{1,0:T(8,128)(2,1)S(1)}, bf16[32,4096]{1,0:T(8,128)(2,1)S(1)}, u32[]{:S(2)}, u32[]{:S(2)}) collective-permute-start(bf16[32,4096]{1,0:T(8,128)(2,1)S(1)} %get-tuple-element.51.refs_1_), channel_id=1, source_target_pairs={{0,96},{1,25},{2,98},{3,27},{4,100},{5,29},{6,102},{7,31},{8,104},... | collective-permute-start | bytes 786440 | tf_op jit(solution)/shard_map/ppermute | solution.py:30
  17.5 7.6 %collective-permute-start.6 = (bf16[32,4096]{1,0:T(8,128)(2,1)S(1)}, bf16[32,4096]{1,0:T(8,128)(2,1)S(1)}, u32[]{:S(2)}, u32[]{:S(2)}) collective-permute-start(bf16[32,4096]{1,0:T(8,128)(2,1)S(1)} %get-tuple-element.50.refs_0_), channel_id=1, source_target_pairs={{0,96},{1,25},{2,98},{3,27},{4,100},{5,29},{6,102},{7,31},{8,104},... | collective-permute-start | bytes 786440 | tf_op jit(solution)/shard_map/ppermute | solution.py:30
  19.1 7.6 %collective-permute-start.7 = (bf16[32,4096]{1,0:T(8,128)(2,1)S(1)}, bf16[32,4096]{1,0:T(8,128)(2,1)S(1)}, u32[]{:S(2)}, u32[]{:S(2)}) collective-permute-start(bf16[32,4096]{1,0:T(8,128)(2,1)S(1)} %get-tuple-element.51.refs_1_), channel_id=1, source_target_pairs={{0,32},{1,9},{2,34},{3,11},{4,36},{5,13},{6,38},{7,15},{8,40},{9,1... | collective-permute-start | bytes 786440 | tf_op jit(solution)/shard_map/ppermute | solution.py:30
  21.9 7.6 %collective-permute-start.8 = (bf16[32,4096]{1,0:T(8,128)(2,1)S(1)}, bf16[32,4096]{1,0:T(8,128)(2,1)S(1)}, u32[]{:S(2)}, u32[]{:S(2)}) collective-permute-start(bf16[32,4096]{1,0:T(8,128)(2,1)S(1)} %collective-permute-done.4.refs_2_), channel_id=1, source_target_pairs={{0,32},{1,9},{2,34},{3,11},{4,36},{5,13},{6,38},{7,15},{8,40},{9,1... | collective-permute-start | bytes 786440 | tf_op jit(solution)/shard_map/ppermute | solution.py:30
  22.2 7.3 %collective-permute-start.9 = (bf16[32,4096]{1,0:T(8,128)(2,1)S(1)}, bf16[32,4096]{1,0:T(8,128)(2,1)S(1)}, u32[]{:S(2)}, u32[]{:S(2)}) collective-permute-start(bf16[32,4096]{1,0:T(8,128)(2,1)S(1)} %collective-permute-done.5.refs_3_), channel_id=1, source_target_pairs={{0,96},{1,25},{2,98},{3,27},{4,100},{5,29},{6,102},{7,31},{8,104},... | collective-permute-start | bytes 786440 | tf_op jit(solution)/shard_map/ppermute | solution.py:30
  29.8 8.7 %collective-permute-start.12 = (bf16[256,4096]{1,0:T(8,128)(2,1)S(1)}, bf16[256,4096]{1,0:T(8,128)(2,1)S(1)}, u32[]{:S(2)}, u32[]{:S(2)}) collective-permute-start(bf16[256,4096]{1,0:T(8,128)(2,1)S(1)} %get-tuple-element.54.refs_1_), channel_id=1, source_target_pairs={{0,1},{1,0},{2,3},{3,2},{4,5},{5,4},{6,7},{7,6},{8,9},{9,8},{10,11... | collective-permute-start | bytes 6291464 | tf_op jit(solution)/shard_map/ppermute | solution.py:30
  29.9 16.9 %collective-permute-start.10 = (bf16[128,4096]{1,0:T(8,128)(2,1)S(1)}, bf16[128,4096]{1,0:T(8,128)(2,1)S(1)}, u32[]{:S(2)}, u32[]{:S(2)}) collective-permute-start(bf16[128,4096]{1,0:T(8,128)(2,1)S(1)} %get-tuple-element.58), channel_id=1, source_target_pairs={{0,8},{1,33},{2,10},{3,35},{4,12},{5,37},{6,14},{7,39},{8,16},{9,4... | collective-permute-start | bytes 3145736 | tf_op jit(solution)/shard_map/ppermute | solution.py:30
  31.9 14.9 %collective-permute-start.11 = (bf16[128,4096]{1,0:T(8,128)(2,1)S(1)}, bf16[128,4096]{1,0:T(8,128)(2,1)S(1)}, u32[]{:S(2)}, u32[]{:S(2)}) collective-permute-start(bf16[128,4096]{1,0:T(8,128)(2,1)S(1)} %get-tuple-element.59), channel_id=1, source_target_pairs={{0,24},{1,97},{2,26},{3,99},{4,28},{5,101},{6,30},{7,103},{8,0},{9... | collective-permute-start | bytes 3145736 | tf_op jit(solution)/shard_map/ppermute | solution.py:30
  36.5 21.5 %collective-permute-start.15 = (bf16[128,4096]{1,0:T(8,128)(2,1)S(1)}, bf16[128,4096]{1,0:T(8,128)(2,1)S(1)}, u32[]{:S(2)}, u32[]{:S(2)}) collective-permute-start(bf16[128,4096]{1,0:T(8,128)(2,1)S(1)} %get-tuple-element.58), channel_id=1, source_target_pairs={{0,24},{1,97},{2,26},{3,99},{4,28},{5,101},{6,30},{7,103},{8,0},{9... | collective-permute-start | bytes 3145736 | tf_op jit(solution)/shard_map/ppermute | solution.py:30
  38.5 19.6 %collective-permute-start.16 = (bf16[128,4096]{1,0:T(8,128)(2,1)S(1)}, bf16[128,4096]{1,0:T(8,128)(2,1)S(1)}, u32[]{:S(2)}, u32[]{:S(2)}) collective-permute-start(bf16[128,4096]{1,0:T(8,128)(2,1)S(1)} %get-tuple-element.59), channel_id=1, source_target_pairs={{0,8},{1,33},{2,10},{3,35},{4,12},{5,37},{6,14},{7,39},{8,16},{9,4... | collective-permute-start | bytes 3145736 | tf_op jit(solution)/shard_map/ppermute | solution.py:30
  46.8 22.5 %collective-permute-start.13 = (bf16[128,4096]{1,0:T(8,128)(2,1)S(1)}, bf16[128,4096]{1,0:T(8,128)(2,1)S(1)}, u32[]{:S(2)}, u32[]{:S(2)}) collective-permute-start(bf16[128,4096]{1,0:T(8,128)(2,1)S(1)} %collective-permute-done.10.refs_2_.upper_ref), channel_id=1, source_target_pairs={{0,8},{1,33},{2,10},{3,35},{4,12},{5,37},{6,14},{7,39},{8,16},{9,4... | collective-permute-start | bytes 3145736 | tf_op jit(solution)/shard_map/ppermute | solution.py:30
  48.6 20.7 %collective-permute-start.14 = (bf16[128,4096]{1,0:T(8,128)(2,1)S(1)}, bf16[128,4096]{1,0:T(8,128)(2,1)S(1)}, u32[]{:S(2)}, u32[]{:S(2)}) collective-permute-start(bf16[128,4096]{1,0:T(8,128)(2,1)S(1)} %collective-permute-done.11.refs_3_.lower_ref), channel_id=1, source_target_pairs={{0,24},{1,97},{2,26},{3,99},{4,28},{5,101},{6,30},{7,103},{8,0},{9... | collective-permute-start | bytes 3145736 | tf_op jit(solution)/shard_map/ppermute | solution.py:30
  50.3 10.1 %collective-permute-start.17 = (bf16[256,4096]{1,0:T(8,128)(2,1)S(1)}, bf16[256,4096]{1,0:T(8,128)(2,1)S(1)}, u32[]{:S(2)}, u32[]{:S(2)}) collective-permute-start(bf16[256,4096]{1,0:T(8,128)(2,1)S(1)} %beside_each.1), channel_id=1, source_target_pairs={{0,1},{1,0},{2,3},{3,2},{4,5},{5,4},{6,7},{7,6},{8,9},{9,8},{10,11... | collective-permute-start | bytes 6291464 | tf_op jit(solution)/shard_map/ppermute | solution.py:30
  69.8 6.0 %collective-permute-start.20 = (bf16[128,4096]{1,0:T(8,128)(2,1)S(1)}, bf16[128,4096]{1,0:T(8,128)(2,1)S(1)}, u32[]{:S(2)}, u32[]{:S(2)}) collective-permute-start(bf16[128,4096]{1,0:T(8,128)(2,1)S(1)} %collective-permute-done.13.refs_2_), channel_id=1, source_target_pairs={{0,1},{1,0},{2,3},{3,2},{4,5},{5,4},{6,7},{7,6},{8,9},{9,8},{10,11... | collective-permute-start | bytes 3145736 | tf_op jit(solution)/shard_map/ppermute | solution.py:30
  69.8 6.6 %collective-permute-start.21 = (bf16[128,4096]{1,0:T(8,128)(2,1)S(1)}, bf16[128,4096]{1,0:T(8,128)(2,1)S(1)}, u32[]{:S(2)}, u32[]{:S(2)}) collective-permute-start(bf16[128,4096]{1,0:T(8,128)(2,1)S(1)} %collective-permute-done.14.refs_3_), channel_id=1, source_target_pairs={{0,1},{1,0},{2,3},{3,2},{4,5},{5,4},{6,7},{7,6},{8,9},{9,8},{10,11... | collective-permute-start | bytes 3145736 | tf_op jit(solution)/shard_map/ppermute | solution.py:30
  82.5 4.8 %collective-permute-start.25 = (f32[40,128]{1,0:T(8,128)S(1)}, f32[40,128]{1,0:T(8,128)S(1)}, u32[]{:S(2)}, u32[]{:S(2)}) collective-permute-start(f32[40,128]{1,0:T(8,128)S(1)} %get-tuple-element.72.refs_0_), channel_id=1, source_target_pairs={{0,5},{1,4},{2,7},{3,6},{4,1},{5,0},{6,3},{7,2},{8,13},{9,12},{10,... | collective-permute-start | bytes 61448 | tf_op jit(solution)/shard_map/ppermute | solution.py:30
  85.6 4.4 %collective-permute-start.23 = (f32[40,128]{1,0:T(8,128)S(1)}, f32[40,128]{1,0:T(8,128)S(1)}, u32[]{:S(2)}, u32[]{:S(2)}) collective-permute-start(f32[40,128]{1,0:T(8,128)S(1)} %get-tuple-element.72.refs_0_), channel_id=1, source_target_pairs={{0,3},{1,2},{2,5},{3,4},{4,7},{5,6},{6,1},{7,0},{8,11},{9,10},{10,... | collective-permute-start | bytes 61448 | tf_op jit(solution)/shard_map/ppermute | solution.py:30
  90.1 5.1 %collective-permute-start.28 = (f32[40,128]{1,0:T(8,128)S(1)}, f32[40,128]{1,0:T(8,128)S(1)}, u32[]{:S(2)}, u32[]{:S(2)}) collective-permute-start(f32[40,128]{1,0:T(8,128)S(1)} %get-tuple-element.74.refs_0_), channel_id=1, source_target_pairs={{0,17},{1,16},{2,19},{3,18},{4,21},{5,20},{6,23},{7,22},{8,25},{9,... | collective-permute-start | bytes 61448 | tf_op jit(solution)/shard_map/ppermute | solution.py:30
  94.4 4.4 %collective-permute-start.26 = (f32[40,128]{1,0:T(8,128)S(1)}, f32[40,128]{1,0:T(8,128)S(1)}, u32[]{:S(2)}, u32[]{:S(2)}) collective-permute-start(f32[40,128]{1,0:T(8,128)S(1)} %get-tuple-element.74.refs_0_), channel_id=1, source_target_pairs={{0,9},{1,8},{2,11},{3,10},{4,13},{5,12},{6,15},{7,14},{8,17},{9,16... | collective-permute-start | bytes 61448 | tf_op jit(solution)/shard_map/ppermute | solution.py:30
  98.8 5.3 %collective-permute-start.31 = (f32[40,128]{1,0:T(8,128)S(1)}, f32[40,128]{1,0:T(8,128)S(1)}, u32[]{:S(2)}, u32[]{:S(2)}) collective-permute-start(f32[40,128]{1,0:T(8,128)S(1)} %get-tuple-element.76.refs_0_), channel_id=1, source_target_pairs={{0,65},{1,64},{2,67},{3,66},{4,69},{5,68},{6,71},{7,70},{8,73},{9,... | collective-permute-start | bytes 61448 | tf_op jit(solution)/shard_map/ppermute | solution.py:30
  (10 other events, 55.7 us)

commit v8 on v7

--- a/solution.py
+++ b/solution.py
@@ -56,7 +56,7 @@
                 (targets_hbm, targets_ref),
                 (gain_hbm, gain_ref),
                 (hidden_hbm, hidden_ref),
-                (weight_hbm, weight_ref),
+                (weight_hbm.at[:, 0:4096], weight_ref),
             ))
         ]
         for copy in copies:
@@ -86,7 +86,7 @@
     return pl.pallas_call(
         body,
         out_shape=(
-            pltpu.VMEM(weight.shape, jnp.bfloat16),
+            pltpu.VMEM((entries, 4096), jnp.bfloat16),
             pltpu.VMEM(hidden.shape, jnp.bfloat16),
             pltpu.VMEM((1024, 128), jnp.float32),
             pltpu.VMEM((1, 8192), jnp.float32),
@@ -104,6 +104,23 @@
         compiler_params=pltpu.CompilerParams(vmem_limit_bytes=2 << 20),
         name="prepare",
     )(*(pltpu.with_memory_space_constraint(operand, pltpu.HBM) for operand in operands))
+
+
+def load(weight):
+    def body(weight_hbm, weight_ref, sem):
+        copy = pltpu.make_async_copy(weight_hbm.at[:, 4096:8192], weight_ref, sem)
+        copy.start()
+        copy.wait()
+
+    return pl.pallas_call(
+        body,
+        out_shape=pltpu.VMEM((weight.shape[0], 4096), jnp.bfloat16),
+        in_specs=[pl.BlockSpec(memory_space=pltpu.HBM)],
+        out_specs=VMEM,
+        scratch_shapes=[pltpu.SemaphoreType.DMA],
+        compiler_params=pltpu.CompilerParams(vmem_limit_bytes=2 << 20),
+        name="load",
+    )(pltpu.with_memory_space_constraint(weight, pltpu.HBM))
 
 
 def first_entry(entries):
@@ -359,23 +376,23 @@
 
 
 def multiply(weight, products, pieces, side, axes, cost=1):
-    entries = weight.shape[0]
+    entries = weight[0].shape[0]
     arrays = [pieces[0][0]] if pieces[0][0] is pieces[1][0] else [piece[0] for piece in pieces]
-    inputs = [weight] + ([] if products is None else [products]) + arrays
+    inputs = list(weight) + ([] if products is None else [products]) + arrays
 
     def body(*refs):
-        weight_ref, out_ref = refs[0], refs[len(inputs)]
+        weight_refs, out_ref = refs[:2], refs[len(inputs)]
         token_refs = refs[len(inputs) - len(arrays):len(inputs)]
         core = lax.rem(lax.axis_index(TENSOR), 2)
         features = core if side == 0 else 1 - core
         mine = coordinate_of(features, axes)
         total = None
         for y in range(4):
-            far = pl.ds(pl.multiple_of((y * 2 + features) * 1024, 1024), 1024)
+            far = pl.ds(pl.multiple_of((y % 2 * 2 + features) * 1024, 1024), 1024)
             value = [ref[:, y * 1024:(y + 1) * 1024] for ref in token_refs]
             value = value[0] if len(value) == 1 else jnp.concatenate(value, axis=0)
             product = lax.dot_general(
-                weight_ref[:, far], value, (((1,), (1,)), ((), ())), preferred_element_type=jnp.float32
+                weight_refs[y // 2][:, far], value, (((1,), (1,)), ((), ())), preferred_element_type=jnp.float32
             )
             total = product if total is None else total + product
         for i, (_, hops, half) in enumerate(pieces):
@@ -389,7 +406,7 @@
         "multiply",
         inputs,
         vmem_mib=6,
-        input_output_aliases={} if products is None else {1: 0},
+        input_output_aliases={} if products is None else {2: 0},
         cost_estimate=pl.CostEstimate(
             flops=cost * 2 * entries * 4096 * 256, bytes_accessed=4 << 20, transcendentals=0
         ),
@@ -415,16 +432,18 @@
     targets = targets.reshape(8, 128)
 
     beside = [shift(hidden, "y", k) for k in (1, 3, 2)]
-    weight, hidden, floors, gain, floor_stats = prepare(
+    first_half, hidden, floors, gain, floor_stats = prepare(
         weight, hidden, floor_counts.reshape(1, entries), norm_gain, targets
     )
-    weight, *beside = lax.optimization_barrier((weight, *beside))
+    first_half, *beside = lax.optimization_barrier((first_half, *beside))
     raw, own = square_sums([hidden] + beside)
     upper, lower = normalize(raw, own, shift(own, "c", 1), gain)
     axes = "xz"
     upper_1, lower_3 = shift(upper, axes, 1), shift(lower, axes, 3)
     upper_3, lower_1 = shift(upper, axes, 3), shift(lower, axes, 1)
     upper_2, lower_2 = shift(upper_1, axes, 1), shift(lower_3, axes, 3)
+    second_half, upper_3, lower_1 = lax.optimization_barrier((load(weight), upper_3, lower_1))
+    weight = first_half, second_half
     pieces = [(0, 0, upper), (1, 0, lower), (0, 1, upper_1), (1, 3, lower_3)]
     pieces += [(0, 3, upper_3), (1, 1, lower_1), (0, 2, upper_2), (1, 2, lower_2)]
     block, upper, lower = stack(pieces, axes)

time: 110 us -> 110 us (level)
  waiting for transfers between devices: 38.3 us -> 35.8 us
    ppermute x32, waiting for transfers between devices: 38.3 us -> 35.8 us  [shift(): return lax.ppermute(value, BOTH, pairs)]
    pallas_call x1 -> x2, Pallas kernels: 5.87 us -> 6.87 us  [the longest x1 3.51 us: prepare(): pl.pallas_call(body, out_shape=(pltpu.VMEM((entries, 4096), jnp.bfloat16)...]
  transfers between devices with their start and end apart: 32 -> 32, of which waited for: 17 -> 18; matrix products, arithmetic and copies ran while one was open for 0% -> 0% of each run, Pallas kernels for 22% -> 23%
where the time goes in v8:
time: 110 us; the launch traced here: 108 us
  starting transfers between devices  38.9 us (35%)
  waiting for transfers between devices  35.8 us (33%)
  Pallas kernels  32.5 us (30%)
    ppermute x32, starting transfers between devices, shift(): return lax.ppermute(value, BOTH, pairs)  38.9 us
    ppermute x32, waiting for transfers between devices, shift(): return lax.ppermute(value, BOTH, pairs)  35.8 us
    pallas_call x19, Pallas kernels, call(): pl.pallas_call(body, out_shape=out_shape, in_specs=[VMEM] * len(inputs),...  25.7 us
    pallas_call x1, Pallas kernels, prepare(): pl.pallas_call(body, out_shape=(pltpu.VMEM((entries, 4096), jnp.bfloat16)...  3.51 us
    pallas_call x1, Pallas kernels, load(): pl.pallas_call(body, out_shape=pltpu.VMEM((weight.shape[0], 4096), jnp.bf...  3.35 us
  transfers between devices with their start and end apart: 32, of which 18 were waited for; matrix products, arithmetic and copies ran while one was open for 0% of the time, Pallas kernels for 23%

profile of v8, /device:TPU:0, one launch (start us, length us, event | category | flops | bytes accessed | tf_op | source)
XLA Modules:
  0.0 108.4 jit_solution(8091697969073290381)
XLA Ops:
  2.4 2.9 %collective-permute-start.2 = (bf16[64,1024]{1,0:T(8,128)(2,1)}, bf16[64,1024]{1,0:T(8,128)(2,1)S(1)}, u32[]{:S(2)}, u32[]{:S(2)}) collective-permute-start(bf16[64,1024]{1,0:T(8,128)(2,1)} %hidden_hbm.1), channel_id=1, source_target_pairs={{0,4},{1,5},{2,6},{3,7},{4,0},{5,1},{6,2},{7,3},{8,12},{9,13},{10,... | collective-permute-start | bytes 393224 | tf_op jit(solution)/shard_map/ppermute | solution.py:30
  6.6 3.5 %prepare.1 = (bf16[1002,4096]{1,0:T(8,128)(2,1)S(1)}, bf16[64,1024]{1,0:T(8,128)(2,1)S(1)}, f32[1024,128]{1,0:T(8,128)S(1)}, f32[1,8192]{1,0:T(1,128)S(1)}, f32[16,128]{1,0:T(8,128)S(1)}) custom-call(bf16[1002,8192]{1,0:T(8,128)(2,1)} %bitcast.9, bf16[64,1024]{1,0:T(8,128)(2,1)} %hidden_hbm.1, s32[1,1002]{1,0:T(1,128)} %bitcast.11, ...), custom_call_target="tpu_custom_call" | custom-call | tf_op jit(solution)/shard_map/prepare/pallas_call | solution.py:86
  18.5 2.3 %collective-permute-done.6.refs_2_ = bf16[32,4096]{1,0:T(8,128)(2,1)S(1)} collective-permute-done((bf16[32,4096]{1,0:T(8,128)(2,1)S(1)}, bf16[32,4096]{1,0:T(8,128)(2,1)S(1)}, u32[]{:S(2)}, u32[]{:S(2)}) %collective-permute-start.6) | collective-permute-done | bytes 262176 | tf_op jit(solution)/shard_map/ppermute | solution.py:30
  21.1 3.0 %collective-permute-start.9 = (bf16[32,4096]{1,0:T(8,128)(2,1)S(1)}, bf16[32,4096]{1,0:T(8,128)(2,1)S(1)}, u32[]{:S(2)}, u32[]{:S(2)}) collective-permute-start(bf16[32,4096]{1,0:T(8,128)(2,1)S(1)} %collective-permute-done.7.refs_3_), channel_id=1, source_target_pairs={{0,96},{1,25},{2,98},{3,27},{4,100},{5,29},{6,102},{7,31},{8,104},... | collective-permute-start | bytes 786440 | tf_op jit(solution)/shard_map/ppermute | solution.py:30
  24.1 3.4 %load.1.refs_1_ = bf16[1002,4096]{1,0:T(8,128)(2,1)S(1)} custom-call(bf16[1002,8192]{1,0:T(8,128)(2,1)} %bitcast.10), custom_call_target="tpu_custom_call" | custom-call | tf_op jit(solution)/shard_map/load/pallas_call | solution.py:115
  30.9 2.2 %collective-permute-start.11 = (bf16[128,4096]{1,0:T(8,128)(2,1)S(1)}, bf16[128,4096]{1,0:T(8,128)(2,1)S(1)}, u32[]{:S(2)}, u32[]{:S(2)}) collective-permute-start(bf16[128,4096]{1,0:T(8,128)(2,1)S(1)} %get-tuple-element.65), channel_id=1, source_target_pairs={{0,24},{1,97},{2,26},{3,99},{4,28},{5,101},{6,30},{7,103},{8,0},{9... | collective-permute-start | bytes 3145736 | tf_op jit(solution)/shard_map/ppermute | solution.py:30
  33.1 2.3 %multiply.8.refs_2_ = f32[2,4,1002,256]{3,2,1,0:T(8,128)S(1)} custom-call(bf16[1002,4096]{1,0:T(8,128)(2,1)S(1)} %get-tuple-element.45.refs_0_, bf16[1002,4096]{1,0:T(8,128)(2,1)S(1)} %load.1.refs_1_, bf16[256,4096]{1,0:T(8,128)(2,1)S(1)} %get-tuple-element.60.refs_2_), custom_call_target="tpu_custom_call" | custom-call | flops 2101346304 | bytes 4194304 | tf_op jit(solution)/shard_map/multiply/pallas_call | solution.py:34
  35.4 2.0 %collective-permute-start.15 = (bf16[128,4096]{1,0:T(8,128)(2,1)S(1)}, bf16[128,4096]{1,0:T(8,128)(2,1)S(1)}, u32[]{:S(2)}, u32[]{:S(2)}) collective-permute-start(bf16[128,4096]{1,0:T(8,128)(2,1)S(1)} %get-tuple-element.64), channel_id=1, source_target_pairs={{0,24},{1,97},{2,26},{3,99},{4,28},{5,101},{6,30},{7,103},{8,0},{9... | collective-permute-start | bytes 3145736 | tf_op jit(solution)/shard_map/ppermute | solution.py:30
  37.5 2.3 %multiply.9.refs_2_ = f32[2,4,1002,256]{3,2,1,0:T(8,128)S(1)} custom-call(bf16[1002,4096]{1,0:T(8,128)(2,1)S(1)} %get-tuple-element.45.refs_0_, bf16[1002,4096]{1,0:T(8,128)(2,1)S(1)} %load.1.refs_1_, f32[2,4,1002,256]{3,2,1,0:T(8,128)S(1)} %multiply.8.refs_2_, bf16[256,4096]{1,0:T(8,128)(2,1)S(1)} %collective-permute-done.12.refs_3_), custom_call_target="tpu_custom_call", output_to_operand_aliasing={{}: (2, {})} | custom-call | flops 2101346304 | bytes 4194304 | tf_op jit(solution)/shard_map/multiply/pallas_call | solution.py:34
  39.9 5.9 %collective-permute-done.10.refs_3_.upper_ref = bf16[128,4096]{1,0:T(8,128)(2,1)S(1)} collective-permute-done((bf16[128,4096]{1,0:T(8,128)(2,1)S(1)}, bf16[128,4096]{1,0:T(8,128)(2,1)S(1)}, u32[]{:S(2)}, u32[]{:S(2)}) %collective-permute-start.10) | collective-permute-done | bytes 1048608 | tf_op jit(solution)/shard_map/ppermute | solution.py:30
  49.5 2.3 %multiply.10.refs_2_ = f32[2,4,1002,256]{3,2,1,0:T(8,128)S(1)} custom-call(bf16[1002,4096]{1,0:T(8,128)(2,1)S(1)} %get-tuple-element.45.refs_0_, bf16[1002,4096]{1,0:T(8,128)(2,1)S(1)} %load.1.refs_1_, f32[2,4,1002,256]{3,2,1,0:T(8,128)S(1)} %multiply.9.refs_2_, ...), custom_call_target="tpu_custom_call", output_to_operand_aliasing={{}: (2, {})} | custom-call | flops 2101346304 | bytes 4194304 | tf_op jit(solution)/shard_map/multiply/pallas_call | solution.py:34
  51.9 5.1 %collective-permute-done.15.refs_3_ = bf16[128,4096]{1,0:T(8,128)(2,1)S(1)} collective-permute-done((bf16[128,4096]{1,0:T(8,128)(2,1)S(1)}, bf16[128,4096]{1,0:T(8,128)(2,1)S(1)}, u32[]{:S(2)}, u32[]{:S(2)}) %collective-permute-start.15) | collective-permute-done | bytes 1048608 | tf_op jit(solution)/shard_map/ppermute | solution.py:30
  57.0 2.3 %multiply.11.refs_2_ = f32[2,4,1002,256]{3,2,1,0:T(8,128)S(1)} custom-call(bf16[1002,4096]{1,0:T(8,128)(2,1)S(1)} %get-tuple-element.45.refs_0_, bf16[1002,4096]{1,0:T(8,128)(2,1)S(1)} %load.1.refs_1_, f32[2,4,1002,256]{3,2,1,0:T(8,128)S(1)} %multiply.10.refs_2_, ...), custom_call_target="tpu_custom_call", output_to_operand_aliasing={{}: (2, {})} | custom-call | flops 21013463040 | bytes 4194304 | tf_op jit(solution)/shard_map/multiply/pallas_call | solution.py:34
  59.4 2.3 %multiply.12.refs_2_ = f32[2,4,1002,256]{3,2,1,0:T(8,128)S(1)} custom-call(bf16[1002,4096]{1,0:T(8,128)(2,1)S(1)} %get-tuple-element.45.refs_0_, bf16[1002,4096]{1,0:T(8,128)(2,1)S(1)} %load.1.refs_1_, f32[2,4,1002,256]{3,2,1,0:T(8,128)S(1)} %multiply.11.refs_2_, bf16[256,4096]{1,0:T(8,128)(2,1)S(1)} %collective-permute-done.17.refs_3_), custom_call_target="tpu_custom_call", output_to_operand_aliasing={{}: (2, {})} | custom-call | flops 2101346304 | bytes 4194304 | tf_op jit(solution)/shard_map/multiply/pallas_call | solution.py:34
  61.7 6.6 %collective-permute-done.13.refs_3_ = bf16[128,4096]{1,0:T(8,128)(2,1)S(1)} collective-permute-done((bf16[128,4096]{1,0:T(8,128)(2,1)S(1)}, bf16[128,4096]{1,0:T(8,128)(2,1)S(1)}, u32[]{:S(2)}, u32[]{:S(2)}) %collective-permute-start.13) | collective-permute-done | bytes 1048608 | tf_op jit(solution)/shard_map/ppermute | solution.py:30
  69.3 2.3 %multiply.13.refs_2_ = f32[2,4,1002,256]{3,2,1,0:T(8,128)S(1)} custom-call(bf16[1002,4096]{1,0:T(8,128)(2,1)S(1)} %get-tuple-element.45.refs_0_, bf16[1002,4096]{1,0:T(8,128)(2,1)S(1)} %load.1.refs_1_, f32[2,4,1002,256]{3,2,1,0:T(8,128)S(1)} %multiply.12.refs_2_, ...), custom_call_target="tpu_custom_call", output_to_operand_aliasing={{}: (2, {})} | custom-call | flops 2101346304 | bytes 4194304 | tf_op jit(solution)/shard_map/multiply/pallas_call | solution.py:34
  72.4 2.3 %multiply.14.refs_2_ = f32[2,4,1002,256]{3,2,1,0:T(8,128)S(1)} custom-call(bf16[1002,4096]{1,0:T(8,128)(2,1)S(1)} %get-tuple-element.45.refs_0_, bf16[1002,4096]{1,0:T(8,128)(2,1)S(1)} %load.1.refs_1_, f32[2,4,1002,256]{3,2,1,0:T(8,128)S(1)} %multiply.13.refs_2_, ...), custom_call_target="tpu_custom_call", output_to_operand_aliasing={{}: (2, {})} | custom-call | flops 2101346304 | bytes 4194304 | tf_op jit(solution)/shard_map/multiply/pallas_call | solution.py:34
  75.4 2.3 %multiply.15.products_ref = f32[2,4,1002,256]{3,2,1,0:T(8,128)S(1)} custom-call(bf16[1002,4096]{1,0:T(8,128)(2,1)S(1)} %get-tuple-element.45.refs_0_, bf16[1002,4096]{1,0:T(8,128)(2,1)S(1)} %load.1.refs_1_, f32[2,4,1002,256]{3,2,1,0:T(8,128)S(1)} %multiply.14.refs_2_, ...), custom_call_target="tpu_custom_call", output_to_operand_aliasing={{}: (2, {})} | custom-call | flops 2101346304 | bytes 4194304 | tf_op jit(solution)/shard_map/multiply/pallas_call | solution.py:34
  77.8 2.4 %join_halves.1 = (f32[1024,1024]{1,0:T(8,128)S(1)}, f32[40,128]{1,0:T(8,128)S(1)}) custom-call(f32[2,4,1002,256]{3,2,1,0:T(8,128)S(1)} %multiply.15.products_ref, f32[16,128]{1,0:T(8,128)S(1)} %get-tuple-element.72.floors_ref, s32[8,128]{1,0:T(8,128)S(1)} %bitcast.7), custom_call_target="tpu_custom_call" | custom-call | tf_op jit(solution)/shard_map/join_halves/pallas_call | solution.py:34
  81.5 2.4 %collective-permute-start.25 = (f32[40,128]{1,0:T(8,128)S(1)}, f32[40,128]{1,0:T(8,128)S(1)}, u32[]{:S(2)}, u32[]{:S(2)}) collective-permute-start(f32[40,128]{1,0:T(8,128)S(1)} %get-tuple-element.78.refs_0_), channel_id=1, source_target_pairs={{0,5},{1,4},{2,7},{3,6},{4,1},{5,0},{6,3},{7,2},{8,13},{9,12},{10,... | collective-permute-start | bytes 61448 | tf_op jit(solution)/shard_map/ppermute | solution.py:30
  87.1 2.5 %collective-permute-done.23.refs_1_ = f32[40,128]{1,0:T(8,128)S(1)} collective-permute-done((f32[40,128]{1,0:T(8,128)S(1)}, f32[40,128]{1,0:T(8,128)S(1)}, u32[]{:S(2)}, u32[]{:S(2)}) %collective-permute-start.23) | collective-permute-done | bytes 20512 | tf_op jit(solution)/shard_map/ppermute | solution.py:30
  89.6 3.3 %collective-permute-start.28 = (f32[40,128]{1,0:T(8,128)S(1)}, f32[40,128]{1,0:T(8,128)S(1)}, u32[]{:S(2)}, u32[]{:S(2)}) collective-permute-start(f32[40,128]{1,0:T(8,128)S(1)} %get-tuple-element.80.refs_0_), channel_id=1, source_target_pairs={{0,17},{1,16},{2,19},{3,18},{4,21},{5,20},{6,23},{7,22},{8,25},{9,... | collective-permute-start | bytes 61448 | tf_op jit(solution)/shard_map/ppermute | solution.py:30
  96.2 2.2 %collective-permute-done.26.refs_1_ = f32[40,128]{1,0:T(8,128)S(1)} collective-permute-done((f32[40,128]{1,0:T(8,128)S(1)}, f32[40,128]{1,0:T(8,128)S(1)}, u32[]{:S(2)}, u32[]{:S(2)}) %collective-permute-start.26) | collective-permute-done | bytes 20512 | tf_op jit(solution)/shard_map/ppermute | solution.py:30
  106.0 2.2 %finish.1 = (f32[1002,1024]{1,0:T(8,128)}, f32[8,128]{1,0:T(8,128)}) custom-call(f32[1024,1024]{1,0:T(8,128)S(1)} %get-tuple-element.75.sums_ref, f32[1024,128]{1,0:T(8,128)S(1)} %get-tuple-element.76.floors_ref, f32[32,128]{1,0:T(8,128)S(1)} %join_x.1.terms_ref), custom_call_target="tpu_custom_call" | custom-call | tf_op jit(solution)/shard_map/finish/pallas_call | solution.py:34
  (65 shorter events, 36.9 us)
Async XLA Ops:
  0.6 9.5 %collective-permute-start = (bf16[64,1024]{1,0:T(8,128)(2,1)}, bf16[64,1024]{1,0:T(8,128)(2,1)S(1)}, u32[]{:S(2)}, u32[]{:S(2)}) collective-permute-start(bf16[64,1024]{1,0:T(8,128)(2,1)} %hidden_hbm.1), channel_id=1, source_target_pairs={{0,2},{1,3},{2,4},{3,5},{4,6},{5,7},{6,0},{7,1},{8,10},{9,11},{10,... | collective-permute-start | bytes 393224 | tf_op jit(solution)/shard_map/ppermute | solution.py:30
  2.4 9.1 %collective-permute-start.2 = (bf16[64,1024]{1,0:T(8,128)(2,1)}, bf16[64,1024]{1,0:T(8,128)(2,1)S(1)}, u32[]{:S(2)}, u32[]{:S(2)}) collective-permute-start(bf16[64,1024]{1,0:T(8,128)(2,1)} %hidden_hbm.1), channel_id=1, source_target_pairs={{0,4},{1,5},{2,6},{3,7},{4,0},{5,1},{6,2},{7,3},{8,12},{9,13},{10,... | collective-permute-start | bytes 393224 | tf_op jit(solution)/shard_map/ppermute | solution.py:30
  5.3 6.2 %collective-permute-start.1 = (bf16[64,1024]{1,0:T(8,128)(2,1)}, bf16[64,1024]{1,0:T(8,128)(2,1)S(1)}, u32[]{:S(2)}, u32[]{:S(2)}) collective-permute-start(bf16[64,1024]{1,0:T(8,128)(2,1)} %hidden_hbm.1), channel_id=1, source_target_pairs={{0,6},{1,7},{2,0},{3,1},{4,2},{5,3},{6,4},{7,5},{8,14},{9,15},{10,... | collective-permute-start | bytes 393224 | tf_op jit(solution)/shard_map/ppermute | solution.py:30
  13.2 7.7 %collective-permute-start.6 = (bf16[32,4096]{1,0:T(8,128)(2,1)S(1)}, bf16[32,4096]{1,0:T(8,128)(2,1)S(1)}, u32[]{:S(2)}, u32[]{:S(2)}) collective-permute-start(bf16[32,4096]{1,0:T(8,128)(2,1)S(1)} %get-tuple-element.53.refs_0_), channel_id=1, source_target_pairs={{0,32},{1,9},{2,34},{3,11},{4,36},{5,13},{6,38},{7,15},{8,40},{9,1... | collective-permute-start | bytes 786440 | tf_op jit(solution)/shard_map/ppermute | solution.py:30
  14.8 6.4 %collective-permute-start.7 = (bf16[32,4096]{1,0:T(8,128)(2,1)S(1)}, bf16[32,4096]{1,0:T(8,128)(2,1)S(1)}, u32[]{:S(2)}, u32[]{:S(2)}) collective-permute-start(bf16[32,4096]{1,0:T(8,128)(2,1)S(1)} %get-tuple-element.54.refs_1_), channel_id=1, source_target_pairs={{0,96},{1,25},{2,98},{3,27},{4,100},{5,29},{6,102},{7,31},{8,104},... | collective-permute-start | bytes 786440 | tf_op jit(solution)/shard_map/ppermute | solution.py:30
  16.5 10.9 %collective-permute-start.4 = (bf16[32,4096]{1,0:T(8,128)(2,1)S(1)}, bf16[32,4096]{1,0:T(8,128)(2,1)S(1)}, u32[]{:S(2)}, u32[]{:S(2)}) collective-permute-start(bf16[32,4096]{1,0:T(8,128)(2,1)S(1)} %get-tuple-element.53.refs_0_), channel_id=1, source_target_pairs={{0,96},{1,25},{2,98},{3,27},{4,100},{5,29},{6,102},{7,31},{8,104},... | collective-permute-start | bytes 786440 | tf_op jit(solution)/shard_map/ppermute | solution.py:30
  18.1 9.4 %collective-permute-start.5 = (bf16[32,4096]{1,0:T(8,128)(2,1)S(1)}, bf16[32,4096]{1,0:T(8,128)(2,1)S(1)}, u32[]{:S(2)}, u32[]{:S(2)}) collective-permute-start(bf16[32,4096]{1,0:T(8,128)(2,1)S(1)} %get-tuple-element.54.refs_1_), channel_id=1, source_target_pairs={{0,32},{1,9},{2,34},{3,11},{4,36},{5,13},{6,38},{7,15},{8,40},{9,1... | collective-permute-start | bytes 786440 | tf_op jit(solution)/shard_map/ppermute | solution.py:30
  20.9 7.6 %collective-permute-start.8 = (bf16[32,4096]{1,0:T(8,128)(2,1)S(1)}, bf16[32,4096]{1,0:T(8,128)(2,1)S(1)}, u32[]{:S(2)}, u32[]{:S(2)}) collective-permute-start(bf16[32,4096]{1,0:T(8,128)(2,1)S(1)} %collective-permute-done.6.refs_2_), channel_id=1, source_target_pairs={{0,32},{1,9},{2,34},{3,11},{4,36},{5,13},{6,38},{7,15},{8,40},{9,1... | collective-permute-start | bytes 786440 | tf_op jit(solution)/shard_map/ppermute | solution.py:30
  21.1 7.3 %collective-permute-start.9 = (bf16[32,4096]{1,0:T(8,128)(2,1)S(1)}, bf16[32,4096]{1,0:T(8,128)(2,1)S(1)}, u32[]{:S(2)}, u32[]{:S(2)}) collective-permute-start(bf16[32,4096]{1,0:T(8,128)(2,1)S(1)} %collective-permute-done.7.refs_3_), channel_id=1, source_target_pairs={{0,96},{1,25},{2,98},{3,27},{4,100},{5,29},{6,102},{7,31},{8,104},... | collective-permute-start | bytes 786440 | tf_op jit(solution)/shard_map/ppermute | solution.py:30
  28.8 8.7 %collective-permute-start.12 = (bf16[256,4096]{1,0:T(8,128)(2,1)S(1)}, bf16[256,4096]{1,0:T(8,128)(2,1)S(1)}, u32[]{:S(2)}, u32[]{:S(2)}) collective-permute-start(bf16[256,4096]{1,0:T(8,128)(2,1)S(1)} %get-tuple-element.60.refs_2_), channel_id=1, source_target_pairs={{0,1},{1,0},{2,3},{3,2},{4,5},{5,4},{6,7},{7,6},{8,9},{9,8},{10,11... | collective-permute-start | bytes 6291464 | tf_op jit(solution)/shard_map/ppermute | solution.py:30
  28.9 16.9 %collective-permute-start.10 = (bf16[128,4096]{1,0:T(8,128)(2,1)S(1)}, bf16[128,4096]{1,0:T(8,128)(2,1)S(1)}, u32[]{:S(2)}, u32[]{:S(2)}) collective-permute-start(bf16[128,4096]{1,0:T(8,128)(2,1)S(1)} %get-tuple-element.64), channel_id=1, source_target_pairs={{0,8},{1,33},{2,10},{3,35},{4,12},{5,37},{6,14},{7,39},{8,16},{9,4... | collective-permute-start | bytes 3145736 | tf_op jit(solution)/shard_map/ppermute | solution.py:30
  30.9 14.9 %collective-permute-start.11 = (bf16[128,4096]{1,0:T(8,128)(2,1)S(1)}, bf16[128,4096]{1,0:T(8,128)(2,1)S(1)}, u32[]{:S(2)}, u32[]{:S(2)}) collective-permute-start(bf16[128,4096]{1,0:T(8,128)(2,1)S(1)} %get-tuple-element.65), channel_id=1, source_target_pairs={{0,24},{1,97},{2,26},{3,99},{4,28},{5,101},{6,30},{7,103},{8,0},{9... | collective-permute-start | bytes 3145736 | tf_op jit(solution)/shard_map/ppermute | solution.py:30
  35.4 21.5 %collective-permute-start.15 = (bf16[128,4096]{1,0:T(8,128)(2,1)S(1)}, bf16[128,4096]{1,0:T(8,128)(2,1)S(1)}, u32[]{:S(2)}, u32[]{:S(2)}) collective-permute-start(bf16[128,4096]{1,0:T(8,128)(2,1)S(1)} %get-tuple-element.64), channel_id=1, source_target_pairs={{0,24},{1,97},{2,26},{3,99},{4,28},{5,101},{6,30},{7,103},{8,0},{9... | collective-permute-start | bytes 3145736 | tf_op jit(solution)/shard_map/ppermute | solution.py:30
  37.4 19.6 %collective-permute-start.16 = (bf16[128,4096]{1,0:T(8,128)(2,1)S(1)}, bf16[128,4096]{1,0:T(8,128)(2,1)S(1)}, u32[]{:S(2)}, u32[]{:S(2)}) collective-permute-start(bf16[128,4096]{1,0:T(8,128)(2,1)S(1)} %get-tuple-element.65), channel_id=1, source_target_pairs={{0,8},{1,33},{2,10},{3,35},{4,12},{5,37},{6,14},{7,39},{8,16},{9,4... | collective-permute-start | bytes 3145736 | tf_op jit(solution)/shard_map/ppermute | solution.py:30
  45.8 22.5 %collective-permute-start.13 = (bf16[128,4096]{1,0:T(8,128)(2,1)S(1)}, bf16[128,4096]{1,0:T(8,128)(2,1)S(1)}, u32[]{:S(2)}, u32[]{:S(2)}) collective-permute-start(bf16[128,4096]{1,0:T(8,128)(2,1)S(1)} %collective-permute-done.10.refs_3_.upper_ref), channel_id=1, source_target_pairs={{0,8},{1,33},{2,10},{3,35},{4,12},{5,37},{6,14},{7,39},{8,16},{9,4... | collective-permute-start | bytes 3145736 | tf_op jit(solution)/shard_map/ppermute | solution.py:30
  47.6 20.7 %collective-permute-start.14 = (bf16[128,4096]{1,0:T(8,128)(2,1)S(1)}, bf16[128,4096]{1,0:T(8,128)(2,1)S(1)}, u32[]{:S(2)}, u32[]{:S(2)}) collective-permute-start(bf16[128,4096]{1,0:T(8,128)(2,1)S(1)} %collective-permute-done.11.refs_4_.lower_ref), channel_id=1, source_target_pairs={{0,24},{1,97},{2,26},{3,99},{4,28},{5,101},{6,30},{7,103},{8,0},{9... | collective-permute-start | bytes 3145736 | tf_op jit(solution)/shard_map/ppermute | solution.py:30
  49.2 10.1 %collective-permute-start.17 = (bf16[256,4096]{1,0:T(8,128)(2,1)S(1)}, bf16[256,4096]{1,0:T(8,128)(2,1)S(1)}, u32[]{:S(2)}, u32[]{:S(2)}) collective-permute-start(bf16[256,4096]{1,0:T(8,128)(2,1)S(1)} %beside_each.1), channel_id=1, source_target_pairs={{0,1},{1,0},{2,3},{3,2},{4,5},{5,4},{6,7},{7,6},{8,9},{9,8},{10,11... | collective-permute-start | bytes 6291464 | tf_op jit(solution)/shard_map/ppermute | solution.py:30
  68.8 6.0 %collective-permute-start.20 = (bf16[128,4096]{1,0:T(8,128)(2,1)S(1)}, bf16[128,4096]{1,0:T(8,128)(2,1)S(1)}, u32[]{:S(2)}, u32[]{:S(2)}) collective-permute-start(bf16[128,4096]{1,0:T(8,128)(2,1)S(1)} %collective-permute-done.13.refs_3_), channel_id=1, source_target_pairs={{0,1},{1,0},{2,3},{3,2},{4,5},{5,4},{6,7},{7,6},{8,9},{9,8},{10,11... | collective-permute-start | bytes 3145736 | tf_op jit(solution)/shard_map/ppermute | solution.py:30
  68.8 6.6 %collective-permute-start.21 = (bf16[128,4096]{1,0:T(8,128)(2,1)S(1)}, bf16[128,4096]{1,0:T(8,128)(2,1)S(1)}, u32[]{:S(2)}, u32[]{:S(2)}) collective-permute-start(bf16[128,4096]{1,0:T(8,128)(2,1)S(1)} %collective-permute-done.14.refs_4_), channel_id=1, source_target_pairs={{0,1},{1,0},{2,3},{3,2},{4,5},{5,4},{6,7},{7,6},{8,9},{9,8},{10,11... | collective-permute-start | bytes 3145736 | tf_op jit(solution)/shard_map/ppermute | solution.py:30
  81.5 4.8 %collective-permute-start.25 = (f32[40,128]{1,0:T(8,128)S(1)}, f32[40,128]{1,0:T(8,128)S(1)}, u32[]{:S(2)}, u32[]{:S(2)}) collective-permute-start(f32[40,128]{1,0:T(8,128)S(1)} %get-tuple-element.78.refs_0_), channel_id=1, source_target_pairs={{0,5},{1,4},{2,7},{3,6},{4,1},{5,0},{6,3},{7,2},{8,13},{9,12},{10,... | collective-permute-start | bytes 61448 | tf_op jit(solution)/shard_map/ppermute | solution.py:30
  85.2 4.4 %collective-permute-start.23 = (f32[40,128]{1,0:T(8,128)S(1)}, f32[40,128]{1,0:T(8,128)S(1)}, u32[]{:S(2)}, u32[]{:S(2)}) collective-permute-start(f32[40,128]{1,0:T(8,128)S(1)} %get-tuple-element.78.refs_0_), channel_id=1, source_target_pairs={{0,3},{1,2},{2,5},{3,4},{4,7},{5,6},{6,1},{7,0},{8,11},{9,10},{10,... | collective-permute-start | bytes 61448 | tf_op jit(solution)/shard_map/ppermute | solution.py:30
  89.6 5.1 %collective-permute-start.28 = (f32[40,128]{1,0:T(8,128)S(1)}, f32[40,128]{1,0:T(8,128)S(1)}, u32[]{:S(2)}, u32[]{:S(2)}) collective-permute-start(f32[40,128]{1,0:T(8,128)S(1)} %get-tuple-element.80.refs_0_), channel_id=1, source_target_pairs={{0,17},{1,16},{2,19},{3,18},{4,21},{5,20},{6,23},{7,22},{8,25},{9,... | collective-permute-start | bytes 61448 | tf_op jit(solution)/shard_map/ppermute | solution.py:30
  93.9 4.4 %collective-permute-start.26 = (f32[40,128]{1,0:T(8,128)S(1)}, f32[40,128]{1,0:T(8,128)S(1)}, u32[]{:S(2)}, u32[]{:S(2)}) collective-permute-start(f32[40,128]{1,0:T(8,128)S(1)} %get-tuple-element.80.refs_0_), channel_id=1, source_target_pairs={{0,9},{1,8},{2,11},{3,10},{4,13},{5,12},{6,15},{7,14},{8,17},{9,16... | collective-permute-start | bytes 61448 | tf_op jit(solution)/shard_map/ppermute | solution.py:30
  98.4 5.3 %collective-permute-start.31 = (f32[40,128]{1,0:T(8,128)S(1)}, f32[40,128]{1,0:T(8,128)S(1)}, u32[]{:S(2)}, u32[]{:S(2)}) collective-permute-start(f32[40,128]{1,0:T(8,128)S(1)} %get-tuple-element.82.refs_0_), channel_id=1, source_target_pairs={{0,65},{1,64},{2,67},{3,66},{4,69},{5,68},{6,71},{7,70},{8,73},{9,... | collective-permute-start | bytes 61448 | tf_op jit(solution)/shard_map/ppermute | solution.py:30
  (10 other events, 56.1 us)

commit v9 on v8

--- a/solution.py
+++ b/solution.py
@@ -169,7 +169,7 @@
 
 def join(axis, stats, before, last=None):
     size = SIZES[axis]
-    hops = [0, 1] if size == 2 else [0, 1, 3, 2]
+    hops = [0, 1] if size == 2 else [0, 3, 1, 2]
     pieces = [stats] + [shift(stats, axis, k, axis != "c") for k in hops[1:]]
 
     def body(*refs):

time: 110 us -> 107 us (0.973)
  waiting for transfers between devices: 35.8 us -> 29.9 us
  starting transfers between devices: 38.9 us -> 42.4 us
    ppermute x32, waiting for transfers between devices: 35.8 us -> 29.9 us  [shift(): return lax.ppermute(value, BOTH, pairs)]
    ppermute x32, starting transfers between devices: 38.9 us -> 42.4 us  [shift(): return lax.ppermute(value, BOTH, pairs)]
  transfers between devices with their start and end apart: 32 -> 32, of which waited for: 18 -> 14; matrix products, arithmetic and copies ran while one was open for 0% -> 0% of each run, Pallas kernels for 23% -> 23%
where the time goes in v9:
time: 107 us; the launch traced here: 106 us
  starting transfers between devices  42.4 us (40%)
  Pallas kernels  32.5 us (30%)
  waiting for transfers between devices  29.9 us (28%)
    ppermute x32, starting transfers between devices, shift(): return lax.ppermute(value, BOTH, pairs)  42.4 us
    ppermute x32, waiting for transfers between devices, shift(): return lax.ppermute(value, BOTH, pairs)  29.9 us
    pallas_call x19, Pallas kernels, call(): pl.pallas_call(body, out_shape=out_shape, in_specs=[VMEM] * len(inputs),...  25.7 us
    pallas_call x1, Pallas kernels, prepare(): pl.pallas_call(body, out_shape=(pltpu.VMEM((entries, 4096), jnp.bfloat16)...  3.51 us
    pallas_call x1, Pallas kernels, load(): pl.pallas_call(body, out_shape=pltpu.VMEM((weight.shape[0], 4096), jnp.bf...  3.35 us
  transfers between devices with their start and end apart: 32, of which 14 were waited for; matrix products, arithmetic and copies ran while one was open for 0% of the time, Pallas kernels for 23%

profile of v9, /device:TPU:0, one launch (start us, length us, event | category | flops | bytes accessed | tf_op | source)
XLA Modules:
  0.0 105.8 jit_solution(15373350843659585494)
XLA Ops:
  2.4 2.9 %collective-permute-start.2 = (bf16[64,1024]{1,0:T(8,128)(2,1)}, bf16[64,1024]{1,0:T(8,128)(2,1)S(1)}, u32[]{:S(2)}, u32[]{:S(2)}) collective-permute-start(bf16[64,1024]{1,0:T(8,128)(2,1)} %hidden_hbm.1), channel_id=1, source_target_pairs={{0,4},{1,5},{2,6},{3,7},{4,0},{5,1},{6,2},{7,3},{8,12},{9,13},{10,... | collective-permute-start | bytes 393224 | tf_op jit(solution)/shard_map/ppermute | solution.py:30
  6.6 3.5 %prepare.1 = (bf16[1002,4096]{1,0:T(8,128)(2,1)S(1)}, bf16[64,1024]{1,0:T(8,128)(2,1)S(1)}, f32[1024,128]{1,0:T(8,128)S(1)}, f32[1,8192]{1,0:T(1,128)S(1)}, f32[16,128]{1,0:T(8,128)S(1)}) custom-call(bf16[1002,8192]{1,0:T(8,128)(2,1)} %bitcast.9, bf16[64,1024]{1,0:T(8,128)(2,1)} %hidden_hbm.1, s32[1,1002]{1,0:T(1,128)} %bitcast.11, ...), custom_call_target="tpu_custom_call" | custom-call | tf_op jit(solution)/shard_map/prepare/pallas_call | solution.py:86
  18.5 2.3 %collective-permute-done.6.refs_2_ = bf16[32,4096]{1,0:T(8,128)(2,1)S(1)} collective-permute-done((bf16[32,4096]{1,0:T(8,128)(2,1)S(1)}, bf16[32,4096]{1,0:T(8,128)(2,1)S(1)}, u32[]{:S(2)}, u32[]{:S(2)}) %collective-permute-start.6) | collective-permute-done | bytes 262176 | tf_op jit(solution)/shard_map/ppermute | solution.py:30
  21.1 3.0 %collective-permute-start.9 = (bf16[32,4096]{1,0:T(8,128)(2,1)S(1)}, bf16[32,4096]{1,0:T(8,128)(2,1)S(1)}, u32[]{:S(2)}, u32[]{:S(2)}) collective-permute-start(bf16[32,4096]{1,0:T(8,128)(2,1)S(1)} %collective-permute-done.7.refs_3_), channel_id=1, source_target_pairs={{0,96},{1,25},{2,98},{3,27},{4,100},{5,29},{6,102},{7,31},{8,104},... | collective-permute-start | bytes 786440 | tf_op jit(solution)/shard_map/ppermute | solution.py:30
  24.1 3.4 %load.1.refs_1_ = bf16[1002,4096]{1,0:T(8,128)(2,1)S(1)} custom-call(bf16[1002,8192]{1,0:T(8,128)(2,1)} %bitcast.10), custom_call_target="tpu_custom_call" | custom-call | tf_op jit(solution)/shard_map/load/pallas_call | solution.py:115
  30.9 2.2 %collective-permute-start.11 = (bf16[128,4096]{1,0:T(8,128)(2,1)S(1)}, bf16[128,4096]{1,0:T(8,128)(2,1)S(1)}, u32[]{:S(2)}, u32[]{:S(2)}) collective-permute-start(bf16[128,4096]{1,0:T(8,128)(2,1)S(1)} %get-tuple-element.65), channel_id=1, source_target_pairs={{0,24},{1,97},{2,26},{3,99},{4,28},{5,101},{6,30},{7,103},{8,0},{9... | collective-permute-start | bytes 3145736 | tf_op jit(solution)/shard_map/ppermute | solution.py:30
  33.1 2.3 %multiply.8.refs_2_ = f32[2,4,1002,256]{3,2,1,0:T(8,128)S(1)} custom-call(bf16[1002,4096]{1,0:T(8,128)(2,1)S(1)} %get-tuple-element.45.refs_0_, bf16[1002,4096]{1,0:T(8,128)(2,1)S(1)} %load.1.refs_1_, bf16[256,4096]{1,0:T(8,128)(2,1)S(1)} %get-tuple-element.60.refs_2_), custom_call_target="tpu_custom_call" | custom-call | flops 2101346304 | bytes 4194304 | tf_op jit(solution)/shard_map/multiply/pallas_call | solution.py:34
  37.5 2.3 %multiply.9.refs_2_ = f32[2,4,1002,256]{3,2,1,0:T(8,128)S(1)} custom-call(bf16[1002,4096]{1,0:T(8,128)(2,1)S(1)} %get-tuple-element.45.refs_0_, bf16[1002,4096]{1,0:T(8,128)(2,1)S(1)} %load.1.refs_1_, f32[2,4,1002,256]{3,2,1,0:T(8,128)S(1)} %multiply.8.refs_2_, bf16[256,4096]{1,0:T(8,128)(2,1)S(1)} %collective-permute-done.12.refs_3_), custom_call_target="tpu_custom_call", output_to_operand_aliasing={{}: (2, {})} | custom-call | flops 2101346304 | bytes 4194304 | tf_op jit(solution)/shard_map/multiply/pallas_call | solution.py:34
  39.9 5.9 %collective-permute-done.10.refs_3_.upper_ref = bf16[128,4096]{1,0:T(8,128)(2,1)S(1)} collective-permute-done((bf16[128,4096]{1,0:T(8,128)(2,1)S(1)}, bf16[128,4096]{1,0:T(8,128)(2,1)S(1)}, u32[]{:S(2)}, u32[]{:S(2)}) %collective-permute-start.10) | collective-permute-done | bytes 1048608 | tf_op jit(solution)/shard_map/ppermute | solution.py:30
  49.5 2.3 %multiply.10.refs_2_ = f32[2,4,1002,256]{3,2,1,0:T(8,128)S(1)} custom-call(bf16[1002,4096]{1,0:T(8,128)(2,1)S(1)} %get-tuple-element.45.refs_0_, bf16[1002,4096]{1,0:T(8,128)(2,1)S(1)} %load.1.refs_1_, f32[2,4,1002,256]{3,2,1,0:T(8,128)S(1)} %multiply.9.refs_2_, ...), custom_call_target="tpu_custom_call", output_to_operand_aliasing={{}: (2, {})} | custom-call | flops 2101346304 | bytes 4194304 | tf_op jit(solution)/shard_map/multiply/pallas_call | solution.py:34
  51.9 5.1 %collective-permute-done.15.refs_3_ = bf16[128,4096]{1,0:T(8,128)(2,1)S(1)} collective-permute-done((bf16[128,4096]{1,0:T(8,128)(2,1)S(1)}, bf16[128,4096]{1,0:T(8,128)(2,1)S(1)}, u32[]{:S(2)}, u32[]{:S(2)}) %collective-permute-start.15) | collective-permute-done | bytes 1048608 | tf_op jit(solution)/shard_map/ppermute | solution.py:30
  57.0 2.3 %multiply.11.refs_2_ = f32[2,4,1002,256]{3,2,1,0:T(8,128)S(1)} custom-call(bf16[1002,4096]{1,0:T(8,128)(2,1)S(1)} %get-tuple-element.45.refs_0_, bf16[1002,4096]{1,0:T(8,128)(2,1)S(1)} %load.1.refs_1_, f32[2,4,1002,256]{3,2,1,0:T(8,128)S(1)} %multiply.10.refs_2_, ...), custom_call_target="tpu_custom_call", output_to_operand_aliasing={{}: (2, {})} | custom-call | flops 21013463040 | bytes 4194304 | tf_op jit(solution)/shard_map/multiply/pallas_call | solution.py:34
  59.4 2.3 %multiply.12.refs_2_ = f32[2,4,1002,256]{3,2,1,0:T(8,128)S(1)} custom-call(bf16[1002,4096]{1,0:T(8,128)(2,1)S(1)} %get-tuple-element.45.refs_0_, bf16[1002,4096]{1,0:T(8,128)(2,1)S(1)} %load.1.refs_1_, f32[2,4,1002,256]{3,2,1,0:T(8,128)S(1)} %multiply.11.refs_2_, bf16[256,4096]{1,0:T(8,128)(2,1)S(1)} %collective-permute-done.17.refs_3_), custom_call_target="tpu_custom_call", output_to_operand_aliasing={{}: (2, {})} | custom-call | flops 2101346304 | bytes 4194304 | tf_op jit(solution)/shard_map/multiply/pallas_call | solution.py:34
  61.7 6.6 %collective-permute-done.13.refs_3_ = bf16[128,4096]{1,0:T(8,128)(2,1)S(1)} collective-permute-done((bf16[128,4096]{1,0:T(8,128)(2,1)S(1)}, bf16[128,4096]{1,0:T(8,128)(2,1)S(1)}, u32[]{:S(2)}, u32[]{:S(2)}) %collective-permute-start.13) | collective-permute-done | bytes 1048608 | tf_op jit(solution)/shard_map/ppermute | solution.py:30
  69.3 2.3 %multiply.13.refs_2_ = f32[2,4,1002,256]{3,2,1,0:T(8,128)S(1)} custom-call(bf16[1002,4096]{1,0:T(8,128)(2,1)S(1)} %get-tuple-element.45.refs_0_, bf16[1002,4096]{1,0:T(8,128)(2,1)S(1)} %load.1.refs_1_, f32[2,4,1002,256]{3,2,1,0:T(8,128)S(1)} %multiply.12.refs_2_, ...), custom_call_target="tpu_custom_call", output_to_operand_aliasing={{}: (2, {})} | custom-call | flops 2101346304 | bytes 4194304 | tf_op jit(solution)/shard_map/multiply/pallas_call | solution.py:34
  72.4 2.3 %multiply.14.refs_2_ = f32[2,4,1002,256]{3,2,1,0:T(8,128)S(1)} custom-call(bf16[1002,4096]{1,0:T(8,128)(2,1)S(1)} %get-tuple-element.45.refs_0_, bf16[1002,4096]{1,0:T(8,128)(2,1)S(1)} %load.1.refs_1_, f32[2,4,1002,256]{3,2,1,0:T(8,128)S(1)} %multiply.13.refs_2_, ...), custom_call_target="tpu_custom_call", output_to_operand_aliasing={{}: (2, {})} | custom-call | flops 2101346304 | bytes 4194304 | tf_op jit(solution)/shard_map/multiply/pallas_call | solution.py:34
  75.4 2.3 %multiply.15.products_ref = f32[2,4,1002,256]{3,2,1,0:T(8,128)S(1)} custom-call(bf16[1002,4096]{1,0:T(8,128)(2,1)S(1)} %get-tuple-element.45.refs_0_, bf16[1002,4096]{1,0:T(8,128)(2,1)S(1)} %load.1.refs_1_, f32[2,4,1002,256]{3,2,1,0:T(8,128)S(1)} %multiply.14.refs_2_, ...), custom_call_target="tpu_custom_call", output_to_operand_aliasing={{}: (2, {})} | custom-call | flops 2101346304 | bytes 4194304 | tf_op jit(solution)/shard_map/multiply/pallas_call | solution.py:34
  77.8 2.4 %join_halves.1 = (f32[1024,1024]{1,0:T(8,128)S(1)}, f32[40,128]{1,0:T(8,128)S(1)}) custom-call(f32[2,4,1002,256]{3,2,1,0:T(8,128)S(1)} %multiply.15.products_ref, f32[16,128]{1,0:T(8,128)S(1)} %get-tuple-element.72.floors_ref, s32[8,128]{1,0:T(8,128)S(1)} %bitcast.7), custom_call_target="tpu_custom_call" | custom-call | tf_op jit(solution)/shard_map/join_halves/pallas_call | solution.py:34
  81.5 2.4 %collective-permute-start.25 = (f32[40,128]{1,0:T(8,128)S(1)}, f32[40,128]{1,0:T(8,128)S(1)}, u32[]{:S(2)}, u32[]{:S(2)}) collective-permute-start(f32[40,128]{1,0:T(8,128)S(1)} %get-tuple-element.78.refs_0_), channel_id=1, source_target_pairs={{0,5},{1,4},{2,7},{3,6},{4,1},{5,0},{6,3},{7,2},{8,13},{9,12},{10,... | collective-permute-start | bytes 61448 | tf_op jit(solution)/shard_map/ppermute | solution.py:30
  84.3 2.6 %collective-permute-start.23 = (f32[40,128]{1,0:T(8,128)S(1)}, f32[40,128]{1,0:T(8,128)S(1)}, u32[]{:S(2)}, u32[]{:S(2)}) collective-permute-start(f32[40,128]{1,0:T(8,128)S(1)} %get-tuple-element.78.refs_0_), channel_id=1, source_target_pairs={{0,7},{1,6},{2,1},{3,0},{4,3},{5,2},{6,5},{7,4},{8,15},{9,14},{10,... | collective-permute-start | bytes 61448 | tf_op jit(solution)/shard_map/ppermute | solution.py:30
  88.4 3.5 %collective-permute-start.28 = (f32[40,128]{1,0:T(8,128)S(1)}, f32[40,128]{1,0:T(8,128)S(1)}, u32[]{:S(2)}, u32[]{:S(2)}) collective-permute-start(f32[40,128]{1,0:T(8,128)S(1)} %get-tuple-element.80.refs_0_), channel_id=1, source_target_pairs={{0,17},{1,16},{2,19},{3,18},{4,21},{5,20},{6,23},{7,22},{8,25},{9,... | collective-permute-start | bytes 61448 | tf_op jit(solution)/shard_map/ppermute | solution.py:30
  92.3 2.5 %collective-permute-start.26 = (f32[40,128]{1,0:T(8,128)S(1)}, f32[40,128]{1,0:T(8,128)S(1)}, u32[]{:S(2)}, u32[]{:S(2)}) collective-permute-start(f32[40,128]{1,0:T(8,128)S(1)} %get-tuple-element.80.refs_0_), channel_id=1, source_target_pairs={{0,25},{1,24},{2,27},{3,26},{4,29},{5,28},{6,31},{7,30},{8,1},{9,0... | collective-permute-start | bytes 61448 | tf_op jit(solution)/shard_map/ppermute | solution.py:30
  98.1 2.1 %collective-permute-start.30 = (f32[40,128]{1,0:T(8,128)S(1)}, f32[40,128]{1,0:T(8,128)S(1)}, u32[]{:S(2)}, u32[]{:S(2)}) collective-permute-start(f32[40,128]{1,0:T(8,128)S(1)} %get-tuple-element.82.refs_0_), channel_id=1, source_target_pairs={{0,33},{1,32},{2,35},{3,34},{4,37},{5,36},{6,39},{7,38},{8,41},{9,... | collective-permute-start | bytes 61448 | tf_op jit(solution)/shard_map/ppermute | solution.py:30
  103.5 2.2 %finish.1 = (f32[1002,1024]{1,0:T(8,128)}, f32[8,128]{1,0:T(8,128)}) custom-call(f32[1024,1024]{1,0:T(8,128)S(1)} %get-tuple-element.75.sums_ref, f32[1024,128]{1,0:T(8,128)S(1)} %get-tuple-element.76.floors_ref, f32[32,128]{1,0:T(8,128)S(1)} %join_x.1.terms_ref), custom_call_target="tpu_custom_call" | custom-call | tf_op jit(solution)/shard_map/finish/pallas_call | solution.py:34
  (65 shorter events, 33.7 us)
Async XLA Ops:
  0.6 9.5 %collective-permute-start = (bf16[64,1024]{1,0:T(8,128)(2,1)}, bf16[64,1024]{1,0:T(8,128)(2,1)S(1)}, u32[]{:S(2)}, u32[]{:S(2)}) collective-permute-start(bf16[64,1024]{1,0:T(8,128)(2,1)} %hidden_hbm.1), channel_id=1, source_target_pairs={{0,2},{1,3},{2,4},{3,5},{4,6},{5,7},{6,0},{7,1},{8,10},{9,11},{10,... | collective-permute-start | bytes 393224 | tf_op jit(solution)/shard_map/ppermute | solution.py:30
  2.4 9.1 %collective-permute-start.2 = (bf16[64,1024]{1,0:T(8,128)(2,1)}, bf16[64,1024]{1,0:T(8,128)(2,1)S(1)}, u32[]{:S(2)}, u32[]{:S(2)}) collective-permute-start(bf16[64,1024]{1,0:T(8,128)(2,1)} %hidden_hbm.1), channel_id=1, source_target_pairs={{0,4},{1,5},{2,6},{3,7},{4,0},{5,1},{6,2},{7,3},{8,12},{9,13},{10,... | collective-permute-start | bytes 393224 | tf_op jit(solution)/shard_map/ppermute | solution.py:30
  5.3 6.2 %collective-permute-start.1 = (bf16[64,1024]{1,0:T(8,128)(2,1)}, bf16[64,1024]{1,0:T(8,128)(2,1)S(1)}, u32[]{:S(2)}, u32[]{:S(2)}) collective-permute-start(bf16[64,1024]{1,0:T(8,128)(2,1)} %hidden_hbm.1), channel_id=1, source_target_pairs={{0,6},{1,7},{2,0},{3,1},{4,2},{5,3},{6,4},{7,5},{8,14},{9,15},{10,... | collective-permute-start | bytes 393224 | tf_op jit(solution)/shard_map/ppermute | solution.py:30
  13.2 7.7 %collective-permute-start.6 = (bf16[32,4096]{1,0:T(8,128)(2,1)S(1)}, bf16[32,4096]{1,0:T(8,128)(2,1)S(1)}, u32[]{:S(2)}, u32[]{:S(2)}) collective-permute-start(bf16[32,4096]{1,0:T(8,128)(2,1)S(1)} %get-tuple-element.53.refs_0_), channel_id=1, source_target_pairs={{0,32},{1,9},{2,34},{3,11},{4,36},{5,13},{6,38},{7,15},{8,40},{9,1... | collective-permute-start | bytes 786440 | tf_op jit(solution)/shard_map/ppermute | solution.py:30
  14.8 6.4 %collective-permute-start.7 = (bf16[32,4096]{1,0:T(8,128)(2,1)S(1)}, bf16[32,4096]{1,0:T(8,128)(2,1)S(1)}, u32[]{:S(2)}, u32[]{:S(2)}) collective-permute-start(bf16[32,4096]{1,0:T(8,128)(2,1)S(1)} %get-tuple-element.54.refs_1_), channel_id=1, source_target_pairs={{0,96},{1,25},{2,98},{3,27},{4,100},{5,29},{6,102},{7,31},{8,104},... | collective-permute-start | bytes 786440 | tf_op jit(solution)/shard_map/ppermute | solution.py:30
  16.5 10.9 %collective-permute-start.4 = (bf16[32,4096]{1,0:T(8,128)(2,1)S(1)}, bf16[32,4096]{1,0:T(8,128)(2,1)S(1)}, u32[]{:S(2)}, u32[]{:S(2)}) collective-permute-start(bf16[32,4096]{1,0:T(8,128)(2,1)S(1)} %get-tuple-element.53.refs_0_), channel_id=1, source_target_pairs={{0,96},{1,25},{2,98},{3,27},{4,100},{5,29},{6,102},{7,31},{8,104},... | collective-permute-start | bytes 786440 | tf_op jit(solution)/shard_map/ppermute | solution.py:30
  18.1 9.4 %collective-permute-start.5 = (bf16[32,4096]{1,0:T(8,128)(2,1)S(1)}, bf16[32,4096]{1,0:T(8,128)(2,1)S(1)}, u32[]{:S(2)}, u32[]{:S(2)}) collective-permute-start(bf16[32,4096]{1,0:T(8,128)(2,1)S(1)} %get-tuple-element.54.refs_1_), channel_id=1, source_target_pairs={{0,32},{1,9},{2,34},{3,11},{4,36},{5,13},{6,38},{7,15},{8,40},{9,1... | collective-permute-start | bytes 786440 | tf_op jit(solution)/shard_map/ppermute | solution.py:30
  20.9 7.6 %collective-permute-start.8 = (bf16[32,4096]{1,0:T(8,128)(2,1)S(1)}, bf16[32,4096]{1,0:T(8,128)(2,1)S(1)}, u32[]{:S(2)}, u32[]{:S(2)}) collective-permute-start(bf16[32,4096]{1,0:T(8,128)(2,1)S(1)} %collective-permute-done.6.refs_2_), channel_id=1, source_target_pairs={{0,32},{1,9},{2,34},{3,11},{4,36},{5,13},{6,38},{7,15},{8,40},{9,1... | collective-permute-start | bytes 786440 | tf_op jit(solution)/shard_map/ppermute | solution.py:30
  21.1 7.3 %collective-permute-start.9 = (bf16[32,4096]{1,0:T(8,128)(2,1)S(1)}, bf16[32,4096]{1,0:T(8,128)(2,1)S(1)}, u32[]{:S(2)}, u32[]{:S(2)}) collective-permute-start(bf16[32,4096]{1,0:T(8,128)(2,1)S(1)} %collective-permute-done.7.refs_3_), channel_id=1, source_target_pairs={{0,96},{1,25},{2,98},{3,27},{4,100},{5,29},{6,102},{7,31},{8,104},... | collective-permute-start | bytes 786440 | tf_op jit(solution)/shard_map/ppermute | solution.py:30
  28.8 8.7 %collective-permute-start.12 = (bf16[256,4096]{1,0:T(8,128)(2,1)S(1)}, bf16[256,4096]{1,0:T(8,128)(2,1)S(1)}, u32[]{:S(2)}, u32[]{:S(2)}) collective-permute-start(bf16[256,4096]{1,0:T(8,128)(2,1)S(1)} %get-tuple-element.60.refs_2_), channel_id=1, source_target_pairs={{0,1},{1,0},{2,3},{3,2},{4,5},{5,4},{6,7},{7,6},{8,9},{9,8},{10,11... | collective-permute-start | bytes 6291464 | tf_op jit(solution)/shard_map/ppermute | solution.py:30
  28.9 16.9 %collective-permute-start.10 = (bf16[128,4096]{1,0:T(8,128)(2,1)S(1)}, bf16[128,4096]{1,0:T(8,128)(2,1)S(1)}, u32[]{:S(2)}, u32[]{:S(2)}) collective-permute-start(bf16[128,4096]{1,0:T(8,128)(2,1)S(1)} %get-tuple-element.64), channel_id=1, source_target_pairs={{0,8},{1,33},{2,10},{3,35},{4,12},{5,37},{6,14},{7,39},{8,16},{9,4... | collective-permute-start | bytes 3145736 | tf_op jit(solution)/shard_map/ppermute | solution.py:30
  30.9 14.9 %collective-permute-start.11 = (bf16[128,4096]{1,0:T(8,128)(2,1)S(1)}, bf16[128,4096]{1,0:T(8,128)(2,1)S(1)}, u32[]{:S(2)}, u32[]{:S(2)}) collective-permute-start(bf16[128,4096]{1,0:T(8,128)(2,1)S(1)} %get-tuple-element.65), channel_id=1, source_target_pairs={{0,24},{1,97},{2,26},{3,99},{4,28},{5,101},{6,30},{7,103},{8,0},{9... | collective-permute-start | bytes 3145736 | tf_op jit(solution)/shard_map/ppermute | solution.py:30
  35.4 21.5 %collective-permute-start.15 = (bf16[128,4096]{1,0:T(8,128)(2,1)S(1)}, bf16[128,4096]{1,0:T(8,128)(2,1)S(1)}, u32[]{:S(2)}, u32[]{:S(2)}) collective-permute-start(bf16[128,4096]{1,0:T(8,128)(2,1)S(1)} %get-tuple-element.64), channel_id=1, source_target_pairs={{0,24},{1,97},{2,26},{3,99},{4,28},{5,101},{6,30},{7,103},{8,0},{9... | collective-permute-start | bytes 3145736 | tf_op jit(solution)/shard_map/ppermute | solution.py:30
  37.4 19.6 %collective-permute-start.16 = (bf16[128,4096]{1,0:T(8,128)(2,1)S(1)}, bf16[128,4096]{1,0:T(8,128)(2,1)S(1)}, u32[]{:S(2)}, u32[]{:S(2)}) collective-permute-start(bf16[128,4096]{1,0:T(8,128)(2,1)S(1)} %get-tuple-element.65), channel_id=1, source_target_pairs={{0,8},{1,33},{2,10},{3,35},{4,12},{5,37},{6,14},{7,39},{8,16},{9,4... | collective-permute-start | bytes 3145736 | tf_op jit(solution)/shard_map/ppermute | solution.py:30
  45.8 22.5 %collective-permute-start.13 = (bf16[128,4096]{1,0:T(8,128)(2,1)S(1)}, bf16[128,4096]{1,0:T(8,128)(2,1)S(1)}, u32[]{:S(2)}, u32[]{:S(2)}) collective-permute-start(bf16[128,4096]{1,0:T(8,128)(2,1)S(1)} %collective-permute-done.10.refs_3_.upper_ref), channel_id=1, source_target_pairs={{0,8},{1,33},{2,10},{3,35},{4,12},{5,37},{6,14},{7,39},{8,16},{9,4... | collective-permute-start | bytes 3145736 | tf_op jit(solution)/shard_map/ppermute | solution.py:30
  47.6 20.7 %collective-permute-start.14 = (bf16[128,4096]{1,0:T(8,128)(2,1)S(1)}, bf16[128,4096]{1,0:T(8,128)(2,1)S(1)}, u32[]{:S(2)}, u32[]{:S(2)}) collective-permute-start(bf16[128,4096]{1,0:T(8,128)(2,1)S(1)} %collective-permute-done.11.refs_4_.lower_ref), channel_id=1, source_target_pairs={{0,24},{1,97},{2,26},{3,99},{4,28},{5,101},{6,30},{7,103},{8,0},{9... | collective-permute-start | bytes 3145736 | tf_op jit(solution)/shard_map/ppermute | solution.py:30
  49.2 10.1 %collective-permute-start.17 = (bf16[256,4096]{1,0:T(8,128)(2,1)S(1)}, bf16[256,4096]{1,0:T(8,128)(2,1)S(1)}, u32[]{:S(2)}, u32[]{:S(2)}) collective-permute-start(bf16[256,4096]{1,0:T(8,128)(2,1)S(1)} %beside_each.1), channel_id=1, source_target_pairs={{0,1},{1,0},{2,3},{3,2},{4,5},{5,4},{6,7},{7,6},{8,9},{9,8},{10,11... | collective-permute-start | bytes 6291464 | tf_op jit(solution)/shard_map/ppermute | solution.py:30
  68.8 6.0 %collective-permute-start.20 = (bf16[128,4096]{1,0:T(8,128)(2,1)S(1)}, bf16[128,4096]{1,0:T(8,128)(2,1)S(1)}, u32[]{:S(2)}, u32[]{:S(2)}) collective-permute-start(bf16[128,4096]{1,0:T(8,128)(2,1)S(1)} %collective-permute-done.13.refs_3_), channel_id=1, source_target_pairs={{0,1},{1,0},{2,3},{3,2},{4,5},{5,4},{6,7},{7,6},{8,9},{9,8},{10,11... | collective-permute-start | bytes 3145736 | tf_op jit(solution)/shard_map/ppermute | solution.py:30
  68.8 6.6 %collective-permute-start.21 = (bf16[128,4096]{1,0:T(8,128)(2,1)S(1)}, bf16[128,4096]{1,0:T(8,128)(2,1)S(1)}, u32[]{:S(2)}, u32[]{:S(2)}) collective-permute-start(bf16[128,4096]{1,0:T(8,128)(2,1)S(1)} %collective-permute-done.14.refs_4_), channel_id=1, source_target_pairs={{0,1},{1,0},{2,3},{3,2},{4,5},{5,4},{6,7},{7,6},{8,9},{9,8},{10,11... | collective-permute-start | bytes 3145736 | tf_op jit(solution)/shard_map/ppermute | solution.py:30
  81.5 5.4 %collective-permute-start.25 = (f32[40,128]{1,0:T(8,128)S(1)}, f32[40,128]{1,0:T(8,128)S(1)}, u32[]{:S(2)}, u32[]{:S(2)}) collective-permute-start(f32[40,128]{1,0:T(8,128)S(1)} %get-tuple-element.78.refs_0_), channel_id=1, source_target_pairs={{0,5},{1,4},{2,7},{3,6},{4,1},{5,0},{6,3},{7,2},{8,13},{9,12},{10,... | collective-permute-start | bytes 61448 | tf_op jit(solution)/shard_map/ppermute | solution.py:30
  83.9 4.4 %collective-permute-start.24 = (f32[40,128]{1,0:T(8,128)S(1)}, f32[40,128]{1,0:T(8,128)S(1)}, u32[]{:S(2)}, u32[]{:S(2)}) collective-permute-start(f32[40,128]{1,0:T(8,128)S(1)} %get-tuple-element.78.refs_0_), channel_id=1, source_target_pairs={{0,3},{1,2},{2,5},{3,4},{4,7},{5,6},{6,1},{7,0},{8,11},{9,10},{10,... | collective-permute-start | bytes 61448 | tf_op jit(solution)/shard_map/ppermute | solution.py:30
  88.4 6.5 %collective-permute-start.28 = (f32[40,128]{1,0:T(8,128)S(1)}, f32[40,128]{1,0:T(8,128)S(1)}, u32[]{:S(2)}, u32[]{:S(2)}) collective-permute-start(f32[40,128]{1,0:T(8,128)S(1)} %get-tuple-element.80.refs_0_), channel_id=1, source_target_pairs={{0,17},{1,16},{2,19},{3,18},{4,21},{5,20},{6,23},{7,22},{8,25},{9,... | collective-permute-start | bytes 61448 | tf_op jit(solution)/shard_map/ppermute | solution.py:30
  96.3 6.2 %collective-permute-start.31 = (f32[40,128]{1,0:T(8,128)S(1)}, f32[40,128]{1,0:T(8,128)S(1)}, u32[]{:S(2)}, u32[]{:S(2)}) collective-permute-start(f32[40,128]{1,0:T(8,128)S(1)} %get-tuple-element.82.refs_0_), channel_id=1, source_target_pairs={{0,65},{1,64},{2,67},{3,66},{4,69},{5,68},{6,71},{7,70},{8,73},{9,... | collective-permute-start | bytes 61448 | tf_op jit(solution)/shard_map/ppermute | solution.py:30
  98.1 4.4 %collective-permute-start.30 = (f32[40,128]{1,0:T(8,128)S(1)}, f32[40,128]{1,0:T(8,128)S(1)}, u32[]{:S(2)}, u32[]{:S(2)}) collective-permute-start(f32[40,128]{1,0:T(8,128)S(1)} %get-tuple-element.82.refs_0_), channel_id=1, source_target_pairs={{0,33},{1,32},{2,35},{3,34},{4,37},{5,36},{6,39},{7,38},{8,41},{9,... | collective-permute-start | bytes 61448 | tf_op jit(solution)/shard_map/ppermute | solution.py:30
  (10 other events, 54.4 us)
